TPU v7x, 128 devices: a whole 4x4x4 slice. The times are simulated.
128 devices in a mesh: gx: 8 (over z, core), gy: 16 (over y, x).
Axes of the slice: x: 4, y: 4, z: 4, core: 2. Of those that a mesh axis runs over, the one named last changes fastest.
Arguments:
- state_path: float32 [2, 128, 256, 256], P(None, 'gx', 'gy'), may hold values from -6 to 6
- velocity: float32 [3, 128, 256, 256], P(None, 'gx', 'gy'), may hold values from -6 to 6
- weights: bfloat16 [2, 4, 128, 256, 256], P(None, None, 'gx', 'gy'), may hold values from -0.25 to 0.75
- owners: int32 [2, 8, 16, 256, 1], P(None, 'gx', 'gy'), may hold values from 0 to 127; in each aligned block of 256 rows (0 to 255, 256 to 511, ..., all dimensions but the last counted through in order) at most 6 rows name the same one
- sources: int32 [2, 8, 16, 256], P(None, 'gx', 'gy'), may hold values from 0 to 255
Outputs:
- hessian_action: float32 [3, 128, 256, 256], P(None, 'gx', 'gy')
Inputs may be any that keep to these rules, and one draw needn't show every extreme that they name: `owners`: in each step, of the 256 columns of one device at most 6 name any one owner, and in every draw some device's columns name one owner exactly 6 times.
All inputs are finite; a program needn't handle non-finite values.
Results may differ from a plain program's by a relative error of at most 0.0003.
Values sent between devices are 32-bit elements; how exact they have to be, the bound alone decides.
No kernel may reach another device: no remote copies, remote signals or barrier semaphores. Data moves between devices by JAX's collectives and lax.ppermute only.
A program may use at most 64 MiB of HBM per device.

v0:
```python
import jax
import jax.numpy as jnp
from jax import lax
from jax.sharding import PartitionSpec as P

FIRST = (0.8, -0.2, 4.0 / 105.0, -1.0 / 280.0)
SECOND = (-205.0 / 72.0, 1.6, -0.2, 8.0 / 315.0, -1.0 / 560.0)
BETA = 0.05


def with_halo(value, sides, width):
    for axis, dim in sides:
        count, length = (lax.axis_size(axis), value.shape[dim])
        up = [(i, (i + 1) % count) for i in range(count)]
        down = [(j, i) for i, j in up]
        last = lax.slice_in_dim(value, length - width, length, axis=dim)
        first = lax.slice_in_dim(value, 0, width, axis=dim)
        before = lax.ppermute(last, axis, up)
        after = lax.ppermute(first, axis, down)
        value = jnp.concatenate([before, value, after], axis=dim)
    return value


def window(padded, row_off, col_off, rows, cols):
    return padded[..., 4 + row_off : 4 + row_off + rows, 4 + col_off : 4 + col_off + cols, :]


def gradients(padded, rows, cols):
    centre = window(padded, 0, 0, rows, cols)
    grad_x = jnp.zeros_like(centre)
    grad_y = jnp.zeros_like(centre)
    grad_z = jnp.zeros_like(centre)
    for k in range(4):
        grad_x = grad_x + FIRST[k] * (
            window(padded, k + 1, 0, rows, cols) - window(padded, -k - 1, 0, rows, cols)
        )
        grad_y = grad_y + FIRST[k] * (
            window(padded, 0, k + 1, rows, cols) - window(padded, 0, -k - 1, rows, cols)
        )
        grad_z = grad_z + FIRST[k] * (jnp.roll(centre, -(k + 1), -1) - jnp.roll(centre, k + 1, -1))
    return jnp.stack([grad_x, grad_y, grad_z], axis=-4)


def neg_laplace(padded, rows, cols):
    centre = window(padded, 0, 0, rows, cols)
    total = 3.0 * SECOND[0] * centre
    for k in range(4):
        weight = SECOND[k + 1]
        total = total + weight * (
            window(padded, k + 1, 0, rows, cols) + window(padded, -k - 1, 0, rows, cols)
        )
        total = total + weight * (
            window(padded, 0, k + 1, rows, cols) + window(padded, 0, -k - 1, rows, cols)
        )
        total = total + weight * (jnp.roll(centre, -(k + 1), -1) + jnp.roll(centre, k + 1, -1))
    return -total


def route(owner_row, source_row, devices, cap):
    match = (owner_row[:, None] == jnp.arange(devices, dtype=jnp.int32)[None, :]).astype(jnp.int32)
    earlier = jnp.cumsum(match, axis=0) - match
    slot = jnp.sum(earlier * match, axis=1)
    place = owner_row * cap + slot
    wanted = jnp.zeros((devices * cap,), jnp.int32).at[place].set(source_row)
    asked = lax.all_to_all(
        wanted.reshape(devices, cap), ("gx", "gy"), split_axis=0, concat_axis=0, tiled=True
    )
    return (place, asked.reshape(-1))


def carry_values(buffer, devices, cap, depth):
    moved = lax.all_to_all(
        buffer.reshape(devices, cap, depth), ("gx", "gy"), split_axis=0, concat_axis=0, tiled=True
    )
    return moved.reshape(devices * cap, depth)


def pull_field(field_cols, tap_weights, place, asked, devices, cap):
    depth = field_cols.shape[1]
    outgo = field_cols[asked]
    arrived = carry_values(outgo, devices, cap, depth)
    mine = arrived[place]
    total = jnp.zeros_like(mine)
    for k in range(4):
        total = total + tap_weights[k].astype(jnp.float32) * jnp.roll(mine, 1 - k, axis=1)
    return total


def push_field(values, tap_weights, place, asked, devices, cap):
    depth = values.shape[1]
    spread = jnp.zeros_like(values)
    for k in range(4):
        spread = spread + jnp.roll(tap_weights[k].astype(jnp.float32) * values, k - 1, axis=1)
    outgo = jnp.zeros((devices * cap, depth), jnp.float32).at[place].set(spread)
    arrived = carry_values(outgo, devices, cap, depth)
    return jnp.zeros_like(values).at[asked].add(arrived)


def per_device(state_path, velocity, weights, owners, sources):
    steps, rows, cols, depth = state_path.shape
    count = rows * cols
    devices = lax.axis_size("gx") * lax.axis_size("gy")
    cap = max(2, 3 * count // devices)
    step_len = 1.0 / steps
    slopes = []
    plans = []
    moved = jnp.zeros((count, depth), jnp.float32)
    for j in range(steps):
        padded = with_halo(state_path[j], (("gx", 0), ("gy", 1)), 4)
        slope = gradients(padded, rows, cols)
        slopes.append(slope)
        plan = route(owners[j, 0, 0, :, 0], sources[j, 0, 0, :], devices, cap)
        plans.append(plan)
        source_term = -jnp.sum(velocity * slope, axis=0)
        before = moved + step_len * source_term.reshape(count, depth)
        tap_weights = weights[j].reshape(4, count, depth)
        moved = pull_field(before, tap_weights, plan[0], plan[1], devices, cap)
    velocity_padded = with_halo(velocity, (("gx", 1), ("gy", 2)), 4)
    hess = BETA * neg_laplace(velocity_padded, rows, cols)
    adjoint = moved
    for j in range(steps - 1, -1, -1):
        tap_weights = weights[j].reshape(4, count, depth)
        adjoint = push_field(adjoint, tap_weights, plans[j][0], plans[j][1], devices, cap)
        hess = hess - step_len * adjoint.reshape(rows, cols, depth)[None] * slopes[j]
    return hess


def solution(mesh):
    return jax.shard_map(
        per_device,
        mesh=mesh,
        in_specs=(
            P(None, "gx", "gy", None),
            P(None, "gx", "gy", None),
            P(None, None, "gx", "gy", None),
            P(None, "gx", "gy", None, None),
            P(None, "gx", "gy", None),
        ),
        out_specs=P(None, "gx", "gy", None),
        check_vma=False,
    )
```

profile of v0, /device:TPU:1, one launch (start us, length us, event | category | flops | bytes accessed | tf_op | source)
XLA Modules:
  0.0 236.1 jit_solution(7785673200578134169)
XLA Ops:
  12.0 12.2 %all-to-all-start = ((s32[128,1,6]{2,1,0:T(1,128)}), s32[128,1,6]{2,1,0:T(1,128)S(1)}, u32[]{:S(2)}, u32[]{:S(2)}) async-start(s32[128,1,6]{2,1,0:T(1,128)} %bitcast.9), calls=%async_computation | async-start | bytes 131072 | tf_op jit(solution)/shard_map/all_to_all | solution.py:65
  28.7 5.0 %all-to-all-done = s32[128,1,6]{2,1,0:T(1,128)S(1)} async-done(((s32[128,1,6]{2,1,0:T(1,128)}), s32[128,1,6]{2,1,0:T(1,128)S(1)}, u32[]{:S(2)}, u32[]{:S(2)}) %all-to-all-start) | async-done | bytes 3104 | tf_op jit(solution)/shard_map/all_to_all | solution.py:65
  33.7 4.8 %all-to-all-start.1 = ((s32[128,1,6]{2,1,0:T(1,128)}), s32[128,1,6]{2,1,0:T(1,128)S(1)}, u32[]{:S(2)}, u32[]{:S(2)}) async-start(s32[128,1,6]{2,1,0:T(1,128)} %bitcast.44), calls=%async_computation.1 | async-start | bytes 131072 | tf_op jit(solution)/shard_map/all_to_all | solution.py:65
  39.9 8.2 %all-to-all-done.1 = s32[128,1,6]{2,1,0:T(1,128)S(1)} async-done(((s32[128,1,6]{2,1,0:T(1,128)}), s32[128,1,6]{2,1,0:T(1,128)S(1)}, u32[]{:S(2)}, u32[]{:S(2)}) %all-to-all-start.1) | async-done | bytes 3104 | tf_op jit(solution)/shard_map/all_to_all | solution.py:65
  50.9 4.8 %collective-permute-start.10 = (f32[24,4,256]{2,0,1:T(8,128)S(1)}, f32[24,4,256]{2,0,1:T(8,128)S(1)}, u32[]{:S(2)}, u32[]{:S(2)}) collective-permute-start(f32[24,4,256]{2,0,1:T(8,128)S(1)} %copy.242), channel_id=1, source_target_pairs={{1,0},{2,1},{3,2},{4,3},{5,4},{6,5},{7,6},{8,7},{9,8},{10,9},{11,1... | collective-permute-start | bytes 294920 | tf_op jit(solution)/shard_map/ppermute | solution.py:19
  57.7 4.9 %collective-permute-done.11 = f32[24,4,256]{2,0,1:T(8,128)S(1)} collective-permute-done((f32[24,4,256]{2,0,1:T(8,128)S(1)}, f32[24,4,256]{2,0,1:T(8,128)S(1)}, u32[]{:S(2)}, u32[]{:S(2)}) %collective-permute-start.11) | collective-permute-done | bytes 98336 | tf_op jit(solution)/shard_map/ppermute | solution.py:18
  67.2 2.9 %gather_fusion = f32[768,256]{1,0:T(8,128)} fusion(f32[256,256]{1,0:T(8,128)S(1)} %bitcast.173, s32[1024]{0:T(1024)S(1)} %get-tuple-element.129), kind=kCustom, calls=%fused_computation | custom fusion | bytes 1575936 | tf_op jit(solution)/shard_map/gather | solution.py:80
  70.1 2.2 reshape.736
  72.3 7.5 %all-to-all-start.2 = ((f32[128,6,256]{2,1,0:T(8,128)}), f32[128,6,256]{2,1,0:T(8,128)}, u32[]{:S(2)}, u32[]{:S(2)}) async-start(f32[128,6,256]{2,1,0:T(8,128)} %reshape.736), calls=%async_computation.2 | async-start | bytes 2097152 | tf_op jit(solution)/shard_map/all_to_all | solution.py:72
  81.4 2.2 fusion.163
  84.4 14.0 %all-to-all-done.2 = f32[128,6,256]{2,1,0:T(8,128)} async-done(((f32[128,6,256]{2,1,0:T(8,128)}), f32[128,6,256]{2,1,0:T(8,128)}, u32[]{:S(2)}, u32[]{:S(2)}) %all-to-all-start.2) | async-done | bytes 786464 | tf_op jit(solution)/shard_map/all_to_all | solution.py:72
  98.4 2.2 reshape.737
  100.7 2.1 gather_fusion.1
  104.2 2.9 %gather_fusion.2 = f32[768,256]{1,0:T(8,128)} fusion(f32[256,256]{1,0:T(8,128)S(1)} %fusion.52, s32[1024]{0:T(1024)S(1)} %get-tuple-element.128), kind=kCustom, calls=%fused_computation.2 | custom fusion | bytes 1575936 | tf_op jit(solution)/shard_map/gather | solution.py:80
  107.1 2.2 reshape.738
  109.3 5.8 %all-to-all-start.3 = ((f32[128,6,256]{2,1,0:T(8,128)}), f32[128,6,256]{2,1,0:T(8,128)}, u32[]{:S(2)}, u32[]{:S(2)}) async-start(f32[128,6,256]{2,1,0:T(8,128)} %reshape.738), calls=%async_computation.3 | async-start | bytes 2097152 | tf_op jit(solution)/shard_map/all_to_all | solution.py:72
  118.9 14.8 %all-to-all-done.3 = f32[128,6,256]{2,1,0:T(8,128)} async-done(((f32[128,6,256]{2,1,0:T(8,128)}), f32[128,6,256]{2,1,0:T(8,128)}, u32[]{:S(2)}, u32[]{:S(2)}) %all-to-all-start.3) | async-done | bytes 786464 | tf_op jit(solution)/shard_map/all_to_all | solution.py:72
  133.7 2.2 reshape.739
  135.9 2.1 gather_fusion.3
  142.4 2.7 %scatter_custom_fusion.2 = f32[768,256]{1,0:T(8,128)S(1)} fusion(s32[256]{0:T(256)} %bitcast.198, f32[]{:T(128)} %constant.21.clone.1, f32[256,256]{1,0:T(8,128)} %copy-done.8, bf16[256,256]{1,0:T(8,128)(2,1)} %bitcast.179, f32[256,1]{1,0:T(8,128)} %slice.853, f32[]{:T(128)} %constant.50, f32[256,255]{1,0:T(8,128)} %slice.852, f32[256,255]{1,0:T(8,128)} %bitcast.177, ...), kind=kCustom, calls=%fused_computation.92 | custom fusion | flops 524288 | bytes 2360320 | tf_op jit(solution)/shard_map/scatter | solution.py:94
  146.2 5.8 %all-to-all-start.4 = ((f32[128,6,256]{2,1,0:T(8,128)}), f32[128,6,256]{2,1,0:T(8,128)}, u32[]{:S(2)}, u32[]{:S(2)}) async-start(f32[128,6,256]{2,1,0:T(8,128)} %reshape.740), calls=%async_computation.4 | async-start | bytes 2097152 | tf_op jit(solution)/shard_map/all_to_all | solution.py:72
  157.1 13.5 %all-to-all-done.4 = f32[128,6,256]{2,1,0:T(8,128)} async-done(((f32[128,6,256]{2,1,0:T(8,128)}), f32[128,6,256]{2,1,0:T(8,128)}, u32[]{:S(2)}, u32[]{:S(2)}) %all-to-all-start.4) | async-done | bytes 786464 | tf_op jit(solution)/shard_map/all_to_all | solution.py:72
  170.6 2.2 reshape.812
  172.8 6.8 %scatter_custom_fusion.3 = f32[256,256]{1,0:T(8,128)S(1)} fusion(s32[768]{0:T(1024)S(1)} %fusion.155, f32[768,256]{1,0:T(8,128)} %reshape.812, f32[]{:T(128)} %constant.21.clone.1), kind=kCustom, calls=%fused_computation.293 | custom fusion | flops 196608 | bytes 262656 | tf_op jit(solution)/shard_map/scatter-add | solution.py:96
  183.5 2.7 %scatter_custom_fusion.4 = f32[768,256]{1,0:T(8,128)S(1)} fusion(s32[256]{0:T(256)} %bitcast.196, f32[]{:T(128)} %constant.21.clone.1, f32[256,256]{1,0:T(8,128)} %copy-done.9, bf16[256,256]{1,0:T(8,128)(2,1)} %bitcast.178, f32[256,1]{1,0:T(8,128)} %slice.859, f32[]{:T(128)} %constant.50, f32[256,255]{1,0:T(8,128)} %slice.858, f32[256,255]{1,0:T(8,128)} %bitcast.176, ...), kind=kCustom, calls=%fused_computation.90 | custom fusion | flops 524288 | bytes 2360320 | tf_op jit(solution)/shard_map/scatter | solution.py:94
  187.3 5.4 %all-to-all-start.5 = ((f32[128,6,256]{2,1,0:T(8,128)}), f32[128,6,256]{2,1,0:T(8,128)}, u32[]{:S(2)}, u32[]{:S(2)}) async-start(f32[128,6,256]{2,1,0:T(8,128)} %reshape.742), calls=%async_computation.5 | async-start | bytes 2097152 | tf_op jit(solution)/shard_map/all_to_all | solution.py:72
  194.0 5.0 %collective-permute-start.2 = (f32[3,24,4,256]{3,1,2,0:T(8,128)S(1)}, f32[3,24,4,256]{3,1,2,0:T(8,128)S(1)}, u32[]{:S(2)}, u32[]{:S(2)}) collective-permute-start(f32[3,24,4,256]{3,1,2,0:T(8,128)S(1)} %copy.252), channel_id=1, source_target_pairs={{1,0},{2,1},{3,2},{4,3},{5,4},{6,5},{7,6},{8,7},{9,8},{10,9},{11,1... | collective-permute-start | bytes 884744 | tf_op jit(solution)/shard_map/ppermute | solution.py:19
  201.7 9.6 %collective-permute-done.2 = f32[3,24,4,256]{3,1,2,0:T(8,128)S(1)} collective-permute-done((f32[3,24,4,256]{3,1,2,0:T(8,128)S(1)}, f32[3,24,4,256]{3,1,2,0:T(8,128)S(1)}, u32[]{:S(2)}, u32[]{:S(2)}) %collective-permute-start.2) | collective-permute-done | bytes 294944 | tf_op jit(solution)/shard_map/ppermute | solution.py:19
  212.2 2.6 %collective-permute-done.3 = f32[3,24,4,256]{3,1,2,0:T(8,128)S(1)} collective-permute-done((f32[3,24,4,256]{3,1,2,0:T(8,128)S(1)}, f32[3,24,4,256]{3,1,2,0:T(8,128)S(1)}, u32[]{:S(2)}, u32[]{:S(2)}) %collective-permute-start.3) | collective-permute-done | bytes 294944 | tf_op jit(solution)/shard_map/ppermute | solution.py:18
  215.6 2.3 reshape.828
  217.9 7.4 %scatter_custom_fusion.5 = f32[256,256]{1,0:T(8,128)} fusion(s32[768]{0:T(1024)S(1)} %fusion.156, f32[768,256]{1,0:T(8,128)} %reshape.828, f32[]{:T(128)} %constant.21.clone.1), kind=kCustom, calls=%fused_computation.291 | custom fusion | flops 196608 | bytes 262656 | tf_op jit(solution)/shard_map/scatter-add | solution.py:96
  226.3 9.7 %fusion.11 = f32[3,16,16,256]{3,2,1,0:T(8,128)} fusion(f32[3,24,16,256]{3,2,1,0:T(8,128)} %get-tuple-element.101, f32[3,24,4,256]{3,2,1,0:T(4,128)} %copy.227, f32[3,24,4,256]{3,2,1,0:T(4,128)} %copy.225, f32[3,20,16,256]{3,2,1,0:T(8,128)S(1)} %get-tuple-element.20, f32[3,20,16,256]{3,2,1,0:T(8,128)S(1)} %get-tuple-element.100, ...), kind=kLoop, calls=%fused_computation.33 | loop fusion | flops 12386304 | bytes 18022400 | tf_op jit(solution)/shard_map/sub | solution.py:124
  (190 shorter events, 56.5 us)
Async XLA Ops:
  0.0 8.5 %copy-start.28 = (s32[2,1,1,256,1]{3,4,2,1,0:T(1,128)S(1)}, s32[2,1,1,256,1]{3,4,2,1,0:T(1,128)}, u32[]{:S(2)}) copy-start(s32[2,1,1,256,1]{3,4,2,1,0:T(1,128)} %param.8) | copy-start | bytes 6148
  1.6 47.4 %collective-permute-start.4 = (f32[4,16,256]{2,1,0:T(8,128)}, f32[4,16,256]{2,1,0:T(8,128)S(1)}, u32[]{:S(2)}, u32[]{:S(2)}) collective-permute-start(f32[4,16,256]{2,1,0:T(8,128)} %get-tuple-element.41), channel_id=1, source_target_pairs={{16,0},{32,16},{48,32},{64,48},{80,64},{96,80},{112,96},{0,112},{1... | collective-permute-start | bytes 196616 | tf_op jit(solution)/shard_map/ppermute | solution.py:19
  3.1 46.0 %collective-permute-start.5 = (f32[4,16,256]{2,1,0:T(8,128)}, f32[4,16,256]{2,1,0:T(8,128)S(1)}, u32[]{:S(2)}, u32[]{:S(2)}) collective-permute-start(f32[4,16,256]{2,1,0:T(8,128)} %get-tuple-element.40), channel_id=1, source_target_pairs={{0,16},{16,32},{32,48},{48,64},{64,80},{80,96},{96,112},{112,0},{1... | collective-permute-start | bytes 196616 | tf_op jit(solution)/shard_map/ppermute | solution.py:18
  4.7 46.1 %collective-permute-start.8 = (f32[4,16,256]{2,1,0:T(8,128)}, f32[4,16,256]{2,1,0:T(8,128)S(1)}, u32[]{:S(2)}, u32[]{:S(2)}) collective-permute-start(f32[4,16,256]{2,1,0:T(8,128)} %get-tuple-element.43), channel_id=1, source_target_pairs={{16,0},{32,16},{48,32},{64,48},{80,64},{96,80},{112,96},{0,112},{1... | collective-permute-start | bytes 196616 | tf_op jit(solution)/shard_map/ppermute | solution.py:19
  6.6 44.2 %collective-permute-start.9 = (f32[4,16,256]{2,1,0:T(8,128)S(1)}, f32[4,16,256]{2,1,0:T(8,128)S(1)}, u32[]{:S(2)}, u32[]{:S(2)}) collective-permute-start(f32[4,16,256]{2,1,0:T(8,128)S(1)} %get-tuple-element.42), channel_id=1, source_target_pairs={{0,16},{16,32},{32,48},{48,64},{64,80},{80,96},{96,112},{112,0},{1... | collective-permute-start | bytes 196616 | tf_op jit(solution)/shard_map/ppermute | solution.py:18
  8.4 15.7 %copy-start.16 = (f32[2,16,16,256]{3,2,1,0:T(8,128)S(1)}, f32[2,16,16,256]{3,2,1,0:T(8,128)}, u32[]{:S(2)}) copy-start(f32[2,16,16,256]{3,2,1,0:T(8,128)} %param.5) | copy-start | bytes 1572868
  8.4 54.9 %collective-permute-start.1 = (f32[3,4,16,256]{3,2,1,0:T(8,128)}, f32[3,4,16,256]{3,2,1,0:T(8,128)}, u32[]{:S(2)}, u32[]{:S(2)}) collective-permute-start(f32[3,4,16,256]{3,2,1,0:T(8,128)} %get-tuple-element.39), channel_id=1, source_target_pairs={{0,16},{16,32},{32,48},{48,64},{64,80},{80,96},{96,112},{112,0},{1... | collective-permute-start | bytes 589832 | tf_op jit(solution)/shard_map/ppermute | solution.py:18
  9.8 71.6 %copy-start.29 = (s32[256,1]{0,1:T(1,128)}, s32[256,1]{0,1:T(1,128)S(1)}, u32[]{:S(2)}) copy-start(s32[256,1]{0,1:T(1,128)S(1)} %get-tuple-element.107) | copy-start | bytes 3076
  12.0 21.8 %all-to-all-start = ((s32[128,1,6]{2,1,0:T(1,128)}), s32[128,1,6]{2,1,0:T(1,128)S(1)}, u32[]{:S(2)}, u32[]{:S(2)}) async-start(s32[128,1,6]{2,1,0:T(1,128)} %bitcast.9), calls=%async_computation | async-start | bytes 131072 | tf_op jit(solution)/shard_map/all_to_all | solution.py:65
  26.1 39.1 %copy-start.6 = (f32[1,16,16,256]{3,2,1,0:T(8,128)}, f32[1,16,16,256]{3,2,1,0:T(8,128)S(1)}, u32[]{:S(2)}) copy-start(f32[1,16,16,256]{3,2,1,0:T(8,128)S(1)} %fusion.112) | copy-start | bytes 786436
  26.6 38.6 %copy-start.7 = (f32[1,16,16,256]{3,2,1,0:T(8,128)}, f32[1,16,16,256]{3,2,1,0:T(8,128)S(1)}, u32[]{:S(2)}) copy-start(f32[1,16,16,256]{3,2,1,0:T(8,128)S(1)} %fusion.119) | copy-start | bytes 786436
  33.7 14.4 %all-to-all-start.1 = ((s32[128,1,6]{2,1,0:T(1,128)}), s32[128,1,6]{2,1,0:T(1,128)S(1)}, u32[]{:S(2)}, u32[]{:S(2)}) async-start(s32[128,1,6]{2,1,0:T(1,128)} %bitcast.44), calls=%async_computation.1 | async-start | bytes 131072 | tf_op jit(solution)/shard_map/all_to_all | solution.py:65
  49.1 7.0 %collective-permute-start.6 = (f32[24,4,256]{2,0,1:T(8,128)S(1)}, f32[24,4,256]{2,0,1:T(8,128)S(1)}, u32[]{:S(2)}, u32[]{:S(2)}) collective-permute-start(f32[24,4,256]{2,0,1:T(8,128)S(1)} %copy.231), channel_id=1, source_target_pairs={{1,0},{2,1},{3,2},{4,3},{5,4},{6,5},{7,6},{8,7},{9,8},{10,9},{11,1... | collective-permute-start | bytes 294920 | tf_op jit(solution)/shard_map/ppermute | solution.py:19
  50.7 6.9 %collective-permute-start.7 = (f32[24,4,256]{2,0,1:T(8,128)S(1)}, f32[24,4,256]{2,0,1:T(8,128)S(1)}, u32[]{:S(2)}, u32[]{:S(2)}) collective-permute-start(f32[24,4,256]{2,0,1:T(8,128)S(1)} %copy.233), channel_id=1, source_target_pairs={{0,1},{1,2},{2,3},{3,4},{4,5},{5,6},{6,7},{7,8},{8,9},{9,10},{10,1... | collective-permute-start | bytes 294920 | tf_op jit(solution)/shard_map/ppermute | solution.py:18
  50.9 6.7 %collective-permute-start.10 = (f32[24,4,256]{2,0,1:T(8,128)S(1)}, f32[24,4,256]{2,0,1:T(8,128)S(1)}, u32[]{:S(2)}, u32[]{:S(2)}) collective-permute-start(f32[24,4,256]{2,0,1:T(8,128)S(1)} %copy.242), channel_id=1, source_target_pairs={{1,0},{2,1},{3,2},{4,3},{5,4},{6,5},{7,6},{8,7},{9,8},{10,9},{11,1... | collective-permute-start | bytes 294920 | tf_op jit(solution)/shard_map/ppermute | solution.py:19
  55.7 6.9 %collective-permute-start.11 = (f32[24,4,256]{2,0,1:T(8,128)S(1)}, f32[24,4,256]{2,0,1:T(8,128)S(1)}, u32[]{:S(2)}, u32[]{:S(2)}) collective-permute-start(f32[24,4,256]{2,0,1:T(8,128)S(1)} %copy.244), channel_id=1, source_target_pairs={{0,1},{1,2},{2,3},{3,4},{4,5},{5,6},{6,7},{7,8},{8,9},{9,10},{10,1... | collective-permute-start | bytes 294920 | tf_op jit(solution)/shard_map/ppermute | solution.py:18
  55.9 9.2 %copy-start.4 = (f32[1,16,16,256]{3,2,1,0:T(8,128)}, f32[1,16,16,256]{3,2,1,0:T(8,128)S(1)}, u32[]{:S(2)}) copy-start(f32[1,16,16,256]{3,2,1,0:T(8,128)S(1)} %fusion.62) | copy-start | bytes 786436
  56.0 9.1 %copy-start.5 = (f32[1,16,16,256]{3,2,1,0:T(8,128)}, f32[1,16,16,256]{3,2,1,0:T(8,128)S(1)}, u32[]{:S(2)}) copy-start(f32[1,16,16,256]{3,2,1,0:T(8,128)S(1)} %fusion.78) | copy-start | bytes 786436
  72.3 9.0 %copy-start.31 = (s32[256,1]{0,1:T(1,128)S(1)}, s32[256,1]{0,1:T(1,128)}, u32[]{:S(2)}) copy-start(s32[256,1]{0,1:T(1,128)} %copy-done.30) | copy-start | bytes 3076
  72.3 26.1 %all-to-all-start.2 = ((f32[128,6,256]{2,1,0:T(8,128)}), f32[128,6,256]{2,1,0:T(8,128)}, u32[]{:S(2)}, u32[]{:S(2)}) async-start(f32[128,6,256]{2,1,0:T(8,128)} %reshape.736), calls=%async_computation.2 | async-start | bytes 2097152 | tf_op jit(solution)/shard_map/all_to_all | solution.py:72
  79.9 75.6 %collective-permute-start = (f32[3,4,16,256]{3,2,1,0:T(8,128)}, f32[3,4,16,256]{3,2,1,0:T(8,128)}, u32[]{:S(2)}, u32[]{:S(2)}) collective-permute-start(f32[3,4,16,256]{3,2,1,0:T(8,128)} %get-tuple-element.38), channel_id=1, source_target_pairs={{16,0},{32,16},{48,32},{64,48},{80,64},{96,80},{112,96},{0,112},{1... | collective-permute-start | bytes 589832 | tf_op jit(solution)/shard_map/ppermute | solution.py:19
  83.6 19.6 %copy-start.14 = (bf16[1,1,16,16,256]{4,3,2,1,0:T(8,128)(2,1)}, bf16[1,1,16,16,256]{4,3,2,1,0:T(8,128)(2,1)S(1)}, u32[]{:S(2)}) copy-start(bf16[1,1,16,16,256]{4,3,2,1,0:T(8,128)(2,1)S(1)} %get-tuple-element.15) | copy-start | bytes 393220
  83.6 54.8 %copy-start.15 = (bf16[1,1,16,16,256]{4,3,2,1,0:T(8,128)(2,1)}, bf16[1,1,16,16,256]{4,3,2,1,0:T(8,128)(2,1)S(1)}, u32[]{:S(2)}) copy-start(bf16[1,1,16,16,256]{4,3,2,1,0:T(8,128)(2,1)S(1)} %get-tuple-element.12) | copy-start | bytes 393220
  109.3 24.4 %all-to-all-start.3 = ((f32[128,6,256]{2,1,0:T(8,128)}), f32[128,6,256]{2,1,0:T(8,128)}, u32[]{:S(2)}, u32[]{:S(2)}) async-start(f32[128,6,256]{2,1,0:T(8,128)} %reshape.738), calls=%async_computation.3 | async-start | bytes 2097152 | tf_op jit(solution)/shard_map/all_to_all | solution.py:72
  146.2 24.4 %all-to-all-start.4 = ((f32[128,6,256]{2,1,0:T(8,128)}), f32[128,6,256]{2,1,0:T(8,128)}, u32[]{:S(2)}, u32[]{:S(2)}) async-start(f32[128,6,256]{2,1,0:T(8,128)} %reshape.740), calls=%async_computation.4 | async-start | bytes 2097152 | tf_op jit(solution)/shard_map/all_to_all | solution.py:72
  157.1 22.5 %copy-start.18 = (bf16[1,1,16,16,256]{4,3,2,1,0:T(8,128)(2,1)S(1)}, bf16[1,1,16,16,256]{4,3,2,1,0:T(8,128)(2,1)}, u32[]{:S(2)}) copy-start(bf16[1,1,16,16,256]{4,3,2,1,0:T(8,128)(2,1)} %get-tuple-element.13) | copy-start | bytes 393220
  157.1 22.5 %copy-start.20 = (bf16[1,1,16,16,256]{4,3,2,1,0:T(8,128)(2,1)S(1)}, bf16[1,1,16,16,256]{4,3,2,1,0:T(8,128)(2,1)}, u32[]{:S(2)}) copy-start(bf16[1,1,16,16,256]{4,3,2,1,0:T(8,128)(2,1)} %get-tuple-element.14) | copy-start | bytes 393220
  157.1 22.5 %copy-start.22 = (bf16[1,1,16,16,256]{4,3,2,1,0:T(8,128)(2,1)S(1)}, bf16[1,1,16,16,256]{4,3,2,1,0:T(8,128)(2,1)}, u32[]{:S(2)}) copy-start(bf16[1,1,16,16,256]{4,3,2,1,0:T(8,128)(2,1)} %get-tuple-element.16) | copy-start | bytes 393220
  187.3 28.4 %all-to-all-start.5 = ((f32[128,6,256]{2,1,0:T(8,128)}), f32[128,6,256]{2,1,0:T(8,128)}, u32[]{:S(2)}, u32[]{:S(2)}) async-start(f32[128,6,256]{2,1,0:T(8,128)} %reshape.742), calls=%async_computation.5 | async-start | bytes 2097152 | tf_op jit(solution)/shard_map/all_to_all | solution.py:72
  194.0 17.3 %collective-permute-start.2 = (f32[3,24,4,256]{3,1,2,0:T(8,128)S(1)}, f32[3,24,4,256]{3,1,2,0:T(8,128)S(1)}, u32[]{:S(2)}, u32[]{:S(2)}) collective-permute-start(f32[3,24,4,256]{3,1,2,0:T(8,128)S(1)} %copy.252), channel_id=1, source_target_pairs={{1,0},{2,1},{3,2},{4,3},{5,4},{6,5},{7,6},{8,7},{9,8},{10,9},{11,1... | collective-permute-start | bytes 884744 | tf_op jit(solution)/shard_map/ppermute | solution.py:19
  199.1 15.7 %collective-permute-start.3 = (f32[3,24,4,256]{3,1,2,0:T(8,128)S(1)}, f32[3,24,4,256]{3,1,2,0:T(8,128)S(1)}, u32[]{:S(2)}, u32[]{:S(2)}) collective-permute-start(f32[3,24,4,256]{3,1,2,0:T(8,128)S(1)} %copy.253), channel_id=1, source_target_pairs={{0,1},{1,2},{2,3},{3,4},{4,5},{5,6},{6,7},{7,8},{8,9},{9,10},{10,1... | collective-permute-start | bytes 884744 | tf_op jit(solution)/shard_map/ppermute | solution.py:18
  215.6 10.6 %copy-start.1 = (f32[3,16,16,252]{3,2,1,0:T(8,128)S(1)}, f32[3,16,16,252]{3,2,1,0:T(8,128)}, u32[]{:S(2)}) copy-start(f32[3,16,16,252]{3,2,1,0:T(8,128)} %get-tuple-element.24) | copy-start | bytes 2322436
  (19 other events, 41.5 us)
where the time goes:
time: 237 us; the launch traced here: 236 us
  waiting for transfers between devices  74.1 us (31%)
  local copies, waits for them, and re-layouts  62.8 us (26%)
  starting transfers between devices  59.6 us (25%)
  other arithmetic  38.7 us (16%)
    all_to_all x4, waiting for transfers between devices, carry_values(): lax.all_to_all(buffer.reshape(devices, cap, depth), ('gx', 'gy'), split_a...  42.3 us
    all_to_all x4, starting transfers between devices, carry_values(): lax.all_to_all(buffer.reshape(devices, cap, depth), ('gx', 'gy'), split_a...  24.4 us
    all_to_all x2, starting transfers between devices, route(): lax.all_to_all(wanted.reshape(devices, cap), ('gx', 'gy'), split_axis=0,...  17 us
    ppermute x6, starting transfers between devices, with_halo(): after = lax.ppermute(first, axis, down)  16.3 us
    scatter-add x2, other arithmetic, push_field(): return jnp.zeros_like(values).at[asked].add(arrived)  14.1 us
    all_to_all x2, waiting for transfers between devices, route(): lax.all_to_all(wanted.reshape(devices, cap), ('gx', 'gy'), split_axis=0,...  13.1 us
    slice x8, local copies, waits for them, and re-layouts, neg_laplace(): jnp.roll(centre, k + 1, -1)  9.76 us
    sub x1, other arithmetic, per_device(): hess - step_len * adjoint.reshape(rows, cols, depth)[None] * slopes[j]  9.68 us
  transfers between devices with their start and end apart: 18, of which 9 were waited for; matrix products, arithmetic and copies ran while one was open for 22% of the time, Pallas kernels for 0%

commit v1 on v0

v1 whole, which is shorter than its diff:
```python
import jax
import jax.numpy as jnp
from jax import lax
from jax.experimental import pallas as pl
from jax.experimental.pallas import tpu as pltpu
from jax.sharding import PartitionSpec as P

FIRST = (0.8, -0.2, 4.0 / 105.0, -1.0 / 280.0)
SECOND = (-205.0 / 72.0, 1.6, -0.2, 8.0 / 315.0, -1.0 / 560.0)
BETA = 0.05
AXES = ("gx", "gy")
CAP = 6
DEV = 128
COLS = 256
NZ = 256
F32 = jnp.float32
BF16 = jnp.bfloat16
W_ROWS = CAP * 8
A_ROWS = W_ROWS + 1
V_ROWS = CAP * 2


def params(mib):
    return pltpu.CompilerParams(vmem_limit_bytes=mib * 1024 * 1024)


def call(kernel, out_shape, mib, micros, **kw):
    return pl.pallas_call(
        kernel,
        out_shape=out_shape,
        compiler_params=params(mib),
        cost_estimate=pl.CostEstimate(
            flops=int(micros * 1e8), bytes_accessed=int(micros * 2e6), transcendentals=0
        ),
        **kw,
    )


def iota(shape, dim):
    return lax.broadcasted_iota(jnp.int32, shape, dim)


def split3(x):
    hi = x.astype(BF16)
    rest = x - hi.astype(F32)
    mid = rest.astype(BF16)
    low = (rest - mid.astype(F32)).astype(BF16)
    return hi, mid, low


def select(onehot, x):
    return sum(jnp.dot(onehot, part, preferred_element_type=F32) for part in split3(x))


def slots_row(owner_col, owner_row):
    earlier = (owner_col == owner_row) & (iota((COLS, COLS), 0) < iota((COLS, COLS), 1))
    return jnp.sum(earlier.astype(jnp.int32), axis=0, keepdims=True)


def slots_col(owner_col, owner_row):
    earlier = (owner_col == owner_row) & (iota((COLS, COLS), 1) < iota((COLS, COLS), 0))
    return jnp.sum(earlier.astype(jnp.int32), axis=1, keepdims=True)


def place_mask(owner_row, slot_row, s):
    return (iota((DEV, COLS), 0) == owner_row) & (slot_row == s)


def request_kernel(oc_ref, or_ref, sr_ref, w_ref, out_ref):
    lane = iota((DEV, 128), 1)
    wanted = jnp.zeros((DEV, 128), F32)
    for j in range(2):
        owner_row = or_ref[j : j + 1, :]
        slot_row = slots_row(oc_ref[j], owner_row)
        source_row = sr_ref[j : j + 1, :].astype(F32)
        masks = [place_mask(owner_row, slot_row, s) for s in range(CAP)]
        for s in range(CAP):
            column = jnp.sum(jnp.where(masks[s], source_row, 0.0), axis=1, keepdims=True)
            wanted = jnp.where(lane == 8 * j + s, column, wanted)
        if j == 1:
            onehot = jnp.concatenate([m.astype(BF16) for m in masks], axis=0)
            for k in range(4):
                weight = w_ref[0, k].reshape(COLS, NZ)
                placed = jnp.dot(onehot, weight, preferred_element_type=F32)
                for s in range(CAP):
                    for half in range(2):
                        row = s * 8 + k * 2 + half
                        out_ref[pl.ds(row, DEV, stride=A_ROWS), :] = placed[
                            s * DEV : (s + 1) * DEV, half * 128 : half * 128 + 128
                        ]
    out_ref[pl.ds(W_ROWS, DEV, stride=A_ROWS), :] = wanted


def stencil_kernel(st_ref, ve_ref, xlo_ref, xhi_ref, ylo_ref, yhi_ref, g_ref, b_ref, h_ref, xpad, ypad):
    step_len = 0.5
    for field in range(5):
        source = st_ref.at[field] if field < 2 else ve_ref.at[field - 2]
        xpad[0:4] = xlo_ref[field]
        xpad[4:20] = source[...]
        xpad[20:24] = xhi_ref[field]
        ypad[:, 4:8] = ylo_ref[field]
        ypad[:, 8:24] = source[...]
        ypad[:, 24:28] = yhi_ref[field]

        def row(x, carry, field=field):
            centre = xpad[x + 4]
            sign = -1.0 if field < 2 else 1.0
            parts = [jnp.zeros_like(centre) for _ in range(3)]
            coeffs = FIRST if field < 2 else SECOND[1:]
            for k in range(4):
                d = k + 1
                parts[0] += coeffs[k] * (xpad[x + 4 + d] + sign * xpad[x + 4 - d])
                parts[1] += coeffs[k] * (ypad[x, 8 + d : 24 + d, :] + sign * ypad[x, 8 - d : 24 - d, :])
                parts[2] += coeffs[k] * (
                    pltpu.roll(centre, NZ - d, 1) + sign * pltpu.roll(centre, d, 1)
                )
            if field < 2:
                for c in range(3):
                    g_ref[field, c, x] = parts[c]
                dot = ve_ref[0, x] * parts[0] + ve_ref[1, x] * parts[1] + ve_ref[2, x] * parts[2]
                b_ref[field, x] = -step_len * dot
            else:
                total = 3.0 * SECOND[0] * centre + parts[0] + parts[1] + parts[2]
                h_ref[field - 2, x] = -BETA * total
            return carry

        lax.fori_loop(0, 16, row, 0)


def supply_kernel(idx_ref, b_ref, out_ref):
    wanted = idx_ref[:, 0, 0, :]
    place = iota((DEV, COLS), 1).astype(F32)
    onehot = jnp.concatenate(
        [(wanted[:, s : s + 1] == place).astype(BF16) for s in range(CAP)], axis=0
    )
    values = select(onehot, b_ref[0])
    for s in range(CAP):
        for half in range(2):
            out_ref[pl.ds(s * 2 + half, DEV, stride=V_ROWS), :] = values[
                s * DEV : (s + 1) * DEV, half * 128 : half * 128 + 128
            ]


def gathered_rows(wanted_t, first):
    place = iota((COLS, DEV), 0).astype(F32)
    return jnp.concatenate(
        [(place == wanted_t[first + s : first + s + 1, :]).astype(BF16) for s in range(CAP)], axis=1
    )


def normal_kernel(a_ref, d_ref, wt_ref, w_scr):
    wanted_t = a_ref[pl.ds(W_ROWS, DEV, stride=A_ROWS), :].T
    wt_ref[...] = wanted_t[:16]
    onehot_t = gathered_rows(wanted_t, 8)
    for k in range(4):
        for s in range(CAP):
            for half in range(2):
                w_scr[k, s * DEV : (s + 1) * DEV, half * 128 : half * 128 + 128] = a_ref[
                    pl.ds(s * 8 + k * 2 + half, DEV, stride=A_ROWS), :
                ]
    for m in range(4):
        total = None
        for k in range(4 - m):
            product = w_scr[k] * w_scr[k + m]
            high = product.astype(BF16)
            low = (product - high.astype(F32)).astype(BF16)
            part = jnp.dot(onehot_t, high, preferred_element_type=F32) + jnp.dot(
                onehot_t, low, preferred_element_type=F32
            )
            if k != 1:
                part = pltpu.roll(part, (k - 1) % NZ, 1)
            total = part if total is None else total + part
        d_ref[m] = total


def read_slots(ref):
    return jnp.concatenate(
        [
            jnp.concatenate(
                [ref[pl.ds(s * 2 + half, DEV, stride=V_ROWS), :] for half in range(2)], axis=1
            )
            for s in range(CAP)
        ],
        axis=0,
    )


def middle_kernel(arr_ref, oc_ref, or_ref, w_ref, b_ref, d_ref, lam_ref, out_ref):
    owner_col = oc_ref[0]
    owner_row = or_ref[0:1, :]
    slot_col = slots_col(owner_col, owner_row)
    slot_row = slots_row(owner_col, owner_row)
    lane = iota((COLS, DEV), 1)
    taken = jnp.concatenate(
        [((lane == owner_col) & (slot_col == s)).astype(BF16) for s in range(CAP)], axis=1
    )
    mine = select(taken, read_slots(arr_ref))
    weights = [w_ref[0, k].reshape(COLS, NZ).astype(F32) for k in range(4)]
    field = b_ref[0]
    for k in range(4):
        field += weights[k] * (mine if k == 1 else pltpu.roll(mine, (1 - k) % NZ, 1))
    lam = d_ref[0] * field
    for m in range(1, 4):
        lam += d_ref[m] * pltpu.roll(field, NZ - m, 1) + pltpu.roll(d_ref[m] * field, m, 1)
    lam_ref[...] = lam
    spread = weights[1] * lam
    for k in (0, 2, 3):
        spread += pltpu.roll(weights[k] * lam, (k - 1) % NZ, 1)
    onehot = jnp.concatenate(
        [place_mask(owner_row, slot_row, s).astype(BF16) for s in range(CAP)], axis=0
    )
    values = select(onehot, spread)
    for s in range(CAP):
        for half in range(2):
            out_ref[pl.ds(s * 2 + half, DEV, stride=V_ROWS), :] = values[
                s * DEV : (s + 1) * DEV, half * 128 : half * 128 + 128
            ]


def final_kernel(arr_ref, wt_ref, h_ref, g_ref, out_ref):
    onehot_t = gathered_rows(wt_ref[...], 0)
    lam = select(onehot_t, read_slots(arr_ref))
    for c in range(3):
        out_ref[c] = h_ref[c] - 0.5 * (lam * g_ref[0, c])


def exchange(value):
    return lax.all_to_all(value, AXES, split_axis=0, concat_axis=0, tiled=True)


def neighbours(first, last, axis):
    count = lax.axis_size(axis)
    up = [(i, (i + 1) % count) for i in range(count)]
    down = [(j, i) for i, j in up]
    return lax.ppermute(last, axis, up), lax.ppermute(first, axis, down)


def per_device(state_path, velocity, weights, owners, sources):
    owner_col = owners.reshape(2, COLS, 1)
    owner_row = owners.reshape(2, COLS)
    source_row = sources.reshape(2, COLS)
    whole = lambda *shape: pl.BlockSpec(shape, lambda i: (0,) * len(shape))
    weight_spec = lambda j: pl.BlockSpec((1, 4, 16, 16, NZ), lambda i: (j, 0, 0, 0, 0))
    struct = lambda *shape: jax.ShapeDtypeStruct(shape, F32)

    request = call(
        request_kernel,
        struct(DEV * A_ROWS, 128),
        20,
        3,
        grid=(1,),
        in_specs=[whole(2, COLS, 1), whole(2, COLS), whole(2, COLS), weight_spec(1)],
        out_specs=whole(DEV * A_ROWS, 128),
    )(owner_col, owner_row, source_row, weights)
    asked = exchange(request.reshape(DEV, A_ROWS, 1, 128))

    faces = lambda lo, hi, dim: jnp.concatenate(
        [lax.slice_in_dim(v, lo, hi, axis=dim) for v in (state_path, velocity)], axis=0
    )
    xlo, xhi = neighbours(faces(0, 4, 1), faces(12, 16, 1), "gx")
    ylo, yhi = neighbours(faces(0, 4, 2), faces(12, 16, 2), "gy")
    slopes, before, hess = call(
        stencil_kernel,
        (struct(2, 3, 16, 16, NZ), struct(2, 16, 16, NZ), struct(3, 16, 16, NZ)),
        20,
        6,
        scratch_shapes=[pltpu.VMEM((24, 16, NZ), F32), pltpu.VMEM((16, 32, NZ), F32)],
    )(state_path, velocity, xlo, xhi, ylo, yhi)
    slopes = slopes.reshape(2, 3, COLS, NZ)
    before = before.reshape(2, COLS, NZ)
    hess = hess.reshape(3, COLS, NZ)

    step_field = lambda j: pl.BlockSpec((1, COLS, NZ), lambda i: (j, 0, 0))
    supply = call(
        supply_kernel,
        struct(DEV * V_ROWS, 128),
        20,
        1,
        grid=(1,),
        in_specs=[pl.BlockSpec((DEV, 1, 1, 128), lambda i: (0, W_ROWS, 0, 0)), step_field(0)],
        out_specs=whole(DEV * V_ROWS, 128),
    )(asked, before)
    arrived = exchange(supply.reshape(DEV, CAP, 2, 128))

    normal, wanted_t = call(
        normal_kernel,
        (struct(4, COLS, NZ), struct(16, 128)),
        24,
        4,
        scratch_shapes=[pltpu.VMEM((4, CAP * DEV, NZ), F32)],
    )(asked.reshape(DEV * A_ROWS, 128))

    lam, push = call(
        middle_kernel,
        (struct(COLS, NZ), struct(DEV * V_ROWS, 128)),
        24,
        3,
        grid=(1,),
        in_specs=[
            whole(DEV * V_ROWS, 128),
            whole(2, COLS, 1),
            whole(2, COLS),
            weight_spec(0),
            step_field(1),
            whole(4, COLS, NZ),
        ],
        out_specs=(whole(COLS, NZ), whole(DEV * V_ROWS, 128)),
    )(arrived.reshape(DEV * V_ROWS, 128), owner_col, owner_row, weights, before, normal)
    returned = exchange(push.reshape(DEV, CAP, 2, 128))

    hess = hess - 0.5 * (lam[None] * slopes[1])
    out = call(
        final_kernel,
        struct(3, COLS, NZ),
        20,
        2,
        grid=(1,),
        in_specs=[
            whole(DEV * V_ROWS, 128),
            whole(16, 128),
            whole(3, COLS, NZ),
            pl.BlockSpec((1, 3, COLS, NZ), lambda i: (0, 0, 0, 0)),
        ],
        out_specs=whole(3, COLS, NZ),
    )(returned.reshape(DEV * V_ROWS, 128), wanted_t, hess, slopes)
    return out.reshape(3, 16, 16, NZ)


def solution(mesh):
    return jax.shard_map(
        per_device,
        mesh=mesh,
        in_specs=(
            P(None, "gx", "gy", None),
            P(None, "gx", "gy", None),
            P(None, None, "gx", "gy", None),
            P(None, "gx", "gy", None, None),
            P(None, "gx", "gy", None),
        ),
        out_specs=P(None, "gx", "gy", None),
        check_vma=False,
    )
```

time: 237 us -> 133 us (0.56)
  local copies, waits for them, and re-layouts: 62.8 us -> 19 us
  other arithmetic: 38.7 us -> 2.21 us
  starting transfers between devices: 59.6 us -> 29.3 us
  Pallas kernels: 0 us -> 18.4 us
  waiting for transfers between devices: 74.1 us -> 63.1 us
    all_to_all x6 -> x3, waiting for transfers between devices: 55.4 us -> 27 us  [exchange(): return lax.all_to_all(value, AXES, split_axis=0, concat_axis=0, tiled=True)]
    slice x34 -> x5, local copies, waits for them, and re-layouts: 23.7 us -> 4.48 us  [the longest x4 3.3 us: per_device(): lax.slice_in_dim(v, lo, hi, axis=dim)]
    all_to_all x6 -> x3, starting transfers between devices: 41.4 us -> 22.6 us  [exchange(): return lax.all_to_all(value, AXES, split_axis=0, concat_axis=0, tiled=True)]
    pallas_call x0 -> x6, Pallas kernels: none -> 18.4 us  [the longest x1 8.89 us: per_device(): call(stencil_kernel, (struct(2, 3, 16, 16, NZ), struct(2, 16, 16, NZ), st...]
    ppermute x12 -> x4, waiting for transfers between devices: 18.6 us -> 36.1 us  [neighbours(): return (lax.ppermute(last, axis, up), lax.ppermute(first, axis, down))]
    reshape x10 -> x1, local copies, waits for them, and re-layouts: 15.8 us -> 0.12 us  [per_device(): owner_col = owners.reshape(2, COLS, 1)]
    scatter-add x2 -> x0, other arithmetic: 14.1 us -> none  [push_field(): return jnp.zeros_like(values).at[asked].add(arrived)]
    ppermute x12 -> x4, starting transfers between devices: 18.2 us -> 6.71 us  [neighbours(): return (lax.ppermute(last, axis, up), lax.ppermute(first, axis, down))]
  transfers between devices with their start and end apart: 18 -> 7, of which waited for: 9 -> 5; matrix products, arithmetic and copies ran while one was open for 22% -> 5% of each run, Pallas kernels for 0% -> 9%
where the time goes in v1:
time: 133 us; the launch traced here: 132 us
  waiting for transfers between devices  63.1 us (47%)
  starting transfers between devices  29.3 us (22%)
  local copies, waits for them, and re-layouts  19 us (14%)
  Pallas kernels  18.4 us (14%)
  other arithmetic  2.21 us (2%)
    ppermute x4, waiting for transfers between devices, neighbours(): return (lax.ppermute(last, axis, up), lax.ppermute(first, axis, down))  36.1 us
    all_to_all x3, waiting for transfers between devices, exchange(): return lax.all_to_all(value, AXES, split_axis=0, concat_axis=0, tiled=True)  27 us
    all_to_all x3, starting transfers between devices, exchange(): return lax.all_to_all(value, AXES, split_axis=0, concat_axis=0, tiled=True)  22.6 us
    unnamed x34, local copies, waits for them, and re-layouts  14.4 us
    pallas_call x1, Pallas kernels, per_device(): call(stencil_kernel, (struct(2, 3, 16, 16, NZ), struct(2, 16, 16, NZ), st...  8.89 us
    ppermute x4, starting transfers between devices, neighbours(): return (lax.ppermute(last, axis, up), lax.ppermute(first, axis, down))  6.71 us
    pallas_call x1, Pallas kernels, per_device(): call(middle_kernel, (struct(COLS, NZ), struct(DEV * V_ROWS, 128)), 24, 3,...  3.65 us
    slice x4, local copies, waits for them, and re-layouts, per_device(): lax.slice_in_dim(v, lo, hi, axis=dim)  3.3 us
  transfers between devices with their start and end apart: 7, of which 5 were waited for; matrix products, arithmetic and copies ran while one was open for 5% of the time, Pallas kernels for 9%

profile of v1, /device:TPU:1, one launch (start us, length us, event | category | flops | bytes accessed | tf_op | source)
XLA Modules:
  0.0 132.2 jit_solution(12016819752523387439)
XLA Ops:
  2.2 1.2 copy-done.1
  4.3 1.6 %copy-done = f32[6272,128]{1,0:T(8,128)} copy-done((f32[6272,128]{1,0:T(8,128)}, f32[6272,128]{1,0:T(8,128)S(1)}, u32[]{:S(2)}) %copy-start) | copy-done | bytes 3211288
  5.9 11.5 %all-to-all-start = ((f32[128,49,1,128]{3,2,1,0:T(1,128)}), f32[128,49,1,128]{3,2,1,0:T(1,128)S(1)}, u32[]{:S(2)}, u32[]{:S(2)}) async-start(f32[128,49,1,128]{3,2,1,0:T(1,128)} %bitcast.19), calls=%async_computation | async-start | bytes 6422528 | tf_op jit(solution)/shard_map/all_to_all | solution.py:228
  17.4 1.1 fusion.3
  18.5 1.1 fusion.1
  19.6 1.8 %collective-permute-start = (f32[5,4,16,256]{3,2,1,0:T(8,128)S(1)}, f32[5,4,16,256]{3,2,1,0:T(8,128)S(1)}, u32[]{:S(2)}, u32[]{:S(2)}) collective-permute-start(f32[5,4,16,256]{3,2,1,0:T(8,128)S(1)} %pad_maximum_fusion), channel_id=1, source_target_pairs={{0,16},{16,32},{32,48},{48,64},{64,80},{80,96},{96,112},{112,0},{1... | collective-permute-start | bytes 983048 | tf_op jit(solution)/shard_map/ppermute | solution.py:235
  21.4 1.1 fusion.2
  22.7 1.3 collective-permute-start.2
  24.1 3.7 %collective-permute-start.3 = (f32[5,16,4,256]{3,2,1,0:T(4,128)S(1)}, f32[5,16,4,256]{3,2,1,0:T(4,128)S(1)}, u32[]{:S(2)}, u32[]{:S(2)}) collective-permute-start(f32[5,16,4,256]{3,2,1,0:T(4,128)S(1)} %pad_maximum_fusion.3), channel_id=1, source_target_pairs={{1,0},{2,1},{3,2},{4,3},{5,4},{6,5},{7,6},{8,7},{9,8},{10,9},{11,1... | collective-permute-start | bytes 983048 | tf_op jit(solution)/shard_map/ppermute | solution.py:235
  27.7 27.6 %collective-permute-done.xlo_ref = f32[5,4,16,256]{3,2,1,0:T(8,128)S(1)} collective-permute-done((f32[5,4,16,256]{3,2,1,0:T(8,128)S(1)}, f32[5,4,16,256]{3,2,1,0:T(8,128)S(1)}, u32[]{:S(2)}, u32[]{:S(2)}) %collective-permute-start) | collective-permute-done | bytes 327712 | tf_op jit(solution)/shard_map/ppermute | solution.py:235
  55.3 2.2 %collective-permute-done.1.xhi_ref = f32[5,4,16,256]{3,2,1,0:T(8,128)S(1)} collective-permute-done((f32[5,4,16,256]{3,2,1,0:T(8,128)S(1)}, f32[5,4,16,256]{3,2,1,0:T(8,128)S(1)}, u32[]{:S(2)}, u32[]{:S(2)}) %collective-permute-start.1) | collective-permute-done | bytes 327712 | tf_op jit(solution)/shard_map/ppermute | solution.py:235
  57.5 6.2 %collective-permute-done.2.ylo_ref = f32[5,16,4,256]{3,2,1,0:T(4,128)S(1)} collective-permute-done((f32[5,16,4,256]{3,2,1,0:T(4,128)S(1)}, f32[5,16,4,256]{3,2,1,0:T(4,128)S(1)}, u32[]{:S(2)}, u32[]{:S(2)}) %collective-permute-start.2) | collective-permute-done | bytes 327712 | tf_op jit(solution)/shard_map/ppermute | solution.py:235
  63.8 8.9 %shard_map.56 = (f32[2,3,16,16,256]{4,3,2,1,0:T(8,128)S(1)}, f32[2,16,16,256]{3,2,1,0:T(8,128)S(1)}, f32[3,16,16,256]{3,2,1,0:T(8,128)S(1)}) custom-call(f32[2,16,16,256]{3,2,1,0:T(8,128)S(1)} %copy-done.10, f32[3,16,16,256]{3,2,1,0:T(8,128)S(1)} %copy-done.5, f32[5,4,16,256]{3,2,1,0:T(8,128)S(1)} %collective-permute-done.xlo_ref, ...), custom_call_target="tpu_custom_call" | custom-call | flops 600000000 | bytes 12000000 | tf_op jit(solution)/shard_map/pallas_call | solution.py:262
  72.7 1.1 copy-done.3
  74.6 0.9 copy-done.14
  75.6 1.0 copy-done.8
  76.6 1.1 shard_map.57
  77.7 0.9 copy-done.6
  78.6 6.8 %all-to-all-start.1 = ((f32[128,6,2,128]{3,2,1,0:T(2,128)}), f32[128,6,2,128]{3,2,1,0:T(2,128)}, u32[]{:S(2)}, u32[]{:S(2)}) async-start(f32[128,6,2,128]{3,2,1,0:T(2,128)} %bitcast.22), calls=%async_computation.1 | async-start | bytes 1572864 | tf_op jit(solution)/shard_map/all_to_all | solution.py:228
  85.4 2.5 %shard_map.58 = (f32[4,256,256]{2,1,0:T(8,128)S(1)}, f32[16,128]{1,0:T(8,128)S(1)}) custom-call(f32[6272,128]{1,0:T(8,128)S(1)} %bitcast.18), custom_call_target="tpu_custom_call" | custom-call | flops 400000000 | bytes 8000000 | tf_op jit(solution)/shard_map/pallas_call | solution.py:285
  87.9 1.0 copy-done.11
  88.9 12.8 %all-to-all-done.1 = f32[128,6,2,128]{3,2,1,0:T(2,128)} async-done(((f32[128,6,2,128]{3,2,1,0:T(2,128)}), f32[128,6,2,128]{3,2,1,0:T(2,128)}, u32[]{:S(2)}, u32[]{:S(2)}) %all-to-all-start.1) | async-done | bytes 786464 | tf_op jit(solution)/shard_map/all_to_all | solution.py:228
  101.7 1.2 copy-done.2
  102.9 1.0 copy-done.9
  103.9 1.2 copy-done.12
  105.2 3.6 %shard_map.59 = (f32[256,256]{1,0:T(8,128)S(1)}, f32[1536,128]{1,0:T(8,128)S(1)}) custom-call(f32[1536,128]{1,0:T(8,128)} %bitcast.3.arr_ref, s32[2,256,1]{2,1,0:T(8,128)S(1)} %reshape.55.oc_ref, s32[2,256]{1,0:T(2,128)S(1)} %bitcast.27, bf16[2,4,16,16,256]{4,3,2,1,0:T(8,128)(2,1)S(1)} %copy-done.2, f32[2,256,256]{2,1,0:T(8,128)S(1)} %bitcast.24, ...), custom_call_target="tpu_custom_call" | custom-call | flops 300000000 | bytes 6000000 | tf_op jit(solution)/shard_map/pallas_call | solution.py:293
  108.8 0.9 copy-done.13
  109.7 4.4 %all-to-all-start.2 = ((f32[128,6,2,128]{3,2,1,0:T(2,128)}), f32[128,6,2,128]{3,2,1,0:T(2,128)S(1)}, u32[]{:S(2)}, u32[]{:S(2)}) async-start(f32[128,6,2,128]{3,2,1,0:T(2,128)} %bitcast.25), calls=%async_computation.2 | async-start | bytes 1572864 | tf_op jit(solution)/shard_map/all_to_all | solution.py:228
  114.1 1.2 slice.36
  115.3 1.3 bitcast_subtract_fusion.h_ref
  116.6 14.2 %all-to-all-done.2 = f32[128,6,2,128]{3,2,1,0:T(2,128)S(1)} async-done(((f32[128,6,2,128]{3,2,1,0:T(2,128)}), f32[128,6,2,128]{3,2,1,0:T(2,128)S(1)}, u32[]{:S(2)}, u32[]{:S(2)}) %all-to-all-start.2) | async-done | bytes 786464 | tf_op jit(solution)/shard_map/all_to_all | solution.py:228
  130.8 1.4 %shard_map.60 = f32[3,256,256]{2,1,0:T(8,128)} custom-call(f32[1536,128]{1,0:T(8,128)S(1)} %bitcast.21, f32[16,128]{1,0:T(8,128)S(1)} %get-tuple-element.15.wt_ref, f32[3,256,256]{2,1,0:T(8,128)S(1)} %bitcast_subtract_fusion.h_ref, f32[2,3,256,256]{3,2,1,0:T(8,128)S(1)} %bitcast.20), custom_call_target="tpu_custom_call" | custom-call | flops 200000000 | bytes 4000000 | tf_op jit(solution)/shard_map/pallas_call | solution.py:312
  (34 shorter events, 4.2 us)
Async XLA Ops:
  2.2 1.2 copy-start.1
  4.3 1.7 %copy-start = (f32[6272,128]{1,0:T(8,128)}, f32[6272,128]{1,0:T(8,128)S(1)}, u32[]{:S(2)}) copy-start(f32[6272,128]{1,0:T(8,128)S(1)} %shard_map.55) | copy-start | bytes 9633796
  5.9 69.6 %all-to-all-start = ((f32[128,49,1,128]{3,2,1,0:T(1,128)}), f32[128,49,1,128]{3,2,1,0:T(1,128)S(1)}, u32[]{:S(2)}, u32[]{:S(2)}) async-start(f32[128,49,1,128]{3,2,1,0:T(1,128)} %bitcast.19), calls=%async_computation | async-start | bytes 6422528 | tf_op jit(solution)/shard_map/all_to_all | solution.py:228
  17.4 5.1 %copy-start.5 = (f32[3,16,16,256]{3,2,1,0:T(8,128)S(1)}, f32[3,16,16,256]{3,2,1,0:T(8,128)}, u32[]{:S(2)}) copy-start(f32[3,16,16,256]{3,2,1,0:T(8,128)} %ve_ref.1) | copy-start | bytes 2359300
  17.4 46.3 %copy-start.10 = (f32[2,16,16,256]{3,2,1,0:T(8,128)S(1)}, f32[2,16,16,256]{3,2,1,0:T(8,128)}, u32[]{:S(2)}) copy-start(f32[2,16,16,256]{3,2,1,0:T(8,128)} %st_ref.1) | copy-start | bytes 1572868
  19.6 35.7 %collective-permute-start = (f32[5,4,16,256]{3,2,1,0:T(8,128)S(1)}, f32[5,4,16,256]{3,2,1,0:T(8,128)S(1)}, u32[]{:S(2)}, u32[]{:S(2)}) collective-permute-start(f32[5,4,16,256]{3,2,1,0:T(8,128)S(1)} %pad_maximum_fusion), channel_id=1, source_target_pairs={{0,16},{16,32},{32,48},{48,64},{64,80},{80,96},{96,112},{112,0},{1... | collective-permute-start | bytes 983048 | tf_op jit(solution)/shard_map/ppermute | solution.py:235
  21.4 36.1 %collective-permute-start.1 = (f32[5,4,16,256]{3,2,1,0:T(8,128)S(1)}, f32[5,4,16,256]{3,2,1,0:T(8,128)S(1)}, u32[]{:S(2)}, u32[]{:S(2)}) collective-permute-start(f32[5,4,16,256]{3,2,1,0:T(8,128)S(1)} %pad_maximum_fusion.1), channel_id=1, source_target_pairs={{16,0},{32,16},{48,32},{64,48},{80,64},{96,80},{112,96},{0,112},{1... | collective-permute-start | bytes 983048 | tf_op jit(solution)/shard_map/ppermute | solution.py:235
  22.7 41.1 %collective-permute-start.2 = (f32[5,16,4,256]{3,2,1,0:T(4,128)S(1)}, f32[5,16,4,256]{3,2,1,0:T(4,128)S(1)}, u32[]{:S(2)}, u32[]{:S(2)}) collective-permute-start(f32[5,16,4,256]{3,2,1,0:T(4,128)S(1)} %pad_maximum_fusion.2), channel_id=1, source_target_pairs={{0,1},{1,2},{2,3},{3,4},{4,5},{5,6},{6,7},{7,8},{8,9},{9,10},{10,1... | collective-permute-start | bytes 983048 | tf_op jit(solution)/shard_map/ppermute | solution.py:235
  24.1 39.7 %collective-permute-start.3 = (f32[5,16,4,256]{3,2,1,0:T(4,128)S(1)}, f32[5,16,4,256]{3,2,1,0:T(4,128)S(1)}, u32[]{:S(2)}, u32[]{:S(2)}) collective-permute-start(f32[5,16,4,256]{3,2,1,0:T(4,128)S(1)} %pad_maximum_fusion.3), channel_id=1, source_target_pairs={{1,0},{2,1},{3,2},{4,3},{5,4},{6,5},{7,6},{8,7},{9,8},{10,9},{11,1... | collective-permute-start | bytes 983048 | tf_op jit(solution)/shard_map/ppermute | solution.py:235
  72.7 1.2 copy-start.3
  73.8 0.8 copy-start.7
  74.6 0.9 copy-start.14
  75.5 1.0 copy-start.8
  77.7 0.9 copy-start.6
  78.6 23.1 %all-to-all-start.1 = ((f32[128,6,2,128]{3,2,1,0:T(2,128)}), f32[128,6,2,128]{3,2,1,0:T(2,128)}, u32[]{:S(2)}, u32[]{:S(2)}) async-start(f32[128,6,2,128]{3,2,1,0:T(2,128)} %bitcast.22), calls=%async_computation.1 | async-start | bytes 1572864 | tf_op jit(solution)/shard_map/all_to_all | solution.py:228
  87.9 1.0 copy-start.11
  101.7 1.2 copy-start.2
  102.9 1.0 copy-start.9
  103.9 1.2 copy-start.12
  108.8 0.9 copy-start.13
  109.7 5.6 %copy-start.15 = (f32[256,256]{1,0:T(8,128)}, f32[256,256]{1,0:T(8,128)S(1)}, u32[]{:S(2)}) copy-start(f32[256,256]{1,0:T(8,128)S(1)} %get-tuple-element.17) | copy-start | bytes 786436
  109.7 21.1 %copy-start.4 = (f32[2,3,16,16,256]{4,3,2,1,0:T(8,128)S(1)}, f32[2,3,16,16,256]{4,3,2,1,0:T(8,128)}, u32[]{:S(2)}) copy-start(f32[2,3,16,16,256]{4,3,2,1,0:T(8,128)} %copy-done.3) | copy-start | bytes 4718596
  109.7 21.1 %all-to-all-start.2 = ((f32[128,6,2,128]{3,2,1,0:T(2,128)}), f32[128,6,2,128]{3,2,1,0:T(2,128)S(1)}, u32[]{:S(2)}, u32[]{:S(2)}) async-start(f32[128,6,2,128]{3,2,1,0:T(2,128)} %bitcast.25), calls=%async_computation.2 | async-start | bytes 1572864 | tf_op jit(solution)/shard_map/all_to_all | solution.py:228

commit v2 on v1

v2 whole, which is shorter than its diff:
```python
import jax
import jax.numpy as jnp
from jax import lax
from jax.experimental import pallas as pl
from jax.experimental.pallas import tpu as pltpu
from jax.sharding import PartitionSpec as P

FIRST = (0.8, -0.2, 4.0 / 105.0, -1.0 / 280.0)
SECOND = (-205.0 / 72.0, 1.6, -0.2, 8.0 / 315.0, -1.0 / 560.0)
BETA = 0.05
AXES = ("gx", "gy")
CAP = 6
DEV = 128
COLS = 256
NZ = 256
F32 = jnp.float32
BF16 = jnp.bfloat16
W_ROWS = CAP * 8
A_ROWS = W_ROWS + 1
V_ROWS = CAP * 2
PART = 32


def call(kernel, out_shape, mib, micros, **kw):
    return pl.pallas_call(
        kernel,
        out_shape=out_shape,
        compiler_params=pltpu.CompilerParams(vmem_limit_bytes=mib * 1024 * 1024),
        cost_estimate=pl.CostEstimate(
            flops=int(micros * 1e8), bytes_accessed=int(micros * 2e6), transcendentals=0
        ),
        **kw,
    )


def iota(shape, dim):
    return lax.broadcasted_iota(jnp.int32, shape, dim)


def dot(a, b):
    return jnp.dot(a, b, preferred_element_type=F32)


def split3(x):
    hi = x.astype(BF16)
    rest = x - hi.astype(F32)
    mid = rest.astype(BF16)
    low = (rest - mid.astype(F32)).astype(BF16)
    return hi, mid, low


def select(onehot, parts):
    return sum(dot(onehot, part) for part in parts)


def ones(mask):
    return jnp.where(mask, 1.0, 0.0).astype(BF16)


def masks_by_owner(owner_row, first, count):
    match = iota((count, COLS), 0) + first == owner_row
    before = ones(iota((COLS, COLS), 0) < iota((COLS, COLS), 1))
    slot = dot(ones(match), before)
    return [match & (slot == float(s)) for s in range(CAP)]


def masks_by_column(owner_row):
    spread = jnp.broadcast_to(owner_row.astype(F32), (DEV, COLS)).T
    match = iota((COLS, DEV), 1).astype(F32) == spread
    before = ones(iota((COLS, COLS), 1) < iota((COLS, COLS), 0))
    slot = dot(before, ones(match))
    return [match & (slot == float(s)) for s in range(CAP)]


def put_slots(out_ref, start, values, count):
    for s in range(CAP):
        for half in range(2):
            out_ref[pl.ds(start + s * 2 + half, count, stride=V_ROWS), :] = values[
                s * count : (s + 1) * count, half * 128 : half * 128 + 128
            ]


def request_kernel(or_ref, sr_ref, w_ref, out_ref):
    first = pl.program_id(0) * PART
    lane = iota((PART, 128), 1)
    wanted = jnp.zeros((PART, 128), F32)
    for j in range(2):
        masks = masks_by_owner(or_ref[j], first, PART)
        source_row = sr_ref[j].astype(F32)
        for s in range(CAP):
            column = jnp.sum(jnp.where(masks[s], source_row, 0.0), axis=1, keepdims=True)
            wanted = jnp.where(lane == 8 * j + s, column, wanted)
    onehot = jnp.concatenate([ones(m) for m in masks], axis=0)
    for k in range(4):
        placed = dot(onehot, w_ref[0, k].reshape(COLS, NZ))
        for s in range(CAP):
            for half in range(2):
                out_ref[pl.ds(s * 8 + k * 2 + half, PART, stride=A_ROWS), :] = placed[
                    s * PART : (s + 1) * PART, half * 128 : half * 128 + 128
                ]
    out_ref[pl.ds(W_ROWS, PART, stride=A_ROWS), :] = wanted


def stencil_kernel(st_ref, ve_ref, xlo_ref, xhi_ref, ylo_ref, yhi_ref, g_ref, b_ref, h_ref, xpad, ypad):
    step_len = 0.5
    for field in range(5):
        source = st_ref.at[field] if field < 2 else ve_ref.at[field - 2]
        xpad[0:4] = xlo_ref[field]
        xpad[4:20] = source[...]
        xpad[20:24] = xhi_ref[field]
        ypad[:, 4:8] = ylo_ref[field]
        ypad[:, 8:24] = source[...]
        ypad[:, 24:28] = yhi_ref[field]

        def row(x, carry, field=field):
            centre = xpad[x + 4]
            sign = -1.0 if field < 2 else 1.0
            parts = [jnp.zeros_like(centre) for _ in range(3)]
            coeffs = FIRST if field < 2 else SECOND[1:]
            for k in range(4):
                d = k + 1
                parts[0] += coeffs[k] * (xpad[x + 4 + d] + sign * xpad[x + 4 - d])
                parts[1] += coeffs[k] * (ypad[x, 8 + d : 24 + d, :] + sign * ypad[x, 8 - d : 24 - d, :])
                parts[2] += coeffs[k] * (
                    pltpu.roll(centre, NZ - d, 1) + sign * pltpu.roll(centre, d, 1)
                )
            if field < 2:
                for c in range(3):
                    g_ref[field, c, x] = parts[c]
                dot = ve_ref[0, x] * parts[0] + ve_ref[1, x] * parts[1] + ve_ref[2, x] * parts[2]
                b_ref[field, x] = -step_len * dot
            else:
                total = 3.0 * SECOND[0] * centre + parts[0] + parts[1] + parts[2]
                h_ref[field - 2, x] = -BETA * total
            return carry

        lax.fori_loop(0, 16, row, 0)


def supply_kernel(idx_ref, b_ref, out_ref):
    wanted = idx_ref[:, 0, 0, :]
    place = iota((PART, COLS), 1).astype(F32)
    onehot = jnp.concatenate([ones(wanted[:, s : s + 1] == place) for s in range(CAP)], axis=0)
    put_slots(out_ref, 0, select(onehot, split3(b_ref[0])), PART)


def gathered_rows(wanted_t, first):
    place = iota((COLS, DEV), 0).astype(F32)
    return jnp.concatenate(
        [ones(place == wanted_t[first + s : first + s + 1, :]) for s in range(CAP)], axis=1
    )


def normal_kernel(a_ref, d_ref, wt_ref, w_scr):
    wanted_t = a_ref[pl.ds(W_ROWS, DEV, stride=A_ROWS), :].T
    wt_ref[...] = wanted_t[:16]
    onehot_t = gathered_rows(wanted_t, 8)
    for k in range(4):
        for s in range(CAP):
            for half in range(2):
                w_scr[k, s * DEV : (s + 1) * DEV, half * 128 : half * 128 + 128] = a_ref[
                    pl.ds(s * 8 + k * 2 + half, DEV, stride=A_ROWS), :
                ]
    for m in range(4):
        total = None
        for k in range(4 - m):
            product = w_scr[k] * w_scr[k + m]
            high = product.astype(BF16)
            low = (product - high.astype(F32)).astype(BF16)
            part = dot(onehot_t, high) + dot(onehot_t, low)
            if k != 1:
                part = pltpu.roll(part, (k - 1) % NZ, 1)
            total = part if total is None else total + part
        d_ref[m] = total


def read_slots(ref):
    return jnp.concatenate(
        [
            jnp.concatenate(
                [ref[pl.ds(s * 2 + half, DEV, stride=V_ROWS), :] for half in range(2)], axis=1
            )
            for s in range(CAP)
        ],
        axis=0,
    )


def middle_kernel(arr_hbm, own_hbm, w_hbm, b_hbm, d_hbm, lam_hbm, out_hbm, arr, own, w, b, d, lam_scr, out, parts, sems):
    copies = [
        pltpu.make_async_copy(source, target, sems.at[i])
        for i, (source, target) in enumerate(
            ((own_hbm.at[0], own), (arr_hbm, arr), (w_hbm.at[0], w), (b_hbm.at[1], b), (d_hbm, d))
        )
    ]
    for copy in copies:
        copy.start()
    copies[0].wait()
    owner_row = own[...]
    taken = jnp.concatenate([ones(m) for m in masks_by_column(owner_row)], axis=1)
    masks = masks_by_owner(owner_row, 0, DEV)
    copies[1].wait()
    mine_all = select(taken, split3(read_slots(arr)))
    for copy in copies[2:]:
        copy.wait()
    rows = 64
    for start in range(0, COLS, rows):
        here = slice(start, start + rows)
        mine = mine_all[here]
        weights = [
            w[k, start // 16 : (start + rows) // 16].reshape(rows, NZ).astype(F32) for k in range(4)
        ]
        field = b[here]
        for k in range(4):
            field += weights[k] * (mine if k == 1 else pltpu.roll(mine, (1 - k) % NZ, 1))
        lam = d[0, here] * field
        for m in range(1, 4):
            lam += d[m, here] * pltpu.roll(field, NZ - m, 1) + pltpu.roll(d[m, here] * field, m, 1)
        lam_scr[here] = lam
        spread = weights[1] * lam
        for k in (0, 2, 3):
            spread += pltpu.roll(weights[k] * lam, (k - 1) % NZ, 1)
        for i, part in enumerate(split3(spread)):
            parts[i, here] = part
    lam_copy = pltpu.make_async_copy(lam_scr, lam_hbm, sems.at[0])
    lam_copy.start()
    sent = []
    for i, first in enumerate(range(0, DEV, PART)):
        onehot = jnp.concatenate([ones(m[first : first + PART]) for m in masks], axis=0)
        values = select(onehot, [parts[p] for p in range(3)])
        put_slots(out, first * V_ROWS, values, PART)
        block = pl.ds(first * V_ROWS, PART * V_ROWS)
        copy = pltpu.make_async_copy(out.at[block], out_hbm.at[block], sems.at[1 + i])
        copy.start()
        sent.append(copy)
    lam_copy.wait()
    for copy in sent:
        copy.wait()


def final_kernel(arr_hbm, wt_hbm, h_hbm, g_hbm, out_hbm, arr, wt, h, g, out, sems):
    copies = [
        pltpu.make_async_copy(source, target, sems.at[i])
        for i, (source, target) in enumerate(
            ((wt_hbm, wt), (arr_hbm, arr), (h_hbm, h), (g_hbm.at[0], g))
        )
    ]
    for copy in copies:
        copy.start()
    copies[0].wait()
    onehot_t = gathered_rows(wt[...], 0)
    copies[1].wait()
    lam = select(onehot_t, split3(read_slots(arr)))
    copies[2].wait()
    copies[3].wait()
    sent = []
    for c in range(3):
        out[c] = h[c] - 0.5 * (lam * g[c])
        copy = pltpu.make_async_copy(out.at[c], out_hbm.at[c], sems.at[c])
        copy.start()
        sent.append(copy)
    for copy in sent:
        copy.wait()


def exchange(value):
    return lax.all_to_all(value, AXES, split_axis=0, concat_axis=0, tiled=True)


def neighbours(first, last, axis):
    count = lax.axis_size(axis)
    up = [(i, (i + 1) % count) for i in range(count)]
    down = [(j, i) for i, j in up]
    return lax.ppermute(last, axis, up), lax.ppermute(first, axis, down)


def per_device(state_path, velocity, weights, owners, sources):
    owner_row = owners.reshape(2, 1, COLS)
    source_row = sources.reshape(2, 1, COLS)
    whole = lambda *shape: pl.BlockSpec(shape, lambda i: (0,) * len(shape))
    blocks = lambda *shape: pl.BlockSpec(shape, lambda i: (i,) + (0,) * (len(shape) - 1))
    hbm = pl.BlockSpec(memory_space=pltpu.HBM)
    struct = lambda *shape: jax.ShapeDtypeStruct(shape, F32)

    faces = lambda lo, hi, dim: jnp.concatenate(
        [lax.slice_in_dim(v, lo, hi, axis=dim) for v in (state_path, velocity)], axis=0
    )
    xlo, xhi = neighbours(faces(0, 4, 1), faces(12, 16, 1), "gx")
    ylo, yhi = neighbours(faces(0, 4, 2), faces(12, 16, 2), "gy")

    request = call(
        request_kernel,
        struct(DEV * A_ROWS, 128),
        60,
        3,
        grid=(DEV // PART,),
        in_specs=[
            whole(2, 1, COLS),
            whole(2, 1, COLS),
            pl.BlockSpec((1, 4, 16, 16, NZ), lambda i: (1, 0, 0, 0, 0)),
        ],
        out_specs=blocks(PART * A_ROWS, 128),
    )(owner_row, source_row, weights)
    request, xlo, xhi, ylo, yhi = lax.optimization_barrier((request, xlo, xhi, ylo, yhi))
    asked = exchange(request.reshape(DEV, A_ROWS, 1, 128))

    slopes, before, hess = call(
        stencil_kernel,
        (struct(2, 3, 16, 16, NZ), struct(2, 16, 16, NZ), struct(3, 16, 16, NZ)),
        24,
        9,
        scratch_shapes=[pltpu.VMEM((24, 16, NZ), F32), pltpu.VMEM((16, 32, NZ), F32)],
    )(state_path, velocity, xlo, xhi, ylo, yhi)
    slopes = slopes.reshape(2, 3, COLS, NZ)
    before = before.reshape(2, COLS, NZ)
    hess = hess.reshape(3, COLS, NZ)

    supply = call(
        supply_kernel,
        struct(DEV * V_ROWS, 128),
        60,
        2,
        grid=(DEV // PART,),
        in_specs=[
            pl.BlockSpec((PART, 1, 1, 128), lambda i: (i, W_ROWS, 0, 0)),
            pl.BlockSpec((1, COLS, NZ), lambda i: (0, 0, 0)),
        ],
        out_specs=blocks(PART * V_ROWS, 128),
    )(asked, before)
    arrived = exchange(supply.reshape(DEV, CAP, 2, 128))

    normal, wanted_t = call(
        normal_kernel,
        (struct(4, COLS, NZ), struct(16, 128)),
        60,
        4,
        grid=(1,),
        in_specs=[whole(DEV * A_ROWS, 128)],
        out_specs=(whole(4, COLS, NZ), whole(16, 128)),
        scratch_shapes=[pltpu.VMEM((4, CAP * DEV, NZ), F32)],
    )(asked.reshape(DEV * A_ROWS, 128))

    lam, push = call(
        middle_kernel,
        (struct(COLS, NZ), struct(DEV * V_ROWS, 128)),
        60,
        4,
        in_specs=[hbm] * 5,
        out_specs=(hbm, hbm),
        scratch_shapes=[
            pltpu.VMEM((DEV * V_ROWS, 128), F32),
            pltpu.VMEM((1, COLS), jnp.int32),
            pltpu.VMEM((4, 16, 16, NZ), BF16),
            pltpu.VMEM((COLS, NZ), F32),
            pltpu.VMEM((4, COLS, NZ), F32),
            pltpu.VMEM((COLS, NZ), F32),
            pltpu.VMEM((DEV * V_ROWS, 128), F32),
            pltpu.VMEM((3, COLS, NZ), BF16),
            pltpu.SemaphoreType.DMA((5,)),
        ],
    )(arrived.reshape(DEV * V_ROWS, 128), owner_row, weights, before, normal)
    returned = exchange(push.reshape(DEV, CAP, 2, 128))

    hess = hess - 0.5 * (lam[None] * slopes[1])
    out = call(
        final_kernel,
        struct(3, COLS, NZ),
        60,
        2,
        in_specs=[hbm] * 4,
        out_specs=hbm,
        scratch_shapes=[
            pltpu.VMEM((DEV * V_ROWS, 128), F32),
            pltpu.VMEM((16, 128), F32),
            pltpu.VMEM((3, COLS, NZ), F32),
            pltpu.VMEM((3, COLS, NZ), F32),
            pltpu.VMEM((3, COLS, NZ), F32),
            pltpu.SemaphoreType.DMA((4,)),
        ],
    )(returned.reshape(DEV * V_ROWS, 128), wanted_t, hess, slopes)
    return out.reshape(3, 16, 16, NZ)


def solution(mesh):
    return jax.shard_map(
        per_device,
        mesh=mesh,
        in_specs=(
            P(None, "gx", "gy", None),
            P(None, "gx", "gy", None),
            P(None, None, "gx", "gy", None),
            P(None, "gx", "gy", None, None),
            P(None, "gx", "gy", None),
        ),
        out_specs=P(None, "gx", "gy", None),
        check_vma=False,
    )
```

time: 133 us -> 128 us (0.962)
  Pallas kernels: 18.4 us -> 29.1 us
  waiting for transfers between devices: 63.1 us -> 55.3 us
  local copies, waits for them, and re-layouts: 19 us -> 12.1 us
    ppermute x4, waiting for transfers between devices: 36.1 us -> 0.97 us  [neighbours(): return (lax.ppermute(last, axis, up), lax.ppermute(first, axis, down))]
    all_to_all x3, waiting for transfers between devices: 27 us -> 54.4 us  [exchange(): return lax.all_to_all(value, AXES, split_axis=0, concat_axis=0, tiled=True)]
    pallas_call x5, Pallas kernels: 9.49 us -> 20.2 us  [the longest x1 5.35 us: per_device(): call(normal_kernel, (struct(4, COLS, NZ), struct(16, 128)), 60, 4, grid=(...]
    unnamed x34 -> x28, local copies, waits for them, and re-layouts: 14.4 us -> 8.76 us
    all_to_all x3, starting transfers between devices: 22.6 us -> 20.7 us  [exchange(): return lax.all_to_all(value, AXES, split_axis=0, concat_axis=0, tiled=True)]
    ppermute x4, starting transfers between devices: 6.71 us -> 8.14 us  [neighbours(): return (lax.ppermute(last, axis, up), lax.ppermute(first, axis, down))]
  transfers between devices with their start and end apart: 7 -> 7, of which waited for: 5 -> 4; matrix products, arithmetic and copies ran while one was open for 5% -> 2% of each run, Pallas kernels for 9% -> 14%
where the time goes in v2:
time: 128 us; the launch traced here: 127 us
  waiting for transfers between devices  55.3 us (43%)
  Pallas kernels  29.1 us (23%)
  starting transfers between devices  28.9 us (23%)
  local copies, waits for them, and re-layouts  12.1 us (9%)
    all_to_all x3, waiting for transfers between devices, exchange(): return lax.all_to_all(value, AXES, split_axis=0, concat_axis=0, tiled=True)  54.4 us
    all_to_all x3, starting transfers between devices, exchange(): return lax.all_to_all(value, AXES, split_axis=0, concat_axis=0, tiled=True)  20.7 us
    pallas_call x1, Pallas kernels, per_device(): call(stencil_kernel, (struct(2, 3, 16, 16, NZ), struct(2, 16, 16, NZ), st...  8.89 us
    unnamed x28, local copies, waits for them, and re-layouts  8.76 us
    ppermute x4, starting transfers between devices, neighbours(): return (lax.ppermute(last, axis, up), lax.ppermute(first, axis, down))  8.14 us
    pallas_call x1, Pallas kernels, per_device(): call(normal_kernel, (struct(4, COLS, NZ), struct(16, 128)), 60, 4, grid=(...  5.35 us
    pallas_call x1, Pallas kernels, per_device(): call(middle_kernel, (struct(COLS, NZ), struct(DEV * V_ROWS, 128)), 60, 4,...  4.25 us
    pallas_call x1, Pallas kernels, per_device(): call(request_kernel, struct(DEV * A_ROWS, 128), 60, 3, grid=(DEV // PART,...  4.07 us
  transfers between devices with their start and end apart: 7, of which 4 were waited for; matrix products, arithmetic and copies ran while one was open for 2% of the time, Pallas kernels for 14%

profile of v2, /device:TPU:1, one launch (start us, length us, event | category | flops | bytes accessed | tf_op | source)
XLA Modules:
  0.0 126.8 jit_solution(1615449128320885813)
XLA Ops:
  0.0 1.1 fusion.1
  1.1 1.0 fusion.3
  2.1 3.0 %collective-permute-start = (f32[5,4,16,256]{3,2,1,0:T(8,128)S(1)}, f32[5,4,16,256]{3,2,1,0:T(8,128)S(1)}, u32[]{:S(2)}, u32[]{:S(2)}) collective-permute-start(f32[5,4,16,256]{3,2,1,0:T(8,128)S(1)} %pad_maximum_fusion), channel_id=1, source_target_pairs={{0,16},{16,32},{32,48},{48,64},{64,80},{80,96},{96,112},{112,0},{1... | collective-permute-start | bytes 983048 | tf_op jit(solution)/shard_map/ppermute | solution.py:274
  5.2 1.2 fusion
  6.5 0.1 pad_maximum_fusion.2
  6.6 1.3 %collective-permute-start.2 = (f32[5,16,4,256]{3,2,1,0:T(4,128)S(1)}, f32[5,16,4,256]{3,2,1,0:T(4,128)S(1)}, u32[]{:S(2)}, u32[]{:S(2)}) collective-permute-start(f32[5,16,4,256]{3,2,1,0:T(4,128)S(1)} %pad_maximum_fusion.2), channel_id=1, source_target_pairs={{0,1},{1,2},{2,3},{3,4},{4,5},{5,6},{6,7},{7,8},{8,9},{9,10},{10,1... | collective-permute-start | bytes 983048 | tf_op jit(solution)/shard_map/ppermute | solution.py:274
  7.9 0.1 pad_maximum_fusion.3
  7.9 3.8 %collective-permute-start.3 = (f32[5,16,4,256]{3,2,1,0:T(4,128)S(1)}, f32[5,16,4,256]{3,2,1,0:T(4,128)S(1)}, u32[]{:S(2)}, u32[]{:S(2)}) collective-permute-start(f32[5,16,4,256]{3,2,1,0:T(4,128)S(1)} %pad_maximum_fusion.3), channel_id=1, source_target_pairs={{1,0},{2,1},{3,2},{4,3},{5,4},{6,5},{7,6},{8,7},{9,8},{10,9},{11,1... | collective-permute-start | bytes 983048 | tf_op jit(solution)/shard_map/ppermute | solution.py:274
  11.7 4.1 %shard_map.55 = f32[6272,128]{1,0:T(8,128)} custom-call(s32[2,1,256]{2,1,0:T(1,128)} %bitcast.23, s32[2,1,256]{2,1,0:T(1,128)} %bitcast.25, bf16[2,4,16,16,256]{4,3,2,1,0:T(8,128)(2,1)} %w_hbm.1), custom_call_target="tpu_custom_call" | custom-call | flops 300000000 | bytes 6000000 | tf_op jit(solution)/shard_map/pallas_call | solution.py:291
  15.8 0.7 copy-done.5
  16.5 1.0 collective-permute-done.2.ylo_ref
  17.5 0.7 copy-done.7
  18.2 0.7 copy-done.9
  19.0 11.5 %all-to-all-start = ((f32[128,49,1,128]{3,2,1,0:T(1,128)}), f32[128,49,1,128]{3,2,1,0:T(1,128)}, u32[]{:S(2)}, u32[]{:S(2)}) async-start(f32[128,49,1,128]{3,2,1,0:T(1,128)} %bitcast.17), calls=%async_computation | async-start | bytes 6422528 | tf_op jit(solution)/shard_map/all_to_all | solution.py:267
  30.5 1.0 copy-done.4
  31.6 1.0 copy-done.6
  32.5 1.0 copy-done.8
  33.5 1.0 copy-done.10
  34.5 8.9 %shard_map.56 = (f32[2,3,16,16,256]{4,3,2,1,0:T(8,128)S(1)}, f32[2,16,16,256]{3,2,1,0:T(8,128)S(1)}, f32[3,16,16,256]{3,2,1,0:T(8,128)S(1)}) custom-call(f32[2,16,16,256]{3,2,1,0:T(8,128)S(1)} %copy-done.4, f32[3,16,16,256]{3,2,1,0:T(8,128)S(1)} %copy-done.2, f32[5,4,16,256]{3,2,1,0:T(8,128)S(1)} %collective-permute-done.xlo_ref, ...), custom_call_target="tpu_custom_call" | custom-call | flops 900000000 | bytes 18000000 | tf_op jit(solution)/shard_map/pallas_call | solution.py:307
  43.4 0.8 copy-done.1
  44.2 27.6 %all-to-all-done.idx_ref = f32[128,49,1,128]{3,2,1,0:T(1,128)} async-done(((f32[128,49,1,128]{3,2,1,0:T(1,128)}), f32[128,49,1,128]{3,2,1,0:T(1,128)}, u32[]{:S(2)}, u32[]{:S(2)}) %all-to-all-start) | async-done | bytes 3211296 | tf_op jit(solution)/shard_map/all_to_all | solution.py:267
  71.8 3.9 %shard_map.57 = f32[1536,128]{1,0:T(8,128)} custom-call(f32[128,49,1,128]{3,2,1,0:T(1,128)} %all-to-all-done.idx_ref, f32[2,256,256]{2,1,0:T(8,128)} %bitcast.15), custom_call_target="tpu_custom_call" | custom-call | flops 200000000 | bytes 4000000 | tf_op jit(solution)/shard_map/pallas_call | solution.py:318
  75.7 4.8 %all-to-all-start.1 = ((f32[128,6,2,128]{3,2,1,0:T(2,128)}), f32[128,6,2,128]{3,2,1,0:T(2,128)S(1)}, u32[]{:S(2)}, u32[]{:S(2)}) async-start(f32[128,6,2,128]{3,2,1,0:T(2,128)} %bitcast.21), calls=%async_computation.1 | async-start | bytes 1572864 | tf_op jit(solution)/shard_map/all_to_all | solution.py:267
  80.5 5.4 %shard_map.58 = (f32[4,256,256]{2,1,0:T(8,128)}, f32[16,128]{1,0:T(8,128)}) custom-call(f32[6272,128]{1,0:T(8,128)} %bitcast.6.a_ref), custom_call_target="tpu_custom_call" | custom-call | flops 400000000 | bytes 8000000 | tf_op jit(solution)/shard_map/pallas_call | solution.py:332
  85.9 11.2 %all-to-all-done.1 = f32[128,6,2,128]{3,2,1,0:T(2,128)S(1)} async-done(((f32[128,6,2,128]{3,2,1,0:T(2,128)}), f32[128,6,2,128]{3,2,1,0:T(2,128)S(1)}, u32[]{:S(2)}, u32[]{:S(2)}) %all-to-all-start.1) | async-done | bytes 786464 | tf_op jit(solution)/shard_map/all_to_all | solution.py:267
  97.1 0.9 copy-done.11
  98.0 4.2 %shard_map.59 = (f32[256,256]{1,0:T(8,128)}, f32[1536,128]{1,0:T(8,128)}) custom-call(f32[1536,128]{1,0:T(8,128)} %bitcast.18, s32[2,1,256]{2,1,0:T(1,128)} %bitcast.24, bf16[2,4,16,16,256]{4,3,2,1,0:T(8,128)(2,1)} %w_hbm.1, f32[2,256,256]{2,1,0:T(8,128)} %bitcast.16, f32[4,256,256]{2,1,0:T(8,128)} %get-tuple-element.23.d_hbm), custom_call_target="tpu_custom_call" | custom-call | flops 400000000 | bytes 8000000 | tf_op jit(solution)/shard_map/pallas_call | solution.py:343
  102.2 4.4 %all-to-all-start.2 = ((f32[128,6,2,128]{3,2,1,0:T(2,128)}), f32[128,6,2,128]{3,2,1,0:T(2,128)S(1)}, u32[]{:S(2)}, u32[]{:S(2)}) async-start(f32[128,6,2,128]{3,2,1,0:T(2,128)} %bitcast.22), calls=%async_computation.2 | async-start | bytes 1572864 | tf_op jit(solution)/shard_map/all_to_all | solution.py:267
  106.7 1.0 bitcast_subtract_fusion.h_hbm
  107.7 15.6 %all-to-all-done.2 = f32[128,6,2,128]{3,2,1,0:T(2,128)S(1)} async-done(((f32[128,6,2,128]{3,2,1,0:T(2,128)}), f32[128,6,2,128]{3,2,1,0:T(2,128)S(1)}, u32[]{:S(2)}, u32[]{:S(2)}) %all-to-all-start.2) | async-done | bytes 786464 | tf_op jit(solution)/shard_map/all_to_all | solution.py:267
  123.3 0.9 copy-done.12
  124.2 2.6 %shard_map.60 = f32[3,256,256]{2,1,0:T(8,128)} custom-call(f32[1536,128]{1,0:T(8,128)} %bitcast.20, f32[16,128]{1,0:T(8,128)} %get-tuple-element.25.wt_hbm, f32[3,256,256]{2,1,0:T(8,128)} %bitcast_subtract_fusion.h_hbm, f32[2,3,256,256]{3,2,1,0:T(8,128)} %bitcast.14), custom_call_target="tpu_custom_call" | custom-call | flops 200000000 | bytes 4000000 | tf_op jit(solution)/shard_map/pallas_call | solution.py:365
  (26 shorter events, 0.2 us)
Async XLA Ops:
  0.0 6.4 %copy-start.3 = (f32[2,16,16,256]{3,2,1,0:T(8,128)S(1)}, f32[2,16,16,256]{3,2,1,0:T(8,128)}, u32[]{:S(2)}) copy-start(f32[2,16,16,256]{3,2,1,0:T(8,128)} %st_ref.1) | copy-start | bytes 1572868
  2.1 13.7 %collective-permute-start = (f32[5,4,16,256]{3,2,1,0:T(8,128)S(1)}, f32[5,4,16,256]{3,2,1,0:T(8,128)S(1)}, u32[]{:S(2)}, u32[]{:S(2)}) collective-permute-start(f32[5,4,16,256]{3,2,1,0:T(8,128)S(1)} %pad_maximum_fusion), channel_id=1, source_target_pairs={{0,16},{16,32},{32,48},{48,64},{64,80},{80,96},{96,112},{112,0},{1... | collective-permute-start | bytes 983048 | tf_op jit(solution)/shard_map/ppermute | solution.py:274
  5.2 10.6 %collective-permute-start.1 = (f32[5,4,16,256]{3,2,1,0:T(8,128)S(1)}, f32[5,4,16,256]{3,2,1,0:T(8,128)S(1)}, u32[]{:S(2)}, u32[]{:S(2)}) collective-permute-start(f32[5,4,16,256]{3,2,1,0:T(8,128)S(1)} %pad_maximum_fusion.1), channel_id=1, source_target_pairs={{16,0},{32,16},{48,32},{64,48},{80,64},{96,80},{112,96},{0,112},{1... | collective-permute-start | bytes 983048 | tf_op jit(solution)/shard_map/ppermute | solution.py:274
  6.6 10.9 %collective-permute-start.2 = (f32[5,16,4,256]{3,2,1,0:T(4,128)S(1)}, f32[5,16,4,256]{3,2,1,0:T(4,128)S(1)}, u32[]{:S(2)}, u32[]{:S(2)}) collective-permute-start(f32[5,16,4,256]{3,2,1,0:T(4,128)S(1)} %pad_maximum_fusion.2), channel_id=1, source_target_pairs={{0,1},{1,2},{2,3},{3,4},{4,5},{5,6},{6,7},{7,8},{8,9},{9,10},{10,1... | collective-permute-start | bytes 983048 | tf_op jit(solution)/shard_map/ppermute | solution.py:274
  7.9 10.3 %collective-permute-start.3 = (f32[5,16,4,256]{3,2,1,0:T(4,128)S(1)}, f32[5,16,4,256]{3,2,1,0:T(4,128)S(1)}, u32[]{:S(2)}, u32[]{:S(2)}) collective-permute-start(f32[5,16,4,256]{3,2,1,0:T(4,128)S(1)} %pad_maximum_fusion.3), channel_id=1, source_target_pairs={{1,0},{2,1},{3,2},{4,3},{5,4},{6,5},{7,6},{8,7},{9,8},{10,9},{11,1... | collective-permute-start | bytes 983048 | tf_op jit(solution)/shard_map/ppermute | solution.py:274
  15.8 0.7 copy-start.5
  17.5 0.7 copy-start.7
  18.2 0.7 copy-start.9
  18.2 12.3 %copy-start.2 = (f32[3,16,16,256]{3,2,1,0:T(8,128)S(1)}, f32[3,16,16,256]{3,2,1,0:T(8,128)}, u32[]{:S(2)}) copy-start(f32[3,16,16,256]{3,2,1,0:T(8,128)} %ve_ref.1) | copy-start | bytes 2359300
  19.0 52.8 %all-to-all-start = ((f32[128,49,1,128]{3,2,1,0:T(1,128)}), f32[128,49,1,128]{3,2,1,0:T(1,128)}, u32[]{:S(2)}, u32[]{:S(2)}) async-start(f32[128,49,1,128]{3,2,1,0:T(1,128)} %bitcast.17), calls=%async_computation | async-start | bytes 6422528 | tf_op jit(solution)/shard_map/all_to_all | solution.py:267
  30.5 1.0 copy-start.4
  31.6 1.0 copy-start.6
  32.5 1.0 copy-start.8
  33.5 1.0 copy-start.10
  43.4 0.8 copy-start.1
  44.2 62.4 %copy-start = (f32[2,3,16,16,256]{4,3,2,1,0:T(8,128)}, f32[2,3,16,16,256]{4,3,2,1,0:T(8,128)S(1)}, u32[]{:S(2)}) copy-start(f32[2,3,16,16,256]{4,3,2,1,0:T(8,128)S(1)} %get-tuple-element.28) | copy-start | bytes 4718596
  75.7 21.4 %all-to-all-start.1 = ((f32[128,6,2,128]{3,2,1,0:T(2,128)}), f32[128,6,2,128]{3,2,1,0:T(2,128)S(1)}, u32[]{:S(2)}, u32[]{:S(2)}) async-start(f32[128,6,2,128]{3,2,1,0:T(2,128)} %bitcast.21), calls=%async_computation.1 | async-start | bytes 1572864 | tf_op jit(solution)/shard_map/all_to_all | solution.py:267
  97.1 0.9 copy-start.11
  102.2 4.5 %copy-start.13 = (f32[256,256]{1,0:T(8,128)S(1)}, f32[256,256]{1,0:T(8,128)}, u32[]{:S(2)}) copy-start(f32[256,256]{1,0:T(8,128)} %get-tuple-element.27) | copy-start | bytes 786436
  102.2 21.1 %all-to-all-start.2 = ((f32[128,6,2,128]{3,2,1,0:T(2,128)}), f32[128,6,2,128]{3,2,1,0:T(2,128)S(1)}, u32[]{:S(2)}, u32[]{:S(2)}) async-start(f32[128,6,2,128]{3,2,1,0:T(2,128)} %bitcast.22), calls=%async_computation.2 | async-start | bytes 1572864 | tf_op jit(solution)/shard_map/all_to_all | solution.py:267
  123.3 0.9 copy-start.12

commit v3 on v2

v3 whole, which is shorter than its diff:
```python
import functools

import jax
import jax.numpy as jnp
from jax import lax
from jax.experimental import pallas as pl
from jax.experimental.pallas import tpu as pltpu
from jax.sharding import PartitionSpec as P

FIRST = (0.8, -0.2, 4.0 / 105.0, -1.0 / 280.0)
SECOND = (-205.0 / 72.0, 1.6, -0.2, 8.0 / 315.0, -1.0 / 560.0)
BETA = 0.05
AXES = ("gx", "gy")
CAP = 6
DEV = 128
COLS = 256
NZ = 256
F32 = jnp.float32
BF16 = jnp.bfloat16
W_ROWS = CAP * 8
A_ROWS = W_ROWS + 1
V_ROWS = CAP * 2
PART = 32


def call(kernel, out_shape, mib, micros, in_specs, **kw):
    run = pl.pallas_call(
        kernel,
        out_shape=out_shape,
        in_specs=in_specs,
        compiler_params=pltpu.CompilerParams(vmem_limit_bytes=mib * 1024 * 1024),
        cost_estimate=pl.CostEstimate(
            flops=int(micros * 1e8), bytes_accessed=int(micros * 2e6), transcendentals=0
        ),
        **kw,
    )

    def placed(*args):
        return run(
            *(
                pltpu.with_memory_space_constraint(x, pltpu.HBM) if spec.memory_space == pltpu.HBM else x
                for spec, x in zip(in_specs, args)
            )
        )

    return placed


def iota(shape, dim):
    return lax.broadcasted_iota(jnp.int32, shape, dim)


def dot(a, b):
    return jnp.dot(a, b, preferred_element_type=F32)


def split3(x):
    hi = x.astype(BF16)
    rest = x - hi.astype(F32)
    mid = rest.astype(BF16)
    low = (rest - mid.astype(F32)).astype(BF16)
    return hi, mid, low


def select(onehot, parts):
    return sum(dot(onehot, part) for part in parts)


def ones(mask):
    return jnp.where(mask, 1.0, 0.0).astype(BF16)


def masks_by_owner(owner_row, first, count):
    match = iota((count, COLS), 0) + first == owner_row
    before = ones(iota((COLS, COLS), 0) < iota((COLS, COLS), 1))
    slot = dot(ones(match), before)
    return [match & (slot == float(s)) for s in range(CAP)]


def masks_by_column(owner_row):
    spread = jnp.broadcast_to(owner_row.astype(F32), (DEV, COLS)).T
    match = iota((COLS, DEV), 1).astype(F32) == spread
    before = ones(iota((COLS, COLS), 1) < iota((COLS, COLS), 0))
    slot = dot(before, ones(match))
    return [match & (slot == float(s)) for s in range(CAP)]


def put_slots(out_ref, start, values, count):
    for s in range(CAP):
        for half in range(2):
            out_ref[pl.ds(start + s * 2 + half, count, stride=V_ROWS), :] = values[
                s * count : (s + 1) * count, half * 128 : half * 128 + 128
            ]


def start_all(pairs, sems, first=0):
    copies = [
        pltpu.make_async_copy(source, target, sems.at[first + i])
        for i, (source, target) in enumerate(pairs)
    ]
    for copy in copies:
        copy.start()
    return copies


def wait_all(copies):
    for copy in copies:
        copy.wait()


def request_kernel(own_hbm, src_hbm, w_hbm, out_hbm, own, src, w, out, sems):
    copies = start_all(((own_hbm, own), (src_hbm, src), (w_hbm.at[1], w)), sems)
    wait_all(copies[:2])
    lane = iota((DEV, 128), 1)
    wanted = jnp.zeros((DEV, 128), F32)
    for j in range(2):
        masks = masks_by_owner(own[j], 0, DEV)
        source_row = src[j].astype(F32)
        for s in range(CAP):
            column = jnp.sum(jnp.where(masks[s], source_row, 0.0), axis=1, keepdims=True)
            wanted = jnp.where(lane == 8 * j + s, column, wanted)
    out[pl.ds(W_ROWS, DEV, stride=A_ROWS), :] = wanted
    copies[2].wait()
    sent = []
    for i, first in enumerate(range(0, DEV, PART)):
        onehot = jnp.concatenate([ones(m[first : first + PART]) for m in masks], axis=0)
        for k in range(4):
            placed = dot(onehot, w[k].reshape(COLS, NZ))
            for s in range(CAP):
                for half in range(2):
                    row = first * A_ROWS + s * 8 + k * 2 + half
                    out[pl.ds(row, PART, stride=A_ROWS), :] = placed[
                        s * PART : (s + 1) * PART, half * 128 : half * 128 + 128
                    ]
        block = pl.ds(first * A_ROWS, PART * A_ROWS)
        sent += start_all(((out.at[block], out_hbm.at[block]),), sems, 3 + i)
    wait_all(sent)


def stencil_kernel(step, lap, st_hbm, ve_hbm, xlo, xhi, ylo, yhi, *refs):
    if lap:
        refs = refs[1:]
    outs, refs = refs[: 2 + lap], refs[2 + lap :]
    xpad, ypad, ve = refs[:3]
    results, sems = refs[3 : 5 + lap], refs[-1]
    sources = [st_hbm.at[step]] + [ve_hbm.at[c] for c in range(3)] * lap
    pairs = [(source, xpad.at[i, pl.ds(4, 16)]) for i, source in enumerate(sources)]
    pairs += [(source, ypad.at[i, :, pl.ds(8, 16)]) for i, source in enumerate(sources)]
    copies = start_all(pairs + [(ve_hbm, ve)] * (not lap), sems)
    for i in range(len(sources)):
        xpad[i, 0:4] = xlo[i]
        xpad[i, 20:24] = xhi[i]
        ypad[i, :, 4:8] = ylo[i]
        ypad[i, :, 24:28] = yhi[i]
    wait_all(copies)
    rows = 4

    def block(x):
        here = pl.ds(x, rows)

        def differences(i, coeffs, sign):
            centre = xpad[i, pl.ds(x + 4, rows)]
            parts = [None, None, None]
            for k in range(4):
                d = k + 1
                terms = (
                    xpad[i, pl.ds(x + 4 + d, rows)] + sign * xpad[i, pl.ds(x + 4 - d, rows)],
                    ypad[i, here, 8 + d : 24 + d, :] + sign * ypad[i, here, 8 - d : 24 - d, :],
                    pltpu.roll(centre, NZ - d, 2) + sign * pltpu.roll(centre, d, 2),
                )
                for c in range(3):
                    term = coeffs[k] * terms[c]
                    parts[c] = term if parts[c] is None else parts[c] + term
            return centre, parts

        slope = differences(0, FIRST, -1.0)[1]
        total = None
        for c in range(3):
            results[0][c, here] = slope[c]
            along = xpad[1 + c, pl.ds(x + 4, rows)] if lap else ve[c, here]
            total = along * slope[c] if total is None else total + along * slope[c]
        results[1][here] = -0.5 * total
        for c in range(3 * lap):
            centre, parts = differences(1 + c, SECOND[1:], 1.0)
            results[2][c, here] = -BETA * (3.0 * SECOND[0] * centre + parts[0] + parts[1] + parts[2])

    sent = []
    for first in (0, 8):
        pl.loop(first, first + 8, step=rows)(block)
        half = pl.ds(first, 8)
        pairs = [(results[0].at[:, half], outs[0].at[:, half]), (results[1].at[half], outs[1].at[half])]
        if lap:
            pairs.append((results[2].at[:, half], outs[2].at[:, half]))
        sent += start_all(pairs, sems, len(sent))
    wait_all(sent)


def supply_kernel(asked, b_hbm, out_hbm, b, out, sems):
    copies = start_all(((b_hbm, b),), sems)
    wanted = asked[pl.ds(W_ROWS, DEV, stride=A_ROWS), :]
    place = iota((PART, COLS), 1).astype(F32)
    onehots = [
        jnp.concatenate(
            [ones(wanted[first : first + PART, s : s + 1] == place) for s in range(CAP)], axis=0
        )
        for first in range(0, DEV, PART)
    ]
    wait_all(copies)
    parts = split3(b[...])
    sent = []
    for i, first in enumerate(range(0, DEV, PART)):
        put_slots(out, first * V_ROWS, select(onehots[i], parts), PART)
        here = pl.ds(first * V_ROWS, PART * V_ROWS)
        sent += start_all(((out.at[here], out_hbm.at[here]),), sems, 1 + i)
    wait_all(sent)


def gathered_rows(wanted_t, first):
    place = iota((COLS, DEV), 0).astype(F32)
    return jnp.concatenate(
        [ones(place == wanted_t[first + s : first + s + 1, :]) for s in range(CAP)], axis=1
    )


def normal_kernel(asked, d_hbm, wt_hbm, w, d, wt, sems):
    wanted_t = asked[pl.ds(W_ROWS, DEV, stride=A_ROWS), :].T
    wt[...] = wanted_t[:16]
    sent = start_all(((wt, wt_hbm),), sems)
    onehot_t = gathered_rows(wanted_t, 8)
    for k in range(4):
        for s in range(CAP):
            for half in range(2):
                w[k, s * DEV : (s + 1) * DEV, half * 128 : half * 128 + 128] = asked[
                    pl.ds(s * 8 + k * 2 + half, DEV, stride=A_ROWS), :
                ]
    for m in range(4):
        total = None
        for k in range(4 - m):
            product = w[k] * w[k + m]
            high = product.astype(BF16)
            low = (product - high.astype(F32)).astype(BF16)
            part = dot(onehot_t, high) + dot(onehot_t, low)
            if k != 1:
                part = pltpu.roll(part, (k - 1) % NZ, 1)
            total = part if total is None else total + part
        d[m] = total
        sent += start_all(((d.at[m], d_hbm.at[m]),), sems, 1 + m)
    wait_all(sent)


def read_slots(ref):
    return jnp.concatenate(
        [
            jnp.concatenate(
                [ref[pl.ds(s * 2 + half, DEV, stride=V_ROWS), :] for half in range(2)], axis=1
            )
            for s in range(CAP)
        ],
        axis=0,
    )


def middle_kernel(arr, own_hbm, w_hbm, b_hbm, d_hbm, lam_hbm, out_hbm, own, w, b, d, lam_scr, out, parts, sems):
    copies = start_all(((own_hbm.at[0], own), (w_hbm.at[0], w), (b_hbm, b), (d_hbm, d)), sems)
    copies[0].wait()
    owner_row = own[...]
    taken = jnp.concatenate([ones(m) for m in masks_by_column(owner_row)], axis=1)
    masks = masks_by_owner(owner_row, 0, DEV)
    mine_all = select(taken, split3(read_slots(arr)))
    wait_all(copies[1:])
    rows = 64
    for start in range(0, COLS, rows):
        here = slice(start, start + rows)
        mine = mine_all[here]
        weights = [
            w[k, start // 16 : (start + rows) // 16].reshape(rows, NZ).astype(F32) for k in range(4)
        ]
        field = b[here]
        for k in range(4):
            field += weights[k] * (mine if k == 1 else pltpu.roll(mine, (1 - k) % NZ, 1))
        lam = d[0, here] * field
        for m in range(1, 4):
            lam += d[m, here] * pltpu.roll(field, NZ - m, 1) + pltpu.roll(d[m, here] * field, m, 1)
        lam_scr[here] = lam
        spread = weights[1] * lam
        for k in (0, 2, 3):
            spread += pltpu.roll(weights[k] * lam, (k - 1) % NZ, 1)
        for i, part in enumerate(split3(spread)):
            parts[i, here] = part
    sent = start_all(((lam_scr, lam_hbm),), sems)
    for i, first in enumerate(range(0, DEV, PART)):
        onehot = jnp.concatenate([ones(m[first : first + PART]) for m in masks], axis=0)
        put_slots(out, first * V_ROWS, select(onehot, [parts[p] for p in range(3)]), PART)
        here = pl.ds(first * V_ROWS, PART * V_ROWS)
        sent += start_all(((out.at[here], out_hbm.at[here]),), sems, 1 + i)
    wait_all(sent)


def final_kernel(arr, wt_hbm, h_hbm, g_hbm, out_hbm, wt, h, g, out, sems):
    copies = start_all(((wt_hbm, wt), (h_hbm, h), (g_hbm, g)), sems)
    copies[0].wait()
    onehot_t = gathered_rows(wt[...], 0)
    lam = select(onehot_t, split3(read_slots(arr)))
    wait_all(copies[1:])
    sent = []
    for c in range(3):
        out[c] = h[c] - 0.5 * (lam * g[c])
        sent += start_all(((out.at[c], out_hbm.at[c]),), sems, c)
    wait_all(sent)


def exchange(value):
    return lax.all_to_all(value, AXES, split_axis=0, concat_axis=0, tiled=True)


def neighbours(first, last, axis):
    count = lax.axis_size(axis)
    up = [(i, (i + 1) % count) for i in range(count)]
    down = [(j, i) for i, j in up]
    return lax.ppermute(last, axis, up), lax.ppermute(first, axis, down)


def per_device(state_path, velocity, weights, owners, sources):
    owner_row = owners.reshape(2, 1, COLS)
    source_row = sources.reshape(2, 1, COLS)
    hbm = pl.BlockSpec(memory_space=pltpu.HBM)
    near = pl.BlockSpec(memory_space=pltpu.VMEM)
    struct = lambda *shape: pltpu.HBM(shape, F32)
    scratch = lambda *shape: pltpu.VMEM(shape, F32)
    sems = lambda count: pltpu.SemaphoreType.DMA((count,))
    per_field = lambda count: struct(count, 16, 16, NZ)

    request = call(
        request_kernel,
        struct(DEV * A_ROWS, 128),
        16,
        3,
        in_specs=[hbm] * 3,
        out_specs=hbm,
        scratch_shapes=[
            pltpu.VMEM((2, 1, COLS), jnp.int32),
            pltpu.VMEM((2, 1, COLS), jnp.int32),
            pltpu.VMEM((4, 16, 16, NZ), BF16),
            scratch(DEV * A_ROWS, 128),
            sems(7),
        ],
    )(owner_row, source_row, weights)
    asked = exchange(request.reshape(DEV, A_ROWS, 1, 128)).reshape(DEV * A_ROWS, 128)

    def halo(fields):
        xlo, xhi = neighbours(fields(slice(0, 4), slice(None)), fields(slice(12, 16), slice(None)), "gx")
        ylo, yhi = neighbours(fields(slice(None), slice(0, 4)), fields(slice(None), slice(12, 16)), "gy")
        return xlo, xhi, ylo, yhi

    slope0, before0 = call(
        functools.partial(stencil_kernel, 0, False),
        (per_field(3), struct(16, 16, NZ)),
        10,
        3,
        in_specs=[hbm] * 2 + [near] * 4,
        out_specs=(hbm, hbm),
        scratch_shapes=[
            scratch(1, 24, 16, NZ),
            scratch(1, 16, 32, NZ),
            scratch(3, 16, 16, NZ),
            scratch(3, 16, 16, NZ),
            scratch(16, 16, NZ),
            sems(4),
        ],
    )(state_path, velocity, *halo(lambda x, y: state_path[:1, x, y]))

    supply = call(
        supply_kernel,
        struct(DEV * V_ROWS, 128),
        8,
        2,
        in_specs=[near, hbm],
        out_specs=hbm,
        scratch_shapes=[scratch(COLS, NZ), scratch(DEV * V_ROWS, 128), sems(5)],
    )(asked, before0.reshape(COLS, NZ))
    arrived = exchange(supply.reshape(DEV, CAP, 2, 128)).reshape(DEV * V_ROWS, 128)

    later = halo(lambda x, y: jnp.concatenate([state_path[1:, x, y], velocity[:, x, y]], axis=0))
    slope1, before1, hess = call(
        functools.partial(stencil_kernel, 1, True),
        (per_field(3), struct(16, 16, NZ), per_field(3)),
        16,
        7,
        in_specs=[hbm] * 2 + [near] * 4 + [hbm],
        out_specs=(hbm, hbm, hbm),
        scratch_shapes=[
            scratch(4, 24, 16, NZ),
            scratch(4, 16, 32, NZ),
            scratch(8, 128),
            scratch(3, 16, 16, NZ),
            scratch(16, 16, NZ),
            scratch(3, 16, 16, NZ),
            sems(8),
        ],
    )(state_path, velocity, *later, supply)

    normal, wanted_t = call(
        normal_kernel,
        (struct(4, COLS, NZ), struct(16, 128)),
        20,
        4,
        in_specs=[near],
        out_specs=(hbm, hbm),
        scratch_shapes=[scratch(4, CAP * DEV, NZ), scratch(4, COLS, NZ), scratch(16, 128), sems(5)],
    )(asked)

    lam, push = call(
        middle_kernel,
        (struct(COLS, NZ), struct(DEV * V_ROWS, 128)),
        14,
        4,
        in_specs=[near] + [hbm] * 4,
        out_specs=(hbm, hbm),
        scratch_shapes=[
            pltpu.VMEM((1, COLS), jnp.int32),
            pltpu.VMEM((4, 16, 16, NZ), BF16),
            scratch(COLS, NZ),
            scratch(4, COLS, NZ),
            scratch(COLS, NZ),
            scratch(DEV * V_ROWS, 128),
            pltpu.VMEM((3, COLS, NZ), BF16),
            sems(5),
        ],
    )(arrived, owner_row, weights, before1.reshape(COLS, NZ), normal)
    returned = exchange(push.reshape(DEV, CAP, 2, 128)).reshape(DEV * V_ROWS, 128)

    hess = hess - 0.5 * (lam.reshape(1, 16, 16, NZ) * slope1)
    out = call(
        final_kernel,
        struct(3, COLS, NZ),
        14,
        2,
        in_specs=[near] + [hbm] * 3,
        out_specs=hbm,
        scratch_shapes=[
            scratch(16, 128),
            scratch(3, COLS, NZ),
            scratch(3, COLS, NZ),
            scratch(3, COLS, NZ),
            sems(3),
        ],
    )(returned, wanted_t, hess.reshape(3, COLS, NZ), slope0.reshape(3, COLS, NZ))
    return out.reshape(3, 16, 16, NZ)


def solution(mesh):
    return jax.shard_map(
        per_device,
        mesh=mesh,
        in_specs=(
            P(None, "gx", "gy", None),
            P(None, "gx", "gy", None),
            P(None, None, "gx", "gy", None),
            P(None, "gx", "gy", None, None),
            P(None, "gx", "gy", None),
        ),
        out_specs=P(None, "gx", "gy", None),
        check_vma=False,
    )
```

time: 128 us -> 124 us (0.969)
  starting transfers between devices: 28.9 us -> 39 us
  local copies, waits for them, and re-layouts: 12.1 us -> 4.96 us
  waiting for transfers between devices: 55.3 us -> 48.8 us
  other arithmetic: 1.25 us -> 4.46 us
  Pallas kernels: 29.1 us -> 25.9 us
    all_to_all x3, waiting for transfers between devices: 54.4 us -> 14.5 us  [exchange(): return lax.all_to_all(value, AXES, split_axis=0, concat_axis=0, tiled=True)]
    ppermute x4 -> x8, waiting for transfers between devices: 0.97 us -> 34.3 us  [neighbours(): return (lax.ppermute(last, axis, up), lax.ppermute(first, axis, down))]
    unnamed x28 -> x4, local copies, waits for them, and re-layouts: 8.76 us -> 0.01 us
    ppermute x4 -> x8, starting transfers between devices: 8.14 us -> 14.3 us  [neighbours(): return (lax.ppermute(last, axis, up), lax.ppermute(first, axis, down))]
    all_to_all x3, starting transfers between devices: 20.7 us -> 24.6 us  [exchange(): return lax.all_to_all(value, AXES, split_axis=0, concat_axis=0, tiled=True)]
    pallas_call x6 -> x7, Pallas kernels: 29.1 us -> 25.9 us  [placed(): run(*(pltpu.with_memory_space_constraint(x, pltpu.HBM) if spec.memory_spa...]
    concatenate x4, other arithmetic: 0.2 us -> 2.43 us  [per_device(): jnp.concatenate([state_path[1:, x, y], velocity[:, x, y]], axis=0)]
    slice x5 -> x4, local copies, waits for them, and re-layouts: 3.39 us -> 4.95 us  [the longest x2 2.71 us: per_device(): state_path[1:, x, y]]
  transfers between devices with their start and end apart: 7 -> 11, of which waited for: 4 -> 4; matrix products, arithmetic and copies ran while one was open for 2% -> 8% of each run, Pallas kernels for 14% -> 12%
where the time goes in v3:
time: 124 us; the launch traced here: 123 us
  waiting for transfers between devices  48.8 us (39%)
  starting transfers between devices  39 us (31%)
  Pallas kernels  25.9 us (21%)
  local copies, waits for them, and re-layouts  4.96 us (4%)
  other arithmetic  4.46 us (4%)
    ppermute x8, waiting for transfers between devices, neighbours(): return (lax.ppermute(last, axis, up), lax.ppermute(first, axis, down))  34.3 us
    pallas_call x7, Pallas kernels, placed(): run(*(pltpu.with_memory_space_constraint(x, pltpu.HBM) if spec.memory_spa...  25.9 us
    all_to_all x3, starting transfers between devices, exchange(): return lax.all_to_all(value, AXES, split_axis=0, concat_axis=0, tiled=True)  24.6 us
    all_to_all x3, waiting for transfers between devices, exchange(): return lax.all_to_all(value, AXES, split_axis=0, concat_axis=0, tiled=True)  14.5 us
    ppermute x8, starting transfers between devices, neighbours(): return (lax.ppermute(last, axis, up), lax.ppermute(first, axis, down))  14.3 us
    slice x2, local copies, waits for them, and re-layouts, per_device(): state_path[1:, x, y]  2.71 us
  transfers between devices with their start and end apart: 11, of which 4 were waited for; matrix products, arithmetic and copies ran while one was open for 8% of the time, Pallas kernels for 12%

profile of v3, /device:TPU:1, one launch (start us, length us, event | category | flops | bytes accessed | tf_op | source)
XLA Modules:
  0.0 123.3 jit_solution(13600115315608352631)
XLA Ops:
  0.0 3.2 %shard_map.55 = f32[6272,128]{1,0:T(8,128)} custom-call(s32[2,1,256]{2,1,0:T(1,128)} %bitcast.25, s32[2,1,256]{2,1,0:T(1,128)} %bitcast.27, bf16[2,4,16,16,256]{4,3,2,1,0:T(8,128)(2,1)} %w_hbm.3), custom_call_target="tpu_custom_call" | custom-call | flops 300000000 | bytes 6000000 | tf_op jit(solution)/shard_map/pallas_call | solution.py:39
  3.2 11.5 %all-to-all-start = ((f32[128,49,1,128]{3,2,1,0:T(1,128)}), f32[128,49,1,128]{3,2,1,0:T(1,128)S(1)}, u32[]{:S(2)}, u32[]{:S(2)}) async-start(f32[128,49,1,128]{3,2,1,0:T(1,128)} %bitcast.17), calls=%async_computation | async-start | bytes 6422528 | tf_op jit(solution)/shard_map/all_to_all | solution.py:313
  14.7 1.0 fusion.3
  15.7 1.8 %collective-permute-start = (f32[1,4,16,256]{3,2,1,0:T(8,128)S(1)}, f32[1,4,16,256]{3,2,1,0:T(8,128)S(1)}, u32[]{:S(2)}, u32[]{:S(2)}) collective-permute-start(f32[1,4,16,256]{3,2,1,0:T(8,128)S(1)} %get-tuple-element.34), channel_id=1, source_target_pairs={{0,16},{16,32},{32,48},{48,64},{64,80},{80,96},{96,112},{112,0},{1... | collective-permute-start | bytes 196616 | tf_op jit(solution)/shard_map/ppermute | solution.py:320
  17.4 1.8 %fusion.2 = (f32[1,16,4,256]{3,2,1,0:T(4,128)S(1)}, f32[1,16,4,256]{3,2,1,0:T(4,128)}, f32[1,16,4,256]{3,2,1,0:T(4,128)S(1)}, f32[1,16,4,256]{3,2,1,0:T(4,128)S(1)}) fusion(f32[2,16,16,256]{3,2,1,0:T(8,128)} %st_hbm.3), kind=kLoop, calls=%fused_computation.7 | loop fusion | bytes 524288 | tf_op jit(solution)/shard_map/slice | solution.py:383
  19.2 1.2 collective-permute-start.2
  20.4 3.6 %collective-permute-start.3 = (f32[1,16,4,256]{3,2,1,0:T(4,128)S(1)}, f32[1,16,4,256]{3,2,1,0:T(4,128)S(1)}, u32[]{:S(2)}, u32[]{:S(2)}) collective-permute-start(f32[1,16,4,256]{3,2,1,0:T(4,128)S(1)} %get-tuple-element.29), channel_id=1, source_target_pairs={{1,0},{2,1},{3,2},{4,3},{5,4},{6,5},{7,6},{8,7},{9,8},{10,9},{11,1... | collective-permute-start | bytes 196616 | tf_op jit(solution)/shard_map/ppermute | solution.py:320
  24.0 1.0 fusion.1
  25.0 0.7 pad_maximum_fusion
  25.8 2.3 %collective-permute-start.4 = (f32[4,4,16,256]{3,2,1,0:T(8,128)}, f32[4,4,16,256]{3,2,1,0:T(8,128)S(1)}, u32[]{:S(2)}, u32[]{:S(2)}) collective-permute-start(f32[4,4,16,256]{3,2,1,0:T(8,128)} %pad_maximum_fusion), channel_id=1, source_target_pairs={{0,16},{16,32},{32,48},{48,64},{64,80},{80,96},{96,112},{112,0},{1... | collective-permute-start | bytes 786440 | tf_op jit(solution)/shard_map/ppermute | solution.py:320
  28.1 0.7 pad_maximum_fusion.1
  28.8 0.5 collective-permute-start.5
  29.3 6.5 %collective-permute-done.1.xhi = f32[1,4,16,256]{3,2,1,0:T(8,128)S(1)} collective-permute-done((f32[1,4,16,256]{3,2,1,0:T(8,128)S(1)}, f32[1,4,16,256]{3,2,1,0:T(8,128)S(1)}, u32[]{:S(2)}, u32[]{:S(2)}) %collective-permute-start.1) | collective-permute-done | bytes 65568 | tf_op jit(solution)/shard_map/ppermute | solution.py:320
  35.8 19.6 %collective-permute-done.2.ylo = f32[1,16,4,256]{3,2,1,0:T(4,128)S(1)} collective-permute-done((f32[1,16,4,256]{3,2,1,0:T(4,128)S(1)}, f32[1,16,4,256]{3,2,1,0:T(4,128)S(1)}, u32[]{:S(2)}, u32[]{:S(2)}) %collective-permute-start.2) | collective-permute-done | bytes 65568 | tf_op jit(solution)/shard_map/ppermute | solution.py:320
  55.4 3.4 %shard_map.56 = (f32[3,16,16,256]{3,2,1,0:T(8,128)}, f32[16,16,256]{2,1,0:T(8,128)}) custom-call(f32[2,16,16,256]{3,2,1,0:T(8,128)} %st_hbm.3, f32[3,16,16,256]{3,2,1,0:T(8,128)} %ve_hbm.3, f32[1,4,16,256]{3,2,1,0:T(8,128)S(1)} %collective-permute-done.xlo, f32[1,4,16,256]{3,2,1,0:T(8,128)S(1)} %collective-permute-done.1.xhi, ...), custom_call_target="tpu_custom_call" | custom-call | flops 300000000 | bytes 6000000 | tf_op jit(solution)/shard_map/pallas_call | solution.py:39
  58.8 0.0 all-to-all-done
  58.8 2.2 %shard_map.57.refs_0_ = f32[1536,128]{1,0:T(8,128)} custom-call(f32[6272,128]{1,0:T(8,128)S(1)} %bitcast.14, f32[256,256]{1,0:T(8,128)} %bitcast.23), custom_call_target="tpu_custom_call" | custom-call | flops 200000000 | bytes 4000000 | tf_op jit(solution)/shard_map/pallas_call | solution.py:39
  61.1 6.8 %all-to-all-start.1 = ((f32[128,6,2,128]{3,2,1,0:T(2,128)}), f32[128,6,2,128]{3,2,1,0:T(2,128)}, u32[]{:S(2)}, u32[]{:S(2)}) async-start(f32[128,6,2,128]{3,2,1,0:T(2,128)} %bitcast.18), calls=%async_computation.1 | async-start | bytes 1572864 | tf_op jit(solution)/shard_map/all_to_all | solution.py:313
  67.8 1.2 fusion
  69.0 0.9 pad_maximum_fusion.2
  69.9 1.5 %collective-permute-start.6 = (f32[4,16,4,256]{3,2,1,0:T(4,128)S(1)}, f32[4,16,4,256]{3,2,1,0:T(4,128)S(1)}, u32[]{:S(2)}, u32[]{:S(2)}) collective-permute-start(f32[4,16,4,256]{3,2,1,0:T(4,128)S(1)} %pad_maximum_fusion.2), channel_id=1, source_target_pairs={{0,1},{1,2},{2,3},{3,4},{4,5},{5,6},{6,7},{7,8},{8,9},{9,10},{10,1... | collective-permute-start | bytes 786440 | tf_op jit(solution)/shard_map/ppermute | solution.py:320
  71.4 0.1 pad_maximum_fusion.3
  71.5 3.5 %collective-permute-start.7 = (f32[4,16,4,256]{3,2,1,0:T(4,128)S(1)}, f32[4,16,4,256]{3,2,1,0:T(4,128)S(1)}, u32[]{:S(2)}, u32[]{:S(2)}) collective-permute-start(f32[4,16,4,256]{3,2,1,0:T(4,128)S(1)} %pad_maximum_fusion.3), channel_id=1, source_target_pairs={{1,0},{2,1},{3,2},{4,3},{5,4},{6,5},{7,6},{8,7},{9,8},{10,9},{11,1... | collective-permute-start | bytes 786440 | tf_op jit(solution)/shard_map/ppermute | solution.py:320
  75.0 3.3 %shard_map.59 = (f32[4,256,256]{2,1,0:T(8,128)}, f32[16,128]{1,0:T(8,128)}) custom-call(f32[6272,128]{1,0:T(8,128)S(1)} %bitcast.15), custom_call_target="tpu_custom_call" | custom-call | flops 400000000 | bytes 8000000 | tf_op jit(solution)/shard_map/pallas_call | solution.py:39
  78.2 0.0 collective-permute-done.4.xlo
  78.3 8.2 %collective-permute-done.6.ylo = f32[4,16,4,256]{3,2,1,0:T(4,128)S(1)} collective-permute-done((f32[4,16,4,256]{3,2,1,0:T(4,128)S(1)}, f32[4,16,4,256]{3,2,1,0:T(4,128)S(1)}, u32[]{:S(2)}, u32[]{:S(2)}) %collective-permute-start.6) | collective-permute-done | bytes 262176 | tf_op jit(solution)/shard_map/ppermute | solution.py:320
  86.4 6.3 %shard_map.58 = (f32[3,16,16,256]{3,2,1,0:T(8,128)}, f32[16,16,256]{2,1,0:T(8,128)}, f32[3,16,16,256]{3,2,1,0:T(8,128)}) custom-call(f32[2,16,16,256]{3,2,1,0:T(8,128)} %st_hbm.3, f32[3,16,16,256]{3,2,1,0:T(8,128)} %ve_hbm.3, f32[4,4,16,256]{3,2,1,0:T(8,128)S(1)} %collective-permute-done.4.xlo, f32[4,4,16,256]{3,2,1,0:T(8,128)} %collective-permute-done.5.xhi, ...), custom_call_target="tpu_custom_call" | custom-call | flops 700000000 | bytes 14000000 | tf_op jit(solution)/shard_map/pallas_call | solution.py:39
  92.8 5.2 %shard_map.60 = (f32[256,256]{1,0:T(8,128)}, f32[1536,128]{1,0:T(8,128)}) custom-call(f32[1536,128]{1,0:T(8,128)} %bitcast.6.arr, s32[2,1,256]{2,1,0:T(1,128)} %bitcast.26, bf16[2,4,16,16,256]{4,3,2,1,0:T(8,128)(2,1)} %w_hbm.3, f32[256,256]{1,0:T(8,128)} %bitcast.24, f32[4,256,256]{2,1,0:T(8,128)} %get-tuple-element.16.d_hbm), custom_call_target="tpu_custom_call" | custom-call | flops 400000000 | bytes 8000000 | tf_op jit(solution)/shard_map/pallas_call | solution.py:39
  98.0 6.3 %all-to-all-start.2 = ((f32[128,6,2,128]{3,2,1,0:T(2,128)}), f32[128,6,2,128]{3,2,1,0:T(2,128)S(1)}, u32[]{:S(2)}, u32[]{:S(2)}) async-start(f32[128,6,2,128]{3,2,1,0:T(2,128)} %bitcast.20), calls=%async_computation.2 | async-start | bytes 1572864 | tf_op jit(solution)/shard_map/all_to_all | solution.py:313
  104.4 2.0 %multiply_subtract_fusion = f32[3,16,16,256]{3,2,1,0:T(8,128)} fusion(f32[3,16,16,256]{3,2,1,0:T(8,128)S(1)} %copy-done.1, f32[3,16,16,256]{3,2,1,0:T(8,128)S(1)} %copy-done, f32[16,16,256]{2,1,0:T(8,128)} %bitcast.22), kind=kLoop, calls=%fused_computation | loop fusion | flops 589824 | bytes 2621440 | tf_op jit(solution)/shard_map/sub | solution.py:432
  106.4 14.5 %all-to-all-done.2 = f32[128,6,2,128]{3,2,1,0:T(2,128)S(1)} async-done(((f32[128,6,2,128]{3,2,1,0:T(2,128)}), f32[128,6,2,128]{3,2,1,0:T(2,128)S(1)}, u32[]{:S(2)}, u32[]{:S(2)}) %all-to-all-start.2) | async-done | bytes 786464 | tf_op jit(solution)/shard_map/all_to_all | solution.py:313
  120.9 2.3 %shard_map.61 = f32[3,256,256]{2,1,0:T(8,128)} custom-call(f32[1536,128]{1,0:T(8,128)S(1)} %bitcast.16, f32[16,128]{1,0:T(8,128)} %get-tuple-element.18.wt_hbm, f32[3,256,256]{2,1,0:T(8,128)} %bitcast.19, f32[3,256,256]{2,1,0:T(8,128)} %bitcast.21), custom_call_target="tpu_custom_call" | custom-call | flops 200000000 | bytes 4000000 | tf_op jit(solution)/shard_map/pallas_call | solution.py:39
  (10 shorter events, 0.0 us)
Async XLA Ops:
  3.2 55.6 %all-to-all-start = ((f32[128,49,1,128]{3,2,1,0:T(1,128)}), f32[128,49,1,128]{3,2,1,0:T(1,128)S(1)}, u32[]{:S(2)}, u32[]{:S(2)}) async-start(f32[128,49,1,128]{3,2,1,0:T(1,128)} %bitcast.17), calls=%async_computation | async-start | bytes 6422528 | tf_op jit(solution)/shard_map/all_to_all | solution.py:313
  15.7 13.1 %collective-permute-start = (f32[1,4,16,256]{3,2,1,0:T(8,128)S(1)}, f32[1,4,16,256]{3,2,1,0:T(8,128)S(1)}, u32[]{:S(2)}, u32[]{:S(2)}) collective-permute-start(f32[1,4,16,256]{3,2,1,0:T(8,128)S(1)} %get-tuple-element.34), channel_id=1, source_target_pairs={{0,16},{16,32},{32,48},{48,64},{64,80},{80,96},{96,112},{112,0},{1... | collective-permute-start | bytes 196616 | tf_op jit(solution)/shard_map/ppermute | solution.py:320
  17.4 18.4 %collective-permute-start.1 = (f32[1,4,16,256]{3,2,1,0:T(8,128)S(1)}, f32[1,4,16,256]{3,2,1,0:T(8,128)S(1)}, u32[]{:S(2)}, u32[]{:S(2)}) collective-permute-start(f32[1,4,16,256]{3,2,1,0:T(8,128)S(1)} %get-tuple-element.33), channel_id=1, source_target_pairs={{16,0},{32,16},{48,32},{64,48},{80,64},{96,80},{112,96},{0,112},{1... | collective-permute-start | bytes 196616 | tf_op jit(solution)/shard_map/ppermute | solution.py:320
  19.2 36.2 %collective-permute-start.2 = (f32[1,16,4,256]{3,2,1,0:T(4,128)S(1)}, f32[1,16,4,256]{3,2,1,0:T(4,128)S(1)}, u32[]{:S(2)}, u32[]{:S(2)}) collective-permute-start(f32[1,16,4,256]{3,2,1,0:T(4,128)S(1)} %get-tuple-element.30), channel_id=1, source_target_pairs={{0,1},{1,2},{2,3},{3,4},{4,5},{5,6},{6,7},{7,8},{8,9},{9,10},{10,1... | collective-permute-start | bytes 196616 | tf_op jit(solution)/shard_map/ppermute | solution.py:320
  20.4 35.0 %collective-permute-start.3 = (f32[1,16,4,256]{3,2,1,0:T(4,128)S(1)}, f32[1,16,4,256]{3,2,1,0:T(4,128)S(1)}, u32[]{:S(2)}, u32[]{:S(2)}) collective-permute-start(f32[1,16,4,256]{3,2,1,0:T(4,128)S(1)} %get-tuple-element.29), channel_id=1, source_target_pairs={{1,0},{2,1},{3,2},{4,3},{5,4},{6,5},{7,6},{8,7},{9,8},{10,9},{11,1... | collective-permute-start | bytes 196616 | tf_op jit(solution)/shard_map/ppermute | solution.py:320
  25.8 52.5 %collective-permute-start.4 = (f32[4,4,16,256]{3,2,1,0:T(8,128)}, f32[4,4,16,256]{3,2,1,0:T(8,128)S(1)}, u32[]{:S(2)}, u32[]{:S(2)}) collective-permute-start(f32[4,4,16,256]{3,2,1,0:T(8,128)} %pad_maximum_fusion), channel_id=1, source_target_pairs={{0,16},{16,32},{32,48},{48,64},{64,80},{80,96},{96,112},{112,0},{1... | collective-permute-start | bytes 786440 | tf_op jit(solution)/shard_map/ppermute | solution.py:320
  28.8 49.5 %collective-permute-start.5 = (f32[4,4,16,256]{3,2,1,0:T(8,128)}, f32[4,4,16,256]{3,2,1,0:T(8,128)}, u32[]{:S(2)}, u32[]{:S(2)}) collective-permute-start(f32[4,4,16,256]{3,2,1,0:T(8,128)} %pad_maximum_fusion.1), channel_id=1, source_target_pairs={{16,0},{32,16},{48,32},{64,48},{80,64},{96,80},{112,96},{0,112},{1... | collective-permute-start | bytes 786440 | tf_op jit(solution)/shard_map/ppermute | solution.py:320
  61.1 31.7 %all-to-all-start.1 = ((f32[128,6,2,128]{3,2,1,0:T(2,128)}), f32[128,6,2,128]{3,2,1,0:T(2,128)}, u32[]{:S(2)}, u32[]{:S(2)}) async-start(f32[128,6,2,128]{3,2,1,0:T(2,128)} %bitcast.18), calls=%async_computation.1 | async-start | bytes 1572864 | tf_op jit(solution)/shard_map/all_to_all | solution.py:313
  69.9 16.5 %collective-permute-start.6 = (f32[4,16,4,256]{3,2,1,0:T(4,128)S(1)}, f32[4,16,4,256]{3,2,1,0:T(4,128)S(1)}, u32[]{:S(2)}, u32[]{:S(2)}) collective-permute-start(f32[4,16,4,256]{3,2,1,0:T(4,128)S(1)} %pad_maximum_fusion.2), channel_id=1, source_target_pairs={{0,1},{1,2},{2,3},{3,4},{4,5},{5,6},{6,7},{7,8},{8,9},{9,10},{10,1... | collective-permute-start | bytes 786440 | tf_op jit(solution)/shard_map/ppermute | solution.py:320
  71.5 15.0 %collective-permute-start.7 = (f32[4,16,4,256]{3,2,1,0:T(4,128)S(1)}, f32[4,16,4,256]{3,2,1,0:T(4,128)S(1)}, u32[]{:S(2)}, u32[]{:S(2)}) collective-permute-start(f32[4,16,4,256]{3,2,1,0:T(4,128)S(1)} %pad_maximum_fusion.3), channel_id=1, source_target_pairs={{1,0},{2,1},{3,2},{4,3},{5,4},{6,5},{7,6},{8,7},{9,8},{10,9},{11,1... | collective-permute-start | bytes 786440 | tf_op jit(solution)/shard_map/ppermute | solution.py:320
  92.8 11.6 %copy-start = (f32[3,16,16,256]{3,2,1,0:T(8,128)S(1)}, f32[3,16,16,256]{3,2,1,0:T(8,128)}, u32[]{:S(2)}) copy-start(f32[3,16,16,256]{3,2,1,0:T(8,128)} %get-tuple-element.21) | copy-start | bytes 2359300
  92.8 11.6 %copy-start.1 = (f32[3,16,16,256]{3,2,1,0:T(8,128)S(1)}, f32[3,16,16,256]{3,2,1,0:T(8,128)}, u32[]{:S(2)}) copy-start(f32[3,16,16,256]{3,2,1,0:T(8,128)} %get-tuple-element.19) | copy-start | bytes 2359300
  98.0 22.9 %all-to-all-start.2 = ((f32[128,6,2,128]{3,2,1,0:T(2,128)}), f32[128,6,2,128]{3,2,1,0:T(2,128)S(1)}, u32[]{:S(2)}, u32[]{:S(2)}) async-start(f32[128,6,2,128]{3,2,1,0:T(2,128)} %bitcast.20), calls=%async_computation.2 | async-start | bytes 1572864 | tf_op jit(solution)/shard_map/all_to_all | solution.py:313

commit v4 on v3

--- a/solution.py
+++ b/solution.py
@@ -54,12 +54,9 @@
     return jnp.dot(a, b, preferred_element_type=F32)
 
 
-def split3(x):
+def split(x):
     hi = x.astype(BF16)
-    rest = x - hi.astype(F32)
-    mid = rest.astype(BF16)
-    low = (rest - mid.astype(F32)).astype(BF16)
-    return hi, mid, low
+    return hi, (x - hi.astype(F32)).astype(BF16)
 
 
 def select(onehot, parts):
@@ -137,65 +134,80 @@
     wait_all(sent)
 
 
-def stencil_kernel(step, lap, st_hbm, ve_hbm, xlo, xhi, ylo, yhi, *refs):
-    if lap:
-        refs = refs[1:]
-    outs, refs = refs[: 2 + lap], refs[2 + lap :]
-    xpad, ypad, ve = refs[:3]
-    results, sems = refs[3 : 5 + lap], refs[-1]
-    sources = [st_hbm.at[step]] + [ve_hbm.at[c] for c in range(3)] * lap
-    pairs = [(source, xpad.at[i, pl.ds(4, 16)]) for i, source in enumerate(sources)]
-    pairs += [(source, ypad.at[i, :, pl.ds(8, 16)]) for i, source in enumerate(sources)]
-    copies = start_all(pairs + [(ve_hbm, ve)] * (not lap), sems)
+def fill(sources, halos, xpad, ypad, sems, extra=()):
+    xlo, xhi, ylo, yhi = halos
+    pairs = list(extra)
+    for i, source in enumerate(sources):
+        pairs += [(source, xpad.at[i, pl.ds(4, 16)]), (source, ypad.at[i, :, pl.ds(8, 16)])]
+    copies = start_all(pairs, sems)
     for i in range(len(sources)):
         xpad[i, 0:4] = xlo[i]
         xpad[i, 20:24] = xhi[i]
         ypad[i, :, 4:8] = ylo[i]
         ypad[i, :, 24:28] = yhi[i]
-    wait_all(copies)
-    rows = 4
+    return copies
+
+
+def differences(xpad, ypad, i, x, rows, coeffs, sign):
+    centre = xpad[i, pl.ds(x + 4, rows)]
+    parts = [None, None, None]
+    for k in range(4):
+        d = k + 1
+        terms = (
+            xpad[i, pl.ds(x + 4 + d, rows)] + sign * xpad[i, pl.ds(x + 4 - d, rows)],
+            ypad[i, pl.ds(x, rows), 8 + d : 24 + d, :] + sign * ypad[i, pl.ds(x, rows), 8 - d : 24 - d, :],
+            pltpu.roll(centre, NZ - d, 2) + sign * pltpu.roll(centre, d, 2),
+        )
+        for c in range(3):
+            term = coeffs[k] * terms[c]
+            parts[c] = term if parts[c] is None else parts[c] + term
+    return centre, parts
+
+
+ROWS = 4
+
+
+def slope_kernel(step, st_hbm, ve_hbm, *refs):
+    g_hbm, b_hbm, xpad, ypad, ve, g, b, sems = refs[-8:]
+    wait_all(fill([st_hbm.at[step]], refs[:4], xpad, ypad, sems, [(ve_hbm, ve)]))
 
     def block(x):
-        here = pl.ds(x, rows)
-
-        def differences(i, coeffs, sign):
-            centre = xpad[i, pl.ds(x + 4, rows)]
-            parts = [None, None, None]
-            for k in range(4):
-                d = k + 1
-                terms = (
-                    xpad[i, pl.ds(x + 4 + d, rows)] + sign * xpad[i, pl.ds(x + 4 - d, rows)],
-                    ypad[i, here, 8 + d : 24 + d, :] + sign * ypad[i, here, 8 - d : 24 - d, :],
-                    pltpu.roll(centre, NZ - d, 2) + sign * pltpu.roll(centre, d, 2),
-                )
-                for c in range(3):
-                    term = coeffs[k] * terms[c]
-                    parts[c] = term if parts[c] is None else parts[c] + term
-            return centre, parts
-
-        slope = differences(0, FIRST, -1.0)[1]
+        here = pl.ds(x, ROWS)
+        slope = differences(xpad, ypad, 0, x, ROWS, FIRST, -1.0)[1]
         total = None
         for c in range(3):
-            results[0][c, here] = slope[c]
-            along = xpad[1 + c, pl.ds(x + 4, rows)] if lap else ve[c, here]
-            total = along * slope[c] if total is None else total + along * slope[c]
-        results[1][here] = -0.5 * total
-        for c in range(3 * lap):
-            centre, parts = differences(1 + c, SECOND[1:], 1.0)
-            results[2][c, here] = -BETA * (3.0 * SECOND[0] * centre + parts[0] + parts[1] + parts[2])
+            g[c, here] = slope[c]
+            term = ve[c, here] * slope[c]
+            total = term if total is None else total + term
+        b[here] = -0.5 * total
 
     sent = []
     for first in (0, 8):
-        pl.loop(first, first + 8, step=rows)(block)
+        pl.loop(first, first + 8, step=ROWS)(block)
         half = pl.ds(first, 8)
-        pairs = [(results[0].at[:, half], outs[0].at[:, half]), (results[1].at[half], outs[1].at[half])]
-        if lap:
-            pairs.append((results[2].at[:, half], outs[2].at[:, half]))
+        pairs = ((b.at[half], b_hbm.at[half]), (g.at[:, half], g_hbm.at[:, half]))
         sent += start_all(pairs, sems, len(sent))
     wait_all(sent)
 
 
-def supply_kernel(asked, b_hbm, out_hbm, b, out, sems):
+def curve_kernel(ve_hbm, xlo, xhi, ylo, yhi, lam_hbm, g_hbm, h_hbm, xpad, ypad, lam, g, h, sems):
+    sources = [ve_hbm.at[c] for c in range(3)]
+    extra = [(lam_hbm, lam), (g_hbm, g)]
+    wait_all(fill(sources, (xlo, xhi, ylo, yhi), xpad, ypad, sems, extra))
+
+    def block(x):
+        here = pl.ds(x, ROWS)
+        for c in range(3):
+            centre, parts = differences(xpad, ypad, c, x, ROWS, SECOND[1:], 1.0)
+            total = 3.0 * SECOND[0] * centre + parts[0] + parts[1] + parts[2]
+            h[c, here] = -BETA * total - 0.5 * (lam[here] * g[c, here])
+
+    pl.loop(0, 16, step=ROWS)(block)
+    wait_all(start_all(((h, h_hbm),), sems))
+
+
+def supply_kernel(asked, b_hbm, *refs):
+    out_hbm, b, out, sems = refs[-4:]
     copies = start_all(((b_hbm, b),), sems)
     wanted = asked[pl.ds(W_ROWS, DEV, stride=A_ROWS), :]
     place = iota((PART, COLS), 1).astype(F32)
@@ -206,7 +218,7 @@
         for first in range(0, DEV, PART)
     ]
     wait_all(copies)
-    parts = split3(b[...])
+    parts = split(b[...])
     sent = []
     for i, first in enumerate(range(0, DEV, PART)):
         put_slots(out, first * V_ROWS, select(onehots[i], parts), PART)
@@ -260,13 +272,14 @@
     )
 
 
-def middle_kernel(arr, own_hbm, w_hbm, b_hbm, d_hbm, lam_hbm, out_hbm, own, w, b, d, lam_scr, out, parts, sems):
+def middle_kernel(arr, own_hbm, w_hbm, b_hbm, d_hbm, *refs):
+    lam_hbm, out_hbm, own, w, b, d, lam_scr, out, parts, sems = refs[-10:]
     copies = start_all(((own_hbm.at[0], own), (w_hbm.at[0], w), (b_hbm, b), (d_hbm, d)), sems)
     copies[0].wait()
     owner_row = own[...]
     taken = jnp.concatenate([ones(m) for m in masks_by_column(owner_row)], axis=1)
     masks = masks_by_owner(owner_row, 0, DEV)
-    mine_all = select(taken, split3(read_slots(arr)))
+    mine_all = select(taken, split(read_slots(arr)))
     wait_all(copies[1:])
     rows = 64
     for start in range(0, COLS, rows):
@@ -285,12 +298,12 @@
         spread = weights[1] * lam
         for k in (0, 2, 3):
             spread += pltpu.roll(weights[k] * lam, (k - 1) % NZ, 1)
-        for i, part in enumerate(split3(spread)):
+        for i, part in enumerate(split(spread)):
             parts[i, here] = part
     sent = start_all(((lam_scr, lam_hbm),), sems)
     for i, first in enumerate(range(0, DEV, PART)):
         onehot = jnp.concatenate([ones(m[first : first + PART]) for m in masks], axis=0)
-        put_slots(out, first * V_ROWS, select(onehot, [parts[p] for p in range(3)]), PART)
+        put_slots(out, first * V_ROWS, select(onehot, [parts[p] for p in range(2)]), PART)
         here = pl.ds(first * V_ROWS, PART * V_ROWS)
         sent += start_all(((out.at[here], out_hbm.at[here]),), sems, 1 + i)
     wait_all(sent)
@@ -300,7 +313,7 @@
     copies = start_all(((wt_hbm, wt), (h_hbm, h), (g_hbm, g)), sems)
     copies[0].wait()
     onehot_t = gathered_rows(wt[...], 0)
-    lam = select(onehot_t, split3(read_slots(arr)))
+    lam = select(onehot_t, split(read_slots(arr)))
     wait_all(copies[1:])
     sent = []
     for c in range(3):
@@ -352,52 +365,42 @@
         ylo, yhi = neighbours(fields(slice(None), slice(0, 4)), fields(slice(None), slice(12, 16)), "gy")
         return xlo, xhi, ylo, yhi
 
-    slope0, before0 = call(
-        functools.partial(stencil_kernel, 0, False),
-        (per_field(3), struct(16, 16, NZ)),
-        10,
-        3,
-        in_specs=[hbm] * 2 + [near] * 4,
-        out_specs=(hbm, hbm),
-        scratch_shapes=[
-            scratch(1, 24, 16, NZ),
-            scratch(1, 16, 32, NZ),
-            scratch(3, 16, 16, NZ),
-            scratch(3, 16, 16, NZ),
-            scratch(16, 16, NZ),
-            sems(4),
-        ],
-    )(state_path, velocity, *halo(lambda x, y: state_path[:1, x, y]))
+    tie = pl.BlockSpec(memory_space=pl.ANY)
+
+    def slopes(step, faces, *after):
+        return call(
+            functools.partial(slope_kernel, step),
+            (per_field(3), struct(16, 16, NZ)),
+            10,
+            3,
+            in_specs=[hbm] * 2 + [near] * 4 + [hbm] * len(after),
+            out_specs=(hbm, hbm),
+            scratch_shapes=[
+                scratch(1, 24, 16, NZ),
+                scratch(1, 16, 32, NZ),
+                scratch(3, 16, 16, NZ),
+                scratch(3, 16, 16, NZ),
+                scratch(16, 16, NZ),
+                sems(4),
+            ],
+        )(state_path, velocity, *faces, *after)
+
+    slope0, before0 = slopes(0, halo(lambda x, y: state_path[:1, x, y]))
+    faces1 = halo(lambda x, y: state_path[1:, x, y])
 
     supply = call(
         supply_kernel,
         struct(DEV * V_ROWS, 128),
         8,
         2,
-        in_specs=[near, hbm],
+        in_specs=[near, hbm] + [tie] * 4,
         out_specs=hbm,
         scratch_shapes=[scratch(COLS, NZ), scratch(DEV * V_ROWS, 128), sems(5)],
-    )(asked, before0.reshape(COLS, NZ))
+    )(asked, before0.reshape(COLS, NZ), *faces1)
     arrived = exchange(supply.reshape(DEV, CAP, 2, 128)).reshape(DEV * V_ROWS, 128)
 
-    later = halo(lambda x, y: jnp.concatenate([state_path[1:, x, y], velocity[:, x, y]], axis=0))
-    slope1, before1, hess = call(
-        functools.partial(stencil_kernel, 1, True),
-        (per_field(3), struct(16, 16, NZ), per_field(3)),
-        16,
-        7,
-        in_specs=[hbm] * 2 + [near] * 4 + [hbm],
-        out_specs=(hbm, hbm, hbm),
-        scratch_shapes=[
-            scratch(4, 24, 16, NZ),
-            scratch(4, 16, 32, NZ),
-            scratch(8, 128),
-            scratch(3, 16, 16, NZ),
-            scratch(16, 16, NZ),
-            scratch(3, 16, 16, NZ),
-            sems(8),
-        ],
-    )(state_path, velocity, *later, supply)
+    slope1, before1 = slopes(1, faces1, supply)
+    faces = halo(lambda x, y: velocity[:, x, y])
 
     normal, wanted_t = call(
         normal_kernel,
@@ -414,7 +417,7 @@
         (struct(COLS, NZ), struct(DEV * V_ROWS, 128)),
         14,
         4,
-        in_specs=[near] + [hbm] * 4,
+        in_specs=[near] + [hbm] * 4 + [tie] * 4,
         out_specs=(hbm, hbm),
         scratch_shapes=[
             pltpu.VMEM((1, COLS), jnp.int32),
@@ -423,13 +426,28 @@
             scratch(4, COLS, NZ),
             scratch(COLS, NZ),
             scratch(DEV * V_ROWS, 128),
-            pltpu.VMEM((3, COLS, NZ), BF16),
+            pltpu.VMEM((2, COLS, NZ), BF16),
             sems(5),
         ],
-    )(arrived, owner_row, weights, before1.reshape(COLS, NZ), normal)
+    )(arrived, owner_row, weights, before1.reshape(COLS, NZ), normal, *faces)
     returned = exchange(push.reshape(DEV, CAP, 2, 128)).reshape(DEV * V_ROWS, 128)
 
-    hess = hess - 0.5 * (lam.reshape(1, 16, 16, NZ) * slope1)
+    hess = call(
+        curve_kernel,
+        per_field(3),
+        14,
+        5,
+        in_specs=[hbm] + [near] * 4 + [hbm] * 2,
+        out_specs=hbm,
+        scratch_shapes=[
+            scratch(3, 24, 16, NZ),
+            scratch(3, 16, 32, NZ),
+            scratch(16, 16, NZ),
+            scratch(3, 16, 16, NZ),
+            scratch(3, 16, 16, NZ),
+            sems(8),
+        ],
+    )(velocity, *faces, lam.reshape(16, 16, NZ), slope1)
     out = call(
         final_kernel,
         struct(3, COLS, NZ),

time: 124 us -> 125 us (level)
  waiting for transfers between devices: 48.8 us -> 35.4 us
  starting transfers between devices: 39 us -> 50 us
  local copies, waits for them, and re-layouts: 4.96 us -> 10.8 us
  other arithmetic: 4.46 us -> 0 us
  Pallas kernels: 25.9 us -> 27.4 us
    ppermute x8 -> x12, waiting for transfers between devices: 34.3 us -> 23.9 us  [neighbours(): return (lax.ppermute(last, axis, up), lax.ppermute(first, axis, down))]
    ppermute x8 -> x12, starting transfers between devices: 14.3 us -> 24 us  [neighbours(): return (lax.ppermute(last, axis, up), lax.ppermute(first, axis, down))]
    unnamed x4 -> x24, local copies, waits for them, and re-layouts: 0.01 us -> 6.5 us
    all_to_all x3, waiting for transfers between devices: 14.5 us -> 11.5 us  [exchange(): return lax.all_to_all(value, AXES, split_axis=0, concat_axis=0, tiled=True)]
    concatenate x4 -> x0, other arithmetic: 2.43 us -> none  [per_device(): jnp.concatenate([state_path[1:, x, y], velocity[:, x, y]], axis=0)]
    sub x1 -> x0, other arithmetic: 2.03 us -> none  [per_device(): hess = hess - 0.5 * (lam.reshape(1, 16, 16, NZ) * slope1)]
    pallas_call x7 -> x8, Pallas kernels: 25.9 us -> 27.4 us  [placed(): run(*(pltpu.with_memory_space_constraint(x, pltpu.HBM) if spec.memory_spa...]
    all_to_all x3, starting transfers between devices: 24.6 us -> 26 us  [exchange(): return lax.all_to_all(value, AXES, split_axis=0, concat_axis=0, tiled=True)]
  transfers between devices with their start and end apart: 11 -> 15, of which waited for: 4 -> 3; matrix products, arithmetic and copies ran while one was open for 8% -> 4% of each run, Pallas kernels for 12% -> 12%
where the time goes in v4:
time: 125 us; the launch traced here: 124 us
  starting transfers between devices  50 us (40%)
  waiting for transfers between devices  35.4 us (28%)
  Pallas kernels  27.4 us (22%)
  local copies, waits for them, and re-layouts  10.8 us (9%)
    pallas_call x8, Pallas kernels, placed(): run(*(pltpu.with_memory_space_constraint(x, pltpu.HBM) if spec.memory_spa...  27.4 us
    all_to_all x3, starting transfers between devices, exchange(): return lax.all_to_all(value, AXES, split_axis=0, concat_axis=0, tiled=True)  26 us
    ppermute x12, starting transfers between devices, neighbours(): return (lax.ppermute(last, axis, up), lax.ppermute(first, axis, down))  24 us
    ppermute x12, waiting for transfers between devices, neighbours(): return (lax.ppermute(last, axis, up), lax.ppermute(first, axis, down))  23.9 us
    all_to_all x3, waiting for transfers between devices, exchange(): return lax.all_to_all(value, AXES, split_axis=0, concat_axis=0, tiled=True)  11.5 us
    unnamed x24, local copies, waits for them, and re-layouts  6.5 us
  transfers between devices with their start and end apart: 15, of which 3 were waited for; matrix products, arithmetic and copies ran while one was open for 4% of the time, Pallas kernels for 12%

profile of v4, /device:TPU:1, one launch (start us, length us, event | category | flops | bytes accessed | tf_op | source)
XLA Modules:
  0.0 123.9 jit_solution(1412129229573112357)
XLA Ops:
  0.0 3.2 %shard_map.55 = f32[6272,128]{1,0:T(8,128)} custom-call(s32[2,1,256]{2,1,0:T(1,128)} %bitcast.25, s32[2,1,256]{2,1,0:T(1,128)} %bitcast.27, bf16[2,4,16,16,256]{4,3,2,1,0:T(8,128)(2,1)} %w_hbm.3), custom_call_target="tpu_custom_call" | custom-call | flops 300000000 | bytes 6000000 | tf_op jit(solution)/shard_map/pallas_call | solution.py:39
  3.2 11.5 %all-to-all-start = ((f32[128,49,1,128]{3,2,1,0:T(1,128)}), f32[128,49,1,128]{3,2,1,0:T(1,128)S(1)}, u32[]{:S(2)}, u32[]{:S(2)}) async-start(f32[128,49,1,128]{3,2,1,0:T(1,128)} %bitcast.17), calls=%async_computation | async-start | bytes 6422528 | tf_op jit(solution)/shard_map/all_to_all | solution.py:326
  14.7 1.0 fusion.3
  15.7 1.8 %collective-permute-start = (f32[1,4,16,256]{3,2,1,0:T(8,128)S(1)}, f32[1,4,16,256]{3,2,1,0:T(8,128)S(1)}, u32[]{:S(2)}, u32[]{:S(2)}) collective-permute-start(f32[1,4,16,256]{3,2,1,0:T(8,128)S(1)} %get-tuple-element.32), channel_id=1, source_target_pairs={{0,16},{16,32},{32,48},{48,64},{64,80},{80,96},{96,112},{112,0},{1... | collective-permute-start | bytes 196616 | tf_op jit(solution)/shard_map/ppermute | solution.py:333
  17.4 1.1 fusion.2
  18.6 1.3 %collective-permute-start.2 = (f32[1,16,4,256]{3,2,1,0:T(4,128)S(1)}, f32[1,16,4,256]{3,2,1,0:T(4,128)S(1)}, u32[]{:S(2)}, u32[]{:S(2)}) collective-permute-start(f32[1,16,4,256]{3,2,1,0:T(4,128)S(1)} %get-tuple-element.28), channel_id=1, source_target_pairs={{0,1},{1,2},{2,3},{3,4},{4,5},{5,6},{6,7},{7,8},{8,9},{9,10},{10,1... | collective-permute-start | bytes 196616 | tf_op jit(solution)/shard_map/ppermute | solution.py:333
  19.9 3.6 %collective-permute-start.3 = (f32[1,16,4,256]{3,2,1,0:T(4,128)S(1)}, f32[1,16,4,256]{3,2,1,0:T(4,128)S(1)}, u32[]{:S(2)}, u32[]{:S(2)}) collective-permute-start(f32[1,16,4,256]{3,2,1,0:T(4,128)S(1)} %get-tuple-element.27), channel_id=1, source_target_pairs={{1,0},{2,1},{3,2},{4,3},{5,4},{6,5},{7,6},{8,7},{9,8},{10,9},{11,1... | collective-permute-start | bytes 196616 | tf_op jit(solution)/shard_map/ppermute | solution.py:333
  23.5 2.3 %collective-permute-start.4 = (f32[1,4,16,256]{3,2,1,0:T(8,128)S(1)}, f32[1,4,16,256]{3,2,1,0:T(8,128)S(1)}, u32[]{:S(2)}, u32[]{:S(2)}) collective-permute-start(f32[1,4,16,256]{3,2,1,0:T(8,128)S(1)} %get-tuple-element.30), channel_id=1, source_target_pairs={{0,16},{16,32},{32,48},{48,64},{64,80},{80,96},{96,112},{112,0},{1... | collective-permute-start | bytes 196616 | tf_op jit(solution)/shard_map/ppermute | solution.py:333
  25.7 3.3 %collective-permute-start.5 = (f32[1,4,16,256]{3,2,1,0:T(8,128)S(1)}, f32[1,4,16,256]{3,2,1,0:T(8,128)S(1)}, u32[]{:S(2)}, u32[]{:S(2)}) collective-permute-start(f32[1,4,16,256]{3,2,1,0:T(8,128)S(1)} %get-tuple-element.29), channel_id=1, source_target_pairs={{16,0},{32,16},{48,32},{64,48},{80,64},{96,80},{112,96},{0,112},{1... | collective-permute-start | bytes 196616 | tf_op jit(solution)/shard_map/ppermute | solution.py:333
  29.0 6.8 %collective-permute-done.1.refs_1_ = f32[1,4,16,256]{3,2,1,0:T(8,128)S(1)} collective-permute-done((f32[1,4,16,256]{3,2,1,0:T(8,128)S(1)}, f32[1,4,16,256]{3,2,1,0:T(8,128)S(1)}, u32[]{:S(2)}, u32[]{:S(2)}) %collective-permute-start.1) | collective-permute-done | bytes 65568 | tf_op jit(solution)/shard_map/ppermute | solution.py:333
  35.8 2.5 %collective-permute-start.6 = (f32[1,16,4,256]{3,2,1,0:T(4,128)S(1)}, f32[1,16,4,256]{3,2,1,0:T(4,128)S(1)}, u32[]{:S(2)}, u32[]{:S(2)}) collective-permute-start(f32[1,16,4,256]{3,2,1,0:T(4,128)S(1)} %get-tuple-element.26), channel_id=1, source_target_pairs={{0,1},{1,2},{2,3},{3,4},{4,5},{5,6},{6,7},{7,8},{8,9},{9,10},{10,1... | collective-permute-start | bytes 196616 | tf_op jit(solution)/shard_map/ppermute | solution.py:333
  38.3 17.1 %collective-permute-done.2.refs_2_ = f32[1,16,4,256]{3,2,1,0:T(4,128)S(1)} collective-permute-done((f32[1,16,4,256]{3,2,1,0:T(4,128)S(1)}, f32[1,16,4,256]{3,2,1,0:T(4,128)S(1)}, u32[]{:S(2)}, u32[]{:S(2)}) %collective-permute-start.2) | collective-permute-done | bytes 65568 | tf_op jit(solution)/shard_map/ppermute | solution.py:333
  55.4 2.6 %collective-permute-start.7 = (f32[1,16,4,256]{3,2,1,0:T(4,128)S(1)}, f32[1,16,4,256]{3,2,1,0:T(4,128)S(1)}, u32[]{:S(2)}, u32[]{:S(2)}) collective-permute-start(f32[1,16,4,256]{3,2,1,0:T(4,128)S(1)} %get-tuple-element.25), channel_id=1, source_target_pairs={{1,0},{2,1},{3,2},{4,3},{5,4},{6,5},{7,6},{8,7},{9,8},{10,9},{11,1... | collective-permute-start | bytes 196616 | tf_op jit(solution)/shard_map/ppermute | solution.py:333
  58.0 3.3 %shard_map.56 = (f32[3,16,16,256]{3,2,1,0:T(8,128)}, f32[16,16,256]{2,1,0:T(8,128)}) custom-call(f32[2,16,16,256]{3,2,1,0:T(8,128)} %st_hbm.3, f32[3,16,16,256]{3,2,1,0:T(8,128)} %ve_hbm.5, f32[1,4,16,256]{3,2,1,0:T(8,128)S(1)} %collective-permute-done.refs_0_, f32[1,4,16,256]{3,2,1,0:T(8,128)S(1)} %collective-permute-done.1.refs_1_, ...), custom_call_target="tpu_custom_call" | custom-call | flops 300000000 | bytes 6000000 | tf_op jit(solution)/shard_map/pallas_call | solution.py:39
  61.4 2.2 %shard_map.57.refs_4_ = f32[1536,128]{1,0:T(8,128)} custom-call(f32[6272,128]{1,0:T(8,128)S(1)} %bitcast.14, f32[256,256]{1,0:T(8,128)} %bitcast.23, f32[1,4,16,256]{3,2,1,0:T(8,128)S(1)} %collective-permute-done.4.refs_0_, f32[1,4,16,256]{3,2,1,0:T(8,128)S(1)} %collective-permute-done.5.refs_1_, f32[1,16,4,256]{3,2,1,0:T(4,128)S(1)} %collective-permute-done.6.refs_2_, ...), custom_call_target="tpu_custom_call" | custom-call | flops 200000000 | bytes 4000000 | tf_op jit(solution)/shard_map/pallas_call | solution.py:39
  63.5 7.6 %all-to-all-start.1 = ((f32[128,6,2,128]{3,2,1,0:T(2,128)}), f32[128,6,2,128]{3,2,1,0:T(2,128)}, u32[]{:S(2)}, u32[]{:S(2)}) async-start(f32[128,6,2,128]{3,2,1,0:T(2,128)} %bitcast.18), calls=%async_computation.1 | async-start | bytes 1572864 | tf_op jit(solution)/shard_map/all_to_all | solution.py:326
  71.1 1.1 fusion.1
  72.2 1.8 %collective-permute-start.8 = (f32[3,4,16,256]{3,2,1,0:T(8,128)S(1)}, f32[3,4,16,256]{3,2,1,0:T(8,128)S(1)}, u32[]{:S(2)}, u32[]{:S(2)}) collective-permute-start(f32[3,4,16,256]{3,2,1,0:T(8,128)S(1)} %get-tuple-element.24), channel_id=1, source_target_pairs={{0,16},{16,32},{32,48},{48,64},{64,80},{80,96},{96,112},{112,0},{1... | collective-permute-start | bytes 589832 | tf_op jit(solution)/shard_map/ppermute | solution.py:333
  74.0 1.2 fusion
  75.2 1.3 %collective-permute-start.10 = (f32[3,16,4,256]{3,2,1,0:T(4,128)S(1)}, f32[3,16,4,256]{3,2,1,0:T(4,128)S(1)}, u32[]{:S(2)}, u32[]{:S(2)}) collective-permute-start(f32[3,16,4,256]{3,2,1,0:T(4,128)S(1)} %get-tuple-element.22), channel_id=1, source_target_pairs={{0,1},{1,2},{2,3},{3,4},{4,5},{5,6},{6,7},{7,8},{8,9},{9,10},{10,1... | collective-permute-start | bytes 589832 | tf_op jit(solution)/shard_map/ppermute | solution.py:333
  76.4 3.6 %collective-permute-start.11 = (f32[3,16,4,256]{3,2,1,0:T(4,128)S(1)}, f32[3,16,4,256]{3,2,1,0:T(4,128)S(1)}, u32[]{:S(2)}, u32[]{:S(2)}) collective-permute-start(f32[3,16,4,256]{3,2,1,0:T(4,128)S(1)} %get-tuple-element.21), channel_id=1, source_target_pairs={{1,0},{2,1},{3,2},{4,3},{5,4},{6,5},{7,6},{8,7},{9,8},{10,9},{11,1... | collective-permute-start | bytes 589832 | tf_op jit(solution)/shard_map/ppermute | solution.py:333
  80.1 0.8 copy-done.9
  81.8 3.3 %shard_map.58 = (f32[3,16,16,256]{3,2,1,0:T(8,128)}, f32[16,16,256]{2,1,0:T(8,128)}) custom-call(f32[2,16,16,256]{3,2,1,0:T(8,128)} %st_hbm.3, f32[3,16,16,256]{3,2,1,0:T(8,128)} %ve_hbm.5, f32[1,4,16,256]{3,2,1,0:T(8,128)S(1)} %collective-permute-done.4.refs_0_, f32[1,4,16,256]{3,2,1,0:T(8,128)S(1)} %collective-permute-done.5.refs_1_, ...), custom_call_target="tpu_custom_call" | custom-call | flops 300000000 | bytes 6000000 | tf_op jit(solution)/shard_map/pallas_call | solution.py:39
  85.0 3.3 %shard_map.59 = (f32[4,256,256]{2,1,0:T(8,128)}, f32[16,128]{1,0:T(8,128)}) custom-call(f32[6272,128]{1,0:T(8,128)S(1)} %bitcast.15), custom_call_target="tpu_custom_call" | custom-call | flops 400000000 | bytes 8000000 | tf_op jit(solution)/shard_map/pallas_call | solution.py:39
  90.4 0.9 copy-done.1
  91.3 0.9 copy-done.4
  92.2 0.9 copy-done.7
  93.2 4.9 %shard_map.60 = (f32[256,256]{1,0:T(8,128)}, f32[1536,128]{1,0:T(8,128)}) custom-call(f32[1536,128]{1,0:T(8,128)} %bitcast.6.arr, s32[2,1,256]{2,1,0:T(1,128)} %bitcast.26, bf16[2,4,16,16,256]{4,3,2,1,0:T(8,128)(2,1)} %w_hbm.3, f32[256,256]{1,0:T(8,128)} %bitcast.22, f32[4,256,256]{2,1,0:T(8,128)} %get-tuple-element.15.d_hbm, ...), custom_call_target="tpu_custom_call" | custom-call | flops 400000000 | bytes 8000000 | tf_op jit(solution)/shard_map/pallas_call | solution.py:39
  98.1 6.9 %all-to-all-start.2 = ((f32[128,6,2,128]{3,2,1,0:T(2,128)}), f32[128,6,2,128]{3,2,1,0:T(2,128)S(1)}, u32[]{:S(2)}, u32[]{:S(2)}) async-start(f32[128,6,2,128]{3,2,1,0:T(2,128)} %bitcast.20), calls=%async_computation.2 | async-start | bytes 1572864 | tf_op jit(solution)/shard_map/all_to_all | solution.py:326
  105.1 5.0 %shard_map.61 = f32[3,16,16,256]{3,2,1,0:T(8,128)} custom-call(f32[3,16,16,256]{3,2,1,0:T(8,128)} %ve_hbm.5, f32[3,4,16,256]{3,2,1,0:T(8,128)S(1)} %collective-permute-done.8.refs_0_.xlo, f32[3,4,16,256]{3,2,1,0:T(8,128)S(1)} %copy-done.2, f32[3,16,4,256]{3,2,1,0:T(4,128)S(1)} %copy-done.5, f32[3,16,4,256]{3,2,1,0:T(4,128)S(1)} %copy-done.7, ...), custom_call_target="tpu_custom_call" | custom-call | flops 500000000 | bytes 10000000 | tf_op jit(solution)/shard_map/pallas_call | solution.py:39
  110.1 11.5 %all-to-all-done.2 = f32[128,6,2,128]{3,2,1,0:T(2,128)S(1)} async-done(((f32[128,6,2,128]{3,2,1,0:T(2,128)}), f32[128,6,2,128]{3,2,1,0:T(2,128)S(1)}, u32[]{:S(2)}, u32[]{:S(2)}) %all-to-all-start.2) | async-done | bytes 786464 | tf_op jit(solution)/shard_map/all_to_all | solution.py:326
  121.6 2.3 %shard_map.62 = f32[3,256,256]{2,1,0:T(8,128)} custom-call(f32[1536,128]{1,0:T(8,128)S(1)} %bitcast.16, f32[16,128]{1,0:T(8,128)} %get-tuple-element.17.wt_hbm, f32[3,256,256]{2,1,0:T(8,128)} %bitcast.19, f32[3,256,256]{2,1,0:T(8,128)} %bitcast.21), custom_call_target="tpu_custom_call" | custom-call | flops 200000000 | bytes 4000000 | tf_op jit(solution)/shard_map/pallas_call | solution.py:39
  (34 shorter events, 2.9 us)
Async XLA Ops:
  3.2 58.2 %all-to-all-start = ((f32[128,49,1,128]{3,2,1,0:T(1,128)}), f32[128,49,1,128]{3,2,1,0:T(1,128)S(1)}, u32[]{:S(2)}, u32[]{:S(2)}) async-start(f32[128,49,1,128]{3,2,1,0:T(1,128)} %bitcast.17), calls=%async_computation | async-start | bytes 6422528 | tf_op jit(solution)/shard_map/all_to_all | solution.py:326
  15.7 10.1 %collective-permute-start = (f32[1,4,16,256]{3,2,1,0:T(8,128)S(1)}, f32[1,4,16,256]{3,2,1,0:T(8,128)S(1)}, u32[]{:S(2)}, u32[]{:S(2)}) collective-permute-start(f32[1,4,16,256]{3,2,1,0:T(8,128)S(1)} %get-tuple-element.32), channel_id=1, source_target_pairs={{0,16},{16,32},{32,48},{48,64},{64,80},{80,96},{96,112},{112,0},{1... | collective-permute-start | bytes 196616 | tf_op jit(solution)/shard_map/ppermute | solution.py:333
  17.4 18.4 %collective-permute-start.1 = (f32[1,4,16,256]{3,2,1,0:T(8,128)S(1)}, f32[1,4,16,256]{3,2,1,0:T(8,128)S(1)}, u32[]{:S(2)}, u32[]{:S(2)}) collective-permute-start(f32[1,4,16,256]{3,2,1,0:T(8,128)S(1)} %get-tuple-element.31), channel_id=1, source_target_pairs={{16,0},{32,16},{48,32},{64,48},{80,64},{96,80},{112,96},{0,112},{1... | collective-permute-start | bytes 196616 | tf_op jit(solution)/shard_map/ppermute | solution.py:333
  18.6 36.9 %collective-permute-start.2 = (f32[1,16,4,256]{3,2,1,0:T(4,128)S(1)}, f32[1,16,4,256]{3,2,1,0:T(4,128)S(1)}, u32[]{:S(2)}, u32[]{:S(2)}) collective-permute-start(f32[1,16,4,256]{3,2,1,0:T(4,128)S(1)} %get-tuple-element.28), channel_id=1, source_target_pairs={{0,1},{1,2},{2,3},{3,4},{4,5},{5,6},{6,7},{7,8},{8,9},{9,10},{10,1... | collective-permute-start | bytes 196616 | tf_op jit(solution)/shard_map/ppermute | solution.py:333
  19.9 38.2 %collective-permute-start.3 = (f32[1,16,4,256]{3,2,1,0:T(4,128)S(1)}, f32[1,16,4,256]{3,2,1,0:T(4,128)S(1)}, u32[]{:S(2)}, u32[]{:S(2)}) collective-permute-start(f32[1,16,4,256]{3,2,1,0:T(4,128)S(1)} %get-tuple-element.27), channel_id=1, source_target_pairs={{1,0},{2,1},{3,2},{4,3},{5,4},{6,5},{7,6},{8,7},{9,8},{10,9},{11,1... | collective-permute-start | bytes 196616 | tf_op jit(solution)/shard_map/ppermute | solution.py:333
  23.5 37.8 %collective-permute-start.4 = (f32[1,4,16,256]{3,2,1,0:T(8,128)S(1)}, f32[1,4,16,256]{3,2,1,0:T(8,128)S(1)}, u32[]{:S(2)}, u32[]{:S(2)}) collective-permute-start(f32[1,4,16,256]{3,2,1,0:T(8,128)S(1)} %get-tuple-element.30), channel_id=1, source_target_pairs={{0,16},{16,32},{32,48},{48,64},{64,80},{80,96},{96,112},{112,0},{1... | collective-permute-start | bytes 196616 | tf_op jit(solution)/shard_map/ppermute | solution.py:333
  25.7 35.6 %collective-permute-start.5 = (f32[1,4,16,256]{3,2,1,0:T(8,128)S(1)}, f32[1,4,16,256]{3,2,1,0:T(8,128)S(1)}, u32[]{:S(2)}, u32[]{:S(2)}) collective-permute-start(f32[1,4,16,256]{3,2,1,0:T(8,128)S(1)} %get-tuple-element.29), channel_id=1, source_target_pairs={{16,0},{32,16},{48,32},{64,48},{80,64},{96,80},{112,96},{0,112},{1... | collective-permute-start | bytes 196616 | tf_op jit(solution)/shard_map/ppermute | solution.py:333
  35.8 25.5 %collective-permute-start.6 = (f32[1,16,4,256]{3,2,1,0:T(4,128)S(1)}, f32[1,16,4,256]{3,2,1,0:T(4,128)S(1)}, u32[]{:S(2)}, u32[]{:S(2)}) collective-permute-start(f32[1,16,4,256]{3,2,1,0:T(4,128)S(1)} %get-tuple-element.26), channel_id=1, source_target_pairs={{0,1},{1,2},{2,3},{3,4},{4,5},{5,6},{6,7},{7,8},{8,9},{9,10},{10,1... | collective-permute-start | bytes 196616 | tf_op jit(solution)/shard_map/ppermute | solution.py:333
  55.4 5.9 %collective-permute-start.7 = (f32[1,16,4,256]{3,2,1,0:T(4,128)S(1)}, f32[1,16,4,256]{3,2,1,0:T(4,128)S(1)}, u32[]{:S(2)}, u32[]{:S(2)}) collective-permute-start(f32[1,16,4,256]{3,2,1,0:T(4,128)S(1)} %get-tuple-element.25), channel_id=1, source_target_pairs={{1,0},{2,1},{3,2},{4,3},{5,4},{6,5},{7,6},{8,7},{9,8},{10,9},{11,1... | collective-permute-start | bytes 196616 | tf_op jit(solution)/shard_map/ppermute | solution.py:333
  61.3 10.9 %copy-start.8 = (f32[1,16,4,256]{3,2,1,0:T(4,128)}, f32[1,16,4,256]{3,2,1,0:T(4,128)S(1)}, u32[]{:S(2)}) copy-start(f32[1,16,4,256]{3,2,1,0:T(4,128)S(1)} %collective-permute-done.6.refs_2_) | copy-start | bytes 196612
  61.3 10.9 %copy-start.10 = (f32[1,16,4,256]{3,2,1,0:T(4,128)}, f32[1,16,4,256]{3,2,1,0:T(4,128)S(1)}, u32[]{:S(2)}) copy-start(f32[1,16,4,256]{3,2,1,0:T(4,128)S(1)} %collective-permute-done.7.refs_3_) | copy-start | bytes 196612
  63.5 26.9 %all-to-all-start.1 = ((f32[128,6,2,128]{3,2,1,0:T(2,128)}), f32[128,6,2,128]{3,2,1,0:T(2,128)}, u32[]{:S(2)}, u32[]{:S(2)}) async-start(f32[128,6,2,128]{3,2,1,0:T(2,128)} %bitcast.18), calls=%async_computation.1 | async-start | bytes 1572864 | tf_op jit(solution)/shard_map/all_to_all | solution.py:326
  72.2 16.1 %collective-permute-start.8 = (f32[3,4,16,256]{3,2,1,0:T(8,128)S(1)}, f32[3,4,16,256]{3,2,1,0:T(8,128)S(1)}, u32[]{:S(2)}, u32[]{:S(2)}) collective-permute-start(f32[3,4,16,256]{3,2,1,0:T(8,128)S(1)} %get-tuple-element.24), channel_id=1, source_target_pairs={{0,16},{16,32},{32,48},{48,64},{64,80},{80,96},{96,112},{112,0},{1... | collective-permute-start | bytes 589832 | tf_op jit(solution)/shard_map/ppermute | solution.py:333
  74.0 14.3 %collective-permute-start.9 = (f32[3,4,16,256]{3,2,1,0:T(8,128)S(1)}, f32[3,4,16,256]{3,2,1,0:T(8,128)S(1)}, u32[]{:S(2)}, u32[]{:S(2)}) collective-permute-start(f32[3,4,16,256]{3,2,1,0:T(8,128)S(1)} %get-tuple-element.23), channel_id=1, source_target_pairs={{16,0},{32,16},{48,32},{64,48},{80,64},{96,80},{112,96},{0,112},{1... | collective-permute-start | bytes 589832 | tf_op jit(solution)/shard_map/ppermute | solution.py:333
  75.2 13.9 %collective-permute-start.10 = (f32[3,16,4,256]{3,2,1,0:T(4,128)S(1)}, f32[3,16,4,256]{3,2,1,0:T(4,128)S(1)}, u32[]{:S(2)}, u32[]{:S(2)}) collective-permute-start(f32[3,16,4,256]{3,2,1,0:T(4,128)S(1)} %get-tuple-element.22), channel_id=1, source_target_pairs={{0,1},{1,2},{2,3},{3,4},{4,5},{5,6},{6,7},{7,8},{8,9},{9,10},{10,1... | collective-permute-start | bytes 589832 | tf_op jit(solution)/shard_map/ppermute | solution.py:333
  76.4 13.3 %collective-permute-start.11 = (f32[3,16,4,256]{3,2,1,0:T(4,128)S(1)}, f32[3,16,4,256]{3,2,1,0:T(4,128)S(1)}, u32[]{:S(2)}, u32[]{:S(2)}) collective-permute-start(f32[3,16,4,256]{3,2,1,0:T(4,128)S(1)} %get-tuple-element.21), channel_id=1, source_target_pairs={{1,0},{2,1},{3,2},{4,3},{5,4},{6,5},{7,6},{8,7},{9,8},{10,9},{11,1... | collective-permute-start | bytes 589832 | tf_op jit(solution)/shard_map/ppermute | solution.py:333
  80.1 0.8 copy-start.9
  80.9 0.8 copy-start.11
  88.3 0.7 copy-start
  89.0 0.7 copy-start.3
  89.7 0.7 copy-start.6
  90.4 0.9 copy-start.1
  91.3 0.9 copy-start.4
  92.2 0.9 copy-start.7
  93.2 11.9 %copy-start.2 = (f32[3,4,16,256]{3,2,1,0:T(8,128)S(1)}, f32[3,4,16,256]{3,2,1,0:T(8,128)}, u32[]{:S(2)}) copy-start(f32[3,4,16,256]{3,2,1,0:T(8,128)} %copy-done) | copy-start | bytes 589828
  93.2 11.9 %copy-start.5 = (f32[3,16,4,256]{3,2,1,0:T(4,128)S(1)}, f32[3,16,4,256]{3,2,1,0:T(4,128)}, u32[]{:S(2)}) copy-start(f32[3,16,4,256]{3,2,1,0:T(4,128)} %copy-done.3) | copy-start | bytes 589828
  98.1 23.5 %all-to-all-start.2 = ((f32[128,6,2,128]{3,2,1,0:T(2,128)}), f32[128,6,2,128]{3,2,1,0:T(2,128)S(1)}, u32[]{:S(2)}, u32[]{:S(2)}) async-start(f32[128,6,2,128]{3,2,1,0:T(2,128)} %bitcast.20), calls=%async_computation.2 | async-start | bytes 1572864 | tf_op jit(solution)/shard_map/all_to_all | solution.py:326

commit v5 on v4

--- a/solution.py
+++ b/solution.py
@@ -134,18 +134,14 @@
     wait_all(sent)
 
 
-def fill(sources, halos, xpad, ypad, sems, extra=()):
-    xlo, xhi, ylo, yhi = halos
-    pairs = list(extra)
+def fill(sources, halos, xpad, ypad, ylo, yhi, sems, extra=()):
+    pairs = list(extra) + [(halos[2], ylo), (halos[3], yhi)]
+    pairs += [(halos[0], xpad.at[:, pl.ds(0, 4)]), (halos[1], xpad.at[:, pl.ds(20, 4)])]
     for i, source in enumerate(sources):
         pairs += [(source, xpad.at[i, pl.ds(4, 16)]), (source, ypad.at[i, :, pl.ds(8, 16)])]
-    copies = start_all(pairs, sems)
-    for i in range(len(sources)):
-        xpad[i, 0:4] = xlo[i]
-        xpad[i, 20:24] = xhi[i]
-        ypad[i, :, 4:8] = ylo[i]
-        ypad[i, :, 24:28] = yhi[i]
-    return copies
+    wait_all(start_all(pairs, sems))
+    ypad[:, :, 4:8] = ylo[...]
+    ypad[:, :, 24:28] = yhi[...]
 
 
 def differences(xpad, ypad, i, x, rows, coeffs, sign):
@@ -167,48 +163,49 @@
 ROWS = 4
 
 
-def slope_kernel(step, st_hbm, ve_hbm, *refs):
-    g_hbm, b_hbm, xpad, ypad, ve, g, b, sems = refs[-8:]
-    wait_all(fill([st_hbm.at[step]], refs[:4], xpad, ypad, sems, [(ve_hbm, ve)]))
-
-    def block(x):
-        here = pl.ds(x, ROWS)
-        slope = differences(xpad, ypad, 0, x, ROWS, FIRST, -1.0)[1]
-        total = None
+def faces_kernel(st_hbm, ve_hbm, xlo, xhi, ylo, yhi, edges, sems):
+    pairs = []
+    for out, y_out, first, y_first in ((xlo, 0, 0, 0), (xhi, 1, 12, 8)):
+        for source, place in ((st_hbm, pl.ds(0, 2)), (ve_hbm, pl.ds(2, 3))):
+            pairs.append((source.at[:, pl.ds(first, 4)], out.at[place]))
+            pairs.append((source.at[:, :, pl.ds(y_first, 8)], edges.at[y_out, place]))
+    wait_all(start_all(pairs, sems))
+    ylo[...] = edges[0, :, :, 0:4]
+    yhi[...] = edges[1, :, :, 4:8]
+
+
+def stencil_kernel(st_hbm, ve_hbm, xlo, xhi, ylo, yhi, g_hbm, b_hbm, h_hbm, xpad, ypad, ylo_scr, yhi_scr, g, b, h, sems):
+    sources = [st_hbm.at[j] for j in range(2)] + [ve_hbm.at[c] for c in range(3)]
+    fill(sources, (xlo, xhi, ylo, yhi), xpad, ypad, ylo_scr, yhi_scr, sems)
+    sent = []
+    for j in range(2):
+
+        @pl.loop(0, 16, step=ROWS)
+        def slope_rows(x):
+            here = pl.ds(x, ROWS)
+            slope = differences(xpad, ypad, j, x, ROWS, FIRST, -1.0)[1]
+            total = None
+            for c in range(3):
+                g[j, c, here] = slope[c]
+                term = xpad[2 + c, pl.ds(x + 4, ROWS)] * slope[c]
+                total = term if total is None else total + term
+            b[j, here] = -0.5 * total
+
+        sent += start_all(((b.at[j], b_hbm.at[j]), (g.at[j], g_hbm.at[j])), sems, len(sent))
+
+    @pl.loop(0, 16, step=ROWS)
+    def curve_rows(x):
         for c in range(3):
-            g[c, here] = slope[c]
-            term = ve[c, here] * slope[c]
-            total = term if total is None else total + term
-        b[here] = -0.5 * total
-
-    sent = []
-    for first in (0, 8):
-        pl.loop(first, first + 8, step=ROWS)(block)
-        half = pl.ds(first, 8)
-        pairs = ((b.at[half], b_hbm.at[half]), (g.at[:, half], g_hbm.at[:, half]))
-        sent += start_all(pairs, sems, len(sent))
-    wait_all(sent)
-
-
-def curve_kernel(ve_hbm, xlo, xhi, ylo, yhi, lam_hbm, g_hbm, h_hbm, xpad, ypad, lam, g, h, sems):
-    sources = [ve_hbm.at[c] for c in range(3)]
-    extra = [(lam_hbm, lam), (g_hbm, g)]
-    wait_all(fill(sources, (xlo, xhi, ylo, yhi), xpad, ypad, sems, extra))
-
-    def block(x):
-        here = pl.ds(x, ROWS)
-        for c in range(3):
-            centre, parts = differences(xpad, ypad, c, x, ROWS, SECOND[1:], 1.0)
+            centre, parts = differences(xpad, ypad, 2 + c, x, ROWS, SECOND[1:], 1.0)
             total = 3.0 * SECOND[0] * centre + parts[0] + parts[1] + parts[2]
-            h[c, here] = -BETA * total - 0.5 * (lam[here] * g[c, here])
-
-    pl.loop(0, 16, step=ROWS)(block)
-    wait_all(start_all(((h, h_hbm),), sems))
-
-
-def supply_kernel(asked, b_hbm, *refs):
-    out_hbm, b, out, sems = refs[-4:]
-    copies = start_all(((b_hbm, b),), sems)
+            h[c, pl.ds(x, ROWS)] = -BETA * total
+
+    sent += start_all(((h, h_hbm),), sems, len(sent))
+    wait_all(sent)
+
+
+def supply_kernel(asked, b_hbm, out_hbm, b, out, sems):
+    copies = start_all(((b_hbm.at[0], b),), sems)
     wanted = asked[pl.ds(W_ROWS, DEV, stride=A_ROWS), :]
     place = iota((PART, COLS), 1).astype(F32)
     onehots = [
@@ -234,7 +231,8 @@
     )
 
 
-def normal_kernel(asked, d_hbm, wt_hbm, w, d, wt, sems):
+def normal_kernel(asked, *refs):
+    d_hbm, wt_hbm, w, d, wt, sems = refs[-6:]
     wanted_t = asked[pl.ds(W_ROWS, DEV, stride=A_ROWS), :].T
     wt[...] = wanted_t[:16]
     sent = start_all(((wt, wt_hbm),), sems)
@@ -274,7 +272,7 @@
 
 def middle_kernel(arr, own_hbm, w_hbm, b_hbm, d_hbm, *refs):
     lam_hbm, out_hbm, own, w, b, d, lam_scr, out, parts, sems = refs[-10:]
-    copies = start_all(((own_hbm.at[0], own), (w_hbm.at[0], w), (b_hbm, b), (d_hbm, d)), sems)
+    copies = start_all(((own_hbm.at[0], own), (w_hbm.at[0], w), (b_hbm.at[1], b), (d_hbm, d)), sems)
     copies[0].wait()
     owner_row = own[...]
     taken = jnp.concatenate([ones(m) for m in masks_by_column(owner_row)], axis=1)
@@ -310,7 +308,7 @@
 
 
 def final_kernel(arr, wt_hbm, h_hbm, g_hbm, out_hbm, wt, h, g, out, sems):
-    copies = start_all(((wt_hbm, wt), (h_hbm, h), (g_hbm, g)), sems)
+    copies = start_all(((wt_hbm, wt), (h_hbm, h), (g_hbm.at[0], g)), sems)
     copies[0].wait()
     onehot_t = gathered_rows(wt[...], 0)
     lam = select(onehot_t, split(read_slots(arr)))
@@ -360,47 +358,47 @@
     )(owner_row, source_row, weights)
     asked = exchange(request.reshape(DEV, A_ROWS, 1, 128)).reshape(DEV * A_ROWS, 128)
 
-    def halo(fields):
-        xlo, xhi = neighbours(fields(slice(0, 4), slice(None)), fields(slice(12, 16), slice(None)), "gx")
-        ylo, yhi = neighbours(fields(slice(None), slice(0, 4)), fields(slice(None), slice(12, 16)), "gy")
-        return xlo, xhi, ylo, yhi
-
-    tie = pl.BlockSpec(memory_space=pl.ANY)
-
-    def slopes(step, faces, *after):
-        return call(
-            functools.partial(slope_kernel, step),
-            (per_field(3), struct(16, 16, NZ)),
-            10,
-            3,
-            in_specs=[hbm] * 2 + [near] * 4 + [hbm] * len(after),
-            out_specs=(hbm, hbm),
-            scratch_shapes=[
-                scratch(1, 24, 16, NZ),
-                scratch(1, 16, 32, NZ),
-                scratch(3, 16, 16, NZ),
-                scratch(3, 16, 16, NZ),
-                scratch(16, 16, NZ),
-                sems(4),
-            ],
-        )(state_path, velocity, *faces, *after)
-
-    slope0, before0 = slopes(0, halo(lambda x, y: state_path[:1, x, y]))
-    faces1 = halo(lambda x, y: state_path[1:, x, y])
+    edge = pltpu.VMEM((5, 4, 16, NZ), F32), pltpu.VMEM((5, 16, 4, NZ), F32)
+    first_x, last_x, first_y, last_y = call(
+        faces_kernel,
+        (edge[0], edge[0], edge[1], edge[1]),
+        10,
+        1,
+        in_specs=[hbm] * 2,
+        out_specs=(near,) * 4,
+        scratch_shapes=[scratch(2, 5, 16, 8, NZ), sems(8)],
+    )(state_path, velocity)
+    halos = neighbours(first_x, last_x, "gx") + neighbours(first_y, last_y, "gy")
+    slopes, before, hess = call(
+        stencil_kernel,
+        (struct(2, 3, 16, 16, NZ), struct(2, 16, 16, NZ), per_field(3)),
+        24,
+        1000,
+        in_specs=[hbm] * 6,
+        out_specs=(hbm,) * 3,
+        scratch_shapes=[
+            scratch(5, 24, 16, NZ),
+            scratch(5, 16, 32, NZ),
+            scratch(5, 16, 4, NZ),
+            scratch(5, 16, 4, NZ),
+            scratch(2, 3, 16, 16, NZ),
+            scratch(2, 16, 16, NZ),
+            scratch(3, 16, 16, NZ),
+            sems(14),
+        ],
+    )(state_path, velocity, *halos)
+    before = before.reshape(2, COLS, NZ)
 
     supply = call(
         supply_kernel,
         struct(DEV * V_ROWS, 128),
         8,
         2,
-        in_specs=[near, hbm] + [tie] * 4,
+        in_specs=[near, hbm],
         out_specs=hbm,
         scratch_shapes=[scratch(COLS, NZ), scratch(DEV * V_ROWS, 128), sems(5)],
-    )(asked, before0.reshape(COLS, NZ), *faces1)
+    )(asked, before)
     arrived = exchange(supply.reshape(DEV, CAP, 2, 128)).reshape(DEV * V_ROWS, 128)
-
-    slope1, before1 = slopes(1, faces1, supply)
-    faces = halo(lambda x, y: velocity[:, x, y])
 
     normal, wanted_t = call(
         normal_kernel,
@@ -417,7 +415,7 @@
         (struct(COLS, NZ), struct(DEV * V_ROWS, 128)),
         14,
         4,
-        in_specs=[near] + [hbm] * 4 + [tie] * 4,
+        in_specs=[near] + [hbm] * 4,
         out_specs=(hbm, hbm),
         scratch_shapes=[
             pltpu.VMEM((1, COLS), jnp.int32),
@@ -429,25 +427,10 @@
             pltpu.VMEM((2, COLS, NZ), BF16),
             sems(5),
         ],
-    )(arrived, owner_row, weights, before1.reshape(COLS, NZ), normal, *faces)
+    )(arrived, owner_row, weights, before, normal)
     returned = exchange(push.reshape(DEV, CAP, 2, 128)).reshape(DEV * V_ROWS, 128)
 
-    hess = call(
-        curve_kernel,
-        per_field(3),
-        14,
-        5,
-        in_specs=[hbm] + [near] * 4 + [hbm] * 2,
-        out_specs=hbm,
-        scratch_shapes=[
-            scratch(3, 24, 16, NZ),
-            scratch(3, 16, 32, NZ),
-            scratch(16, 16, NZ),
-            scratch(3, 16, 16, NZ),
-            scratch(3, 16, 16, NZ),
-            sems(8),
-        ],
-    )(velocity, *faces, lam.reshape(16, 16, NZ), slope1)
+    hess = hess - 0.5 * (lam.reshape(1, 16, 16, NZ) * slopes[1])
     out = call(
         final_kernel,
         struct(3, COLS, NZ),
@@ -462,7 +445,7 @@
             scratch(3, COLS, NZ),
             sems(3),
         ],
-    )(returned, wanted_t, hess.reshape(3, COLS, NZ), slope0.reshape(3, COLS, NZ))
+    )(returned, wanted_t, hess.reshape(3, COLS, NZ), slopes.reshape(2, 3, COLS, NZ))
     return out.reshape(3, 16, 16, NZ)
 
 

time: 125 us -> 115 us (0.920)
  waiting for transfers between devices: 35.4 us -> 61.3 us
  starting transfers between devices: 50 us -> 24.8 us
  local copies, waits for them, and re-layouts: 10.8 us -> 0.01 us
  other arithmetic: 0 us -> 2.05 us
    all_to_all x3, waiting for transfers between devices: 11.5 us -> 61.3 us  [exchange(): return lax.all_to_all(value, AXES, split_axis=0, concat_axis=0, tiled=True)]
    ppermute x12 -> x4, waiting for transfers between devices: 23.9 us -> 0.01 us  [neighbours(): return (lax.ppermute(last, axis, up), lax.ppermute(first, axis, down))]
    ppermute x12 -> x4, starting transfers between devices: 24 us -> 7.97 us  [neighbours(): return (lax.ppermute(last, axis, up), lax.ppermute(first, axis, down))]
    all_to_all x3, starting transfers between devices: 26 us -> 16.8 us  [exchange(): return lax.all_to_all(value, AXES, split_axis=0, concat_axis=0, tiled=True)]
    unnamed x24 -> x4, local copies, waits for them, and re-layouts: 6.5 us -> 0.01 us
    slice x4 -> x0, local copies, waits for them, and re-layouts: 4.34 us -> none  [the longest x2 2.24 us: per_device(): faces = halo(lambda x, y: velocity[:, x, y])]
    sub x0 -> x1, other arithmetic: none -> 2.05 us  [per_device(): hess = hess - 0.5 * (lam.reshape(1, 16, 16, NZ) * slopes[1])]
    pallas_call x8 -> x7, Pallas kernels: 27.4 us -> 26.2 us  [placed(): run(*(pltpu.with_memory_space_constraint(x, pltpu.HBM) if spec.memory_spa...]
  transfers between devices with their start and end apart: 15 -> 7, of which waited for: 3 -> 3; matrix products, arithmetic and copies ran while one was open for 4% -> 2% of each run, Pallas kernels for 12% -> 12%
where the time goes in v5:
time: 115 us; the launch traced here: 114 us
  waiting for transfers between devices  61.3 us (53%)
  Pallas kernels  26.2 us (23%)
  starting transfers between devices  24.8 us (22%)
  other arithmetic  2.05 us (2%)
    all_to_all x3, waiting for transfers between devices, exchange(): return lax.all_to_all(value, AXES, split_axis=0, concat_axis=0, tiled=True)  61.3 us
    pallas_call x7, Pallas kernels, placed(): run(*(pltpu.with_memory_space_constraint(x, pltpu.HBM) if spec.memory_spa...  26.2 us
    all_to_all x3, starting transfers between devices, exchange(): return lax.all_to_all(value, AXES, split_axis=0, concat_axis=0, tiled=True)  16.8 us
    ppermute x4, starting transfers between devices, neighbours(): return (lax.ppermute(last, axis, up), lax.ppermute(first, axis, down))  7.97 us
  transfers between devices with their start and end apart: 7, of which 3 were waited for; matrix products, arithmetic and copies ran while one was open for 2% of the time, Pallas kernels for 12%

profile of v5, /device:TPU:1, one launch (start us, length us, event | category | flops | bytes accessed | tf_op | source)
XLA Modules:
  0.0 114.5 jit_solution(16217677255258133429)
XLA Ops:
  0.0 2.5 %shard_map.56 = (f32[5,4,16,256]{3,2,1,0:T(8,128)}, f32[5,4,16,256]{3,2,1,0:T(8,128)}, f32[5,16,4,256]{3,2,1,0:T(4,128)S(1)}, f32[5,16,4,256]{3,2,1,0:T(4,128)}) custom-call(f32[2,16,16,256]{3,2,1,0:T(8,128)} %st_hbm.3, f32[3,16,16,256]{3,2,1,0:T(8,128)} %ve_hbm.3), custom_call_target="tpu_custom_call" | custom-call | flops 100000000 | bytes 2000000 | tf_op jit(solution)/shard_map/pallas_call | solution.py:39
  2.6 3.0 %collective-permute-start = (f32[5,4,16,256]{3,2,1,0:T(8,128)}, f32[5,4,16,256]{3,2,1,0:T(8,128)}, u32[]{:S(2)}, u32[]{:S(2)}) collective-permute-start(f32[5,4,16,256]{3,2,1,0:T(8,128)} %get-tuple-element.16), channel_id=1, source_target_pairs={{0,16},{16,32},{32,48},{48,64},{64,80},{80,96},{96,112},{112,0},{1... | collective-permute-start | bytes 983048 | tf_op jit(solution)/shard_map/ppermute | solution.py:331
  5.6 0.0 collective-permute-start.1
  5.6 1.2 %collective-permute-start.2 = (f32[5,16,4,256]{3,2,1,0:T(4,128)}, f32[5,16,4,256]{3,2,1,0:T(4,128)}, u32[]{:S(2)}, u32[]{:S(2)}) collective-permute-start(f32[5,16,4,256]{3,2,1,0:T(4,128)} %get-tuple-element.18), channel_id=1, source_target_pairs={{0,1},{1,2},{2,3},{3,4},{4,5},{5,6},{6,7},{7,8},{8,9},{9,10},{10,1... | collective-permute-start | bytes 983048 | tf_op jit(solution)/shard_map/ppermute | solution.py:331
  6.8 3.7 %collective-permute-start.3 = (f32[5,16,4,256]{3,2,1,0:T(4,128)S(1)}, f32[5,16,4,256]{3,2,1,0:T(4,128)}, u32[]{:S(2)}, u32[]{:S(2)}) collective-permute-start(f32[5,16,4,256]{3,2,1,0:T(4,128)S(1)} %get-tuple-element.19), channel_id=1, source_target_pairs={{1,0},{2,1},{3,2},{4,3},{5,4},{6,5},{7,6},{8,7},{9,8},{10,9},{11,1... | collective-permute-start | bytes 983048 | tf_op jit(solution)/shard_map/ppermute | solution.py:331
  10.5 3.2 %shard_map.55 = f32[6272,128]{1,0:T(8,128)} custom-call(s32[2,1,256]{2,1,0:T(1,128)} %bitcast.30, s32[2,1,256]{2,1,0:T(1,128)} %bitcast.32, bf16[2,4,16,16,256]{4,3,2,1,0:T(8,128)(2,1)} %w_hbm.3), custom_call_target="tpu_custom_call" | custom-call | flops 300000000 | bytes 6000000 | tf_op jit(solution)/shard_map/pallas_call | solution.py:39
  13.7 7.3 %all-to-all-start = ((f32[128,49,1,128]{3,2,1,0:T(1,128)}), f32[128,49,1,128]{3,2,1,0:T(1,128)S(1)}, u32[]{:S(2)}, u32[]{:S(2)}) async-start(f32[128,49,1,128]{3,2,1,0:T(1,128)} %bitcast.22), calls=%async_computation | async-start | bytes 6422528 | tf_op jit(solution)/shard_map/all_to_all | solution.py:324
  21.1 0.0 collective-permute-done.xlo
  21.1 0.0 collective-permute-done.1.xhi
  21.1 0.0 collective-permute-done.2.ylo
  21.1 0.0 collective-permute-done.3.yhi
  21.1 7.8 %shard_map.57 = (f32[2,3,16,16,256]{4,3,2,1,0:T(8,128)}, f32[2,16,16,256]{3,2,1,0:T(8,128)}, f32[3,16,16,256]{3,2,1,0:T(8,128)}) custom-call(f32[2,16,16,256]{3,2,1,0:T(8,128)} %st_hbm.3, f32[3,16,16,256]{3,2,1,0:T(8,128)} %ve_hbm.3, f32[5,4,16,256]{3,2,1,0:T(8,128)} %collective-permute-done.xlo, f32[5,4,16,256]{3,2,1,0:T(8,128)} %collective-permute-done.1.xhi, ...), custom_call_target="tpu_custom_call" | custom-call | flops 99999997952 | bytes 2000000000 | tf_op jit(solution)/shard_map/pallas_call | solution.py:39
  28.9 33.7 %all-to-all-done = f32[128,49,1,128]{3,2,1,0:T(1,128)S(1)} async-done(((f32[128,49,1,128]{3,2,1,0:T(1,128)}), f32[128,49,1,128]{3,2,1,0:T(1,128)S(1)}, u32[]{:S(2)}, u32[]{:S(2)}) %all-to-all-start) | async-done | bytes 3211296 | tf_op jit(solution)/shard_map/all_to_all | solution.py:324
  62.6 2.2 %shard_map.58 = f32[1536,128]{1,0:T(8,128)} custom-call(f32[6272,128]{1,0:T(8,128)S(1)} %bitcast.19, f32[2,256,256]{2,1,0:T(8,128)} %bitcast.26), custom_call_target="tpu_custom_call" | custom-call | flops 200000000 | bytes 4000000 | tf_op jit(solution)/shard_map/pallas_call | solution.py:39
  64.8 5.2 %all-to-all-start.1 = ((f32[128,6,2,128]{3,2,1,0:T(2,128)}), f32[128,6,2,128]{3,2,1,0:T(2,128)}, u32[]{:S(2)}, u32[]{:S(2)}) async-start(f32[128,6,2,128]{3,2,1,0:T(2,128)} %bitcast.24), calls=%async_computation.1 | async-start | bytes 1572864 | tf_op jit(solution)/shard_map/all_to_all | solution.py:324
  70.0 3.3 %shard_map.59 = (f32[4,256,256]{2,1,0:T(8,128)}, f32[16,128]{1,0:T(8,128)}) custom-call(f32[6272,128]{1,0:T(8,128)S(1)} %bitcast.20), custom_call_target="tpu_custom_call" | custom-call | flops 400000000 | bytes 8000000 | tf_op jit(solution)/shard_map/pallas_call | solution.py:39
  73.3 0.0 copy-start
  73.3 0.0 copy-start.1
  73.3 13.0 %all-to-all-done.1 = f32[128,6,2,128]{3,2,1,0:T(2,128)} async-done(((f32[128,6,2,128]{3,2,1,0:T(2,128)}), f32[128,6,2,128]{3,2,1,0:T(2,128)}, u32[]{:S(2)}, u32[]{:S(2)}) %all-to-all-start.1) | async-done | bytes 786464 | tf_op jit(solution)/shard_map/all_to_all | solution.py:324
  86.3 4.9 %shard_map.60 = (f32[256,256]{1,0:T(8,128)}, f32[1536,128]{1,0:T(8,128)}) custom-call(f32[1536,128]{1,0:T(8,128)} %bitcast.6.arr, s32[2,1,256]{2,1,0:T(1,128)} %bitcast.31, bf16[2,4,16,16,256]{4,3,2,1,0:T(8,128)(2,1)} %w_hbm.3, f32[2,256,256]{2,1,0:T(8,128)} %bitcast.27, f32[4,256,256]{2,1,0:T(8,128)} %get-tuple-element.21.d_hbm), custom_call_target="tpu_custom_call" | custom-call | flops 400000000 | bytes 8000000 | tf_op jit(solution)/shard_map/pallas_call | solution.py:39
  91.2 4.3 %all-to-all-start.2 = ((f32[128,6,2,128]{3,2,1,0:T(2,128)}), f32[128,6,2,128]{3,2,1,0:T(2,128)S(1)}, u32[]{:S(2)}, u32[]{:S(2)}) async-start(f32[128,6,2,128]{3,2,1,0:T(2,128)} %bitcast.28), calls=%async_computation.2 | async-start | bytes 1572864 | tf_op jit(solution)/shard_map/all_to_all | solution.py:324
  95.5 0.0 copy-done
  95.5 0.0 copy-done.1
  95.5 2.1 %fusion.1 = f32[3,16,16,256]{3,2,1,0:T(8,128)} fusion(f32[3,16,16,256]{3,2,1,0:T(8,128)S(1)} %copy-done.1, f32[2,3,16,16,256]{4,3,2,1,0:T(8,128)S(1)} %copy-done, f32[16,16,256]{2,1,0:T(8,128)} %bitcast.29), kind=kLoop, calls=%fused_computation.2 | loop fusion | flops 589824 | bytes 2621440 | tf_op jit(solution)/shard_map/sub | solution.py:433
  97.5 14.6 %all-to-all-done.2 = f32[128,6,2,128]{3,2,1,0:T(2,128)S(1)} async-done(((f32[128,6,2,128]{3,2,1,0:T(2,128)}), f32[128,6,2,128]{3,2,1,0:T(2,128)S(1)}, u32[]{:S(2)}, u32[]{:S(2)}) %all-to-all-start.2) | async-done | bytes 786464 | tf_op jit(solution)/shard_map/all_to_all | solution.py:324
  112.2 2.3 %shard_map.61 = f32[3,256,256]{2,1,0:T(8,128)} custom-call(f32[1536,128]{1,0:T(8,128)S(1)} %bitcast.21, f32[16,128]{1,0:T(8,128)} %get-tuple-element.23.wt_hbm, f32[3,256,256]{2,1,0:T(8,128)} %bitcast.25, f32[2,3,256,256]{3,2,1,0:T(8,128)} %bitcast.23), custom_call_target="tpu_custom_call" | custom-call | flops 200000000 | bytes 4000000 | tf_op jit(solution)/shard_map/pallas_call | solution.py:39
Async XLA Ops:
  2.6 18.5 %collective-permute-start = (f32[5,4,16,256]{3,2,1,0:T(8,128)}, f32[5,4,16,256]{3,2,1,0:T(8,128)}, u32[]{:S(2)}, u32[]{:S(2)}) collective-permute-start(f32[5,4,16,256]{3,2,1,0:T(8,128)} %get-tuple-element.16), channel_id=1, source_target_pairs={{0,16},{16,32},{32,48},{48,64},{64,80},{80,96},{96,112},{112,0},{1... | collective-permute-start | bytes 983048 | tf_op jit(solution)/shard_map/ppermute | solution.py:331
  5.6 15.5 %collective-permute-start.1 = (f32[5,4,16,256]{3,2,1,0:T(8,128)}, f32[5,4,16,256]{3,2,1,0:T(8,128)}, u32[]{:S(2)}, u32[]{:S(2)}) collective-permute-start(f32[5,4,16,256]{3,2,1,0:T(8,128)} %get-tuple-element.17), channel_id=1, source_target_pairs={{16,0},{32,16},{48,32},{64,48},{80,64},{96,80},{112,96},{0,112},{1... | collective-permute-start | bytes 983048 | tf_op jit(solution)/shard_map/ppermute | solution.py:331
  5.6 15.5 %collective-permute-start.2 = (f32[5,16,4,256]{3,2,1,0:T(4,128)}, f32[5,16,4,256]{3,2,1,0:T(4,128)}, u32[]{:S(2)}, u32[]{:S(2)}) collective-permute-start(f32[5,16,4,256]{3,2,1,0:T(4,128)} %get-tuple-element.18), channel_id=1, source_target_pairs={{0,1},{1,2},{2,3},{3,4},{4,5},{5,6},{6,7},{7,8},{8,9},{9,10},{10,1... | collective-permute-start | bytes 983048 | tf_op jit(solution)/shard_map/ppermute | solution.py:331
  6.8 14.3 %collective-permute-start.3 = (f32[5,16,4,256]{3,2,1,0:T(4,128)S(1)}, f32[5,16,4,256]{3,2,1,0:T(4,128)}, u32[]{:S(2)}, u32[]{:S(2)}) collective-permute-start(f32[5,16,4,256]{3,2,1,0:T(4,128)S(1)} %get-tuple-element.19), channel_id=1, source_target_pairs={{1,0},{2,1},{3,2},{4,3},{5,4},{6,5},{7,6},{8,7},{9,8},{10,9},{11,1... | collective-permute-start | bytes 983048 | tf_op jit(solution)/shard_map/ppermute | solution.py:331
  13.7 48.9 %all-to-all-start = ((f32[128,49,1,128]{3,2,1,0:T(1,128)}), f32[128,49,1,128]{3,2,1,0:T(1,128)S(1)}, u32[]{:S(2)}, u32[]{:S(2)}) async-start(f32[128,49,1,128]{3,2,1,0:T(1,128)} %bitcast.22), calls=%async_computation | async-start | bytes 6422528 | tf_op jit(solution)/shard_map/all_to_all | solution.py:324
  64.8 21.5 %all-to-all-start.1 = ((f32[128,6,2,128]{3,2,1,0:T(2,128)}), f32[128,6,2,128]{3,2,1,0:T(2,128)}, u32[]{:S(2)}, u32[]{:S(2)}) async-start(f32[128,6,2,128]{3,2,1,0:T(2,128)} %bitcast.24), calls=%async_computation.1 | async-start | bytes 1572864 | tf_op jit(solution)/shard_map/all_to_all | solution.py:324
  73.3 22.1 %copy-start = (f32[2,3,16,16,256]{4,3,2,1,0:T(8,128)S(1)}, f32[2,3,16,16,256]{4,3,2,1,0:T(8,128)}, u32[]{:S(2)}) copy-start(f32[2,3,16,16,256]{4,3,2,1,0:T(8,128)} %get-tuple-element.26) | copy-start | bytes 4718596
  73.3 22.1 %copy-start.1 = (f32[3,16,16,256]{3,2,1,0:T(8,128)S(1)}, f32[3,16,16,256]{3,2,1,0:T(8,128)}, u32[]{:S(2)}) copy-start(f32[3,16,16,256]{3,2,1,0:T(8,128)} %get-tuple-element.24) | copy-start | bytes 2359300
  91.2 21.0 %all-to-all-start.2 = ((f32[128,6,2,128]{3,2,1,0:T(2,128)}), f32[128,6,2,128]{3,2,1,0:T(2,128)S(1)}, u32[]{:S(2)}, u32[]{:S(2)}) async-start(f32[128,6,2,128]{3,2,1,0:T(2,128)} %bitcast.28), calls=%async_computation.2 | async-start | bytes 1572864 | tf_op jit(solution)/shard_map/all_to_all | solution.py:324

commit v6 on v5

--- a/solution.py
+++ b/solution.py
@@ -100,13 +100,27 @@
     return copies
 
 
+def under_way(tile):
+    @pl.loop(0, 2)
+    def touch(i):
+        tile[pl.ds(i * 8, 8), :] = jnp.zeros((8, 128), F32)
+
+
 def wait_all(copies):
     for copy in copies:
         copy.wait()
 
 
-def request_kernel(own_hbm, src_hbm, w_hbm, out_hbm, own, src, w, out, sems):
-    copies = start_all(((own_hbm, own), (src_hbm, src), (w_hbm.at[1], w)), sems)
+def request_kernel(
+    own_hbm, src_hbm, w_hbm, st_hbm, ve_hbm, out_hbm, xlo, xhi, ylo, yhi, own, src, w, out, edges, tile, sems
+):
+    pairs = [(own_hbm, own), (src_hbm, src), (w_hbm.at[1], w)]
+    for x_out, y_out, first, y_first in ((xlo, 0, 0, 0), (xhi, 1, 12, 8)):
+        for source, place in ((st_hbm, pl.ds(0, 2)), (ve_hbm, pl.ds(2, 3))):
+            pairs.append((source.at[:, pl.ds(first, 4)], x_out.at[place]))
+            pairs.append((source.at[:, :, pl.ds(y_first, 8)], edges.at[y_out, place]))
+    copies = start_all(pairs, sems)
+    under_way(tile)
     wait_all(copies[:2])
     lane = iota((DEV, 128), 1)
     wanted = jnp.zeros((DEV, 128), F32)
@@ -130,7 +144,10 @@
                         s * PART : (s + 1) * PART, half * 128 : half * 128 + 128
                     ]
         block = pl.ds(first * A_ROWS, PART * A_ROWS)
-        sent += start_all(((out.at[block], out_hbm.at[block]),), sems, 3 + i)
+        sent += start_all(((out.at[block], out_hbm.at[block]),), sems, 11 + i)
+    wait_all(copies[3:])
+    ylo[...] = edges[0, :, :, 0:4]
+    yhi[...] = edges[1, :, :, 4:8]
     wait_all(sent)
 
 
@@ -163,18 +180,9 @@
 ROWS = 4
 
 
-def faces_kernel(st_hbm, ve_hbm, xlo, xhi, ylo, yhi, edges, sems):
-    pairs = []
-    for out, y_out, first, y_first in ((xlo, 0, 0, 0), (xhi, 1, 12, 8)):
-        for source, place in ((st_hbm, pl.ds(0, 2)), (ve_hbm, pl.ds(2, 3))):
-            pairs.append((source.at[:, pl.ds(first, 4)], out.at[place]))
-            pairs.append((source.at[:, :, pl.ds(y_first, 8)], edges.at[y_out, place]))
-    wait_all(start_all(pairs, sems))
-    ylo[...] = edges[0, :, :, 0:4]
-    yhi[...] = edges[1, :, :, 4:8]
-
-
-def stencil_kernel(st_hbm, ve_hbm, xlo, xhi, ylo, yhi, g_hbm, b_hbm, h_hbm, xpad, ypad, ylo_scr, yhi_scr, g, b, h, sems):
+def stencil_kernel(
+    st_hbm, ve_hbm, xlo, xhi, ylo, yhi, g_hbm, b_hbm, h_hbm, first_parts, xpad, ypad, ylo_scr, yhi_scr, g, b, h, sems
+):
     sources = [st_hbm.at[j] for j in range(2)] + [ve_hbm.at[c] for c in range(3)]
     fill(sources, (xlo, xhi, ylo, yhi), xpad, ypad, ylo_scr, yhi_scr, sems)
     sent = []
@@ -191,7 +199,10 @@
                 total = term if total is None else total + term
             b[j, here] = -0.5 * total
 
-        sent += start_all(((b.at[j], b_hbm.at[j]), (g.at[j], g_hbm.at[j])), sems, len(sent))
+        sent += start_all(((g.at[j], g_hbm.at[j]),), sems, len(sent))
+    for p, part in enumerate(split(b[0].reshape(COLS, NZ))):
+        first_parts[p] = part
+    sent += start_all(((b.at[1], b_hbm),), sems, len(sent))
 
     @pl.loop(0, 16, step=ROWS)
     def curve_rows(x):
@@ -204,23 +215,20 @@
     wait_all(sent)
 
 
-def supply_kernel(asked, b_hbm, out_hbm, b, out, sems):
-    copies = start_all(((b_hbm.at[0], b),), sems)
-    wanted = asked[pl.ds(W_ROWS, DEV, stride=A_ROWS), :]
+def supply_kernel(asked_hbm, parts, out_hbm, asked, out, sems):
+    count = DEV // 8
+    groups = [pl.ds(first, count) for first in range(0, DEV, count)]
+    wait_all(start_all([(asked_hbm.at[here, W_ROWS], asked.at[here]) for here in groups], sems))
+    wanted = asked[:, 0, :]
     place = iota((PART, COLS), 1).astype(F32)
-    onehots = [
-        jnp.concatenate(
+    sent = []
+    for i, first in enumerate(range(0, DEV, PART)):
+        onehot = jnp.concatenate(
             [ones(wanted[first : first + PART, s : s + 1] == place) for s in range(CAP)], axis=0
         )
-        for first in range(0, DEV, PART)
-    ]
-    wait_all(copies)
-    parts = split(b[...])
-    sent = []
-    for i, first in enumerate(range(0, DEV, PART)):
-        put_slots(out, first * V_ROWS, select(onehots[i], parts), PART)
+        put_slots(out, first * V_ROWS, select(onehot, [parts[p] for p in range(2)]), PART)
         here = pl.ds(first * V_ROWS, PART * V_ROWS)
-        sent += start_all(((out.at[here], out_hbm.at[here]),), sems, 1 + i)
+        sent += start_all(((out.at[here], out_hbm.at[here]),), sems, i)
     wait_all(sent)
 
 
@@ -231,11 +239,12 @@
     )
 
 
-def normal_kernel(asked, *refs):
-    d_hbm, wt_hbm, w, d, wt, sems = refs[-6:]
+def normal_kernel(asked_hbm, own_hbm, w_hbm, b_hbm, d, taken, w0, b, placed_hbm, wt_hbm, asked, w, own, wt, placed, sems):
+    copies = start_all(((own_hbm.at[0], own), (w_hbm.at[0], w0), (b_hbm, b)), sems)
+    wait_all(start_all(((asked_hbm, asked),), sems, 3))
     wanted_t = asked[pl.ds(W_ROWS, DEV, stride=A_ROWS), :].T
     wt[...] = wanted_t[:16]
-    sent = start_all(((wt, wt_hbm),), sems)
+    sent = start_all(((wt, wt_hbm),), sems, 3)
     onehot_t = gathered_rows(wanted_t, 8)
     for k in range(4):
         for s in range(CAP):
@@ -254,8 +263,15 @@
                 part = pltpu.roll(part, (k - 1) % NZ, 1)
             total = part if total is None else total + part
         d[m] = total
-        sent += start_all(((d.at[m], d_hbm.at[m]),), sems, 1 + m)
-    wait_all(sent)
+    wait_all(copies)
+    owner_row = own[...]
+    for s, mask in enumerate(masks_by_column(owner_row)):
+        taken[:, s * DEV : (s + 1) * DEV] = ones(mask)
+    for s, mask in enumerate(masks_by_owner(owner_row, 0, DEV)):
+        for i in range(DEV // PART):
+            row = i * CAP * PART + s * PART
+            placed[row : row + PART] = ones(mask[i * PART : (i + 1) * PART])
+    wait_all(sent + start_all(((placed, placed_hbm),), sems, 4))
 
 
 def read_slots(ref):
@@ -270,16 +286,11 @@
     )
 
 
-def middle_kernel(arr, own_hbm, w_hbm, b_hbm, d_hbm, *refs):
-    lam_hbm, out_hbm, own, w, b, d, lam_scr, out, parts, sems = refs[-10:]
-    copies = start_all(((own_hbm.at[0], own), (w_hbm.at[0], w), (b_hbm.at[1], b), (d_hbm, d)), sems)
-    copies[0].wait()
-    owner_row = own[...]
-    taken = jnp.concatenate([ones(m) for m in masks_by_column(owner_row)], axis=1)
-    masks = masks_by_owner(owner_row, 0, DEV)
-    mine_all = select(taken, split(read_slots(arr)))
-    wait_all(copies[1:])
-    rows = 64
+def middle_kernel(arr, d, taken, w, b, placed_hbm, lam_out, out_hbm, placed, out, parts, tile, sems):
+    copies = start_all(((placed_hbm, placed),), sems)
+    under_way(tile)
+    mine_all = select(taken[...], split(read_slots(arr)))
+    rows = 128
     for start in range(0, COLS, rows):
         here = slice(start, start + rows)
         mine = mine_all[here]
@@ -292,27 +303,33 @@
         lam = d[0, here] * field
         for m in range(1, 4):
             lam += d[m, here] * pltpu.roll(field, NZ - m, 1) + pltpu.roll(d[m, here] * field, m, 1)
-        lam_scr[here] = lam
+        lam_out[here] = lam
         spread = weights[1] * lam
         for k in (0, 2, 3):
             spread += pltpu.roll(weights[k] * lam, (k - 1) % NZ, 1)
         for i, part in enumerate(split(spread)):
             parts[i, here] = part
-    sent = start_all(((lam_scr, lam_hbm),), sems)
+    wait_all(copies)
+    sent = []
     for i, first in enumerate(range(0, DEV, PART)):
-        onehot = jnp.concatenate([ones(m[first : first + PART]) for m in masks], axis=0)
+        onehot = placed[i * CAP * PART : (i + 1) * CAP * PART]
         put_slots(out, first * V_ROWS, select(onehot, [parts[p] for p in range(2)]), PART)
         here = pl.ds(first * V_ROWS, PART * V_ROWS)
-        sent += start_all(((out.at[here], out_hbm.at[here]),), sems, 1 + i)
+        sent += start_all(((out.at[here], out_hbm.at[here]),), sems, i)
     wait_all(sent)
 
 
-def final_kernel(arr, wt_hbm, h_hbm, g_hbm, out_hbm, wt, h, g, out, sems):
-    copies = start_all(((wt_hbm, wt), (h_hbm, h), (g_hbm.at[0], g)), sems)
+def blend_kernel(lam, wt_hbm, h_hbm, g_hbm, h, g, onehot, wt, g1, sems):
+    copies = start_all(((wt_hbm, wt), (h_hbm, h), (g_hbm.at[0], g), (g_hbm.at[1], g1)), sems)
     copies[0].wait()
-    onehot_t = gathered_rows(wt[...], 0)
-    lam = select(onehot_t, split(read_slots(arr)))
+    onehot[...] = gathered_rows(wt[...], 0)
     wait_all(copies[1:])
+    for c in range(3):
+        h[c] = h[c] - 0.5 * (lam[...] * g1[c])
+
+
+def final_kernel(arr, onehot, h, g, out_hbm, out, sems):
+    lam = select(onehot[...], split(read_slots(arr)))
     sent = []
     for c in range(3):
         out[c] = h[c] - 0.5 * (lam * g[c])
@@ -341,41 +358,34 @@
     sems = lambda count: pltpu.SemaphoreType.DMA((count,))
     per_field = lambda count: struct(count, 16, 16, NZ)
 
-    request = call(
+    edge_x, edge_y = pltpu.VMEM((5, 4, 16, NZ), F32), pltpu.VMEM((5, 16, 4, NZ), F32)
+    request, first_x, last_x, first_y, last_y = call(
         request_kernel,
-        struct(DEV * A_ROWS, 128),
+        (struct(DEV * A_ROWS, 128), edge_x, edge_x, edge_y, edge_y),
         16,
         3,
-        in_specs=[hbm] * 3,
-        out_specs=hbm,
+        in_specs=[hbm] * 5,
+        out_specs=(hbm,) + (near,) * 4,
         scratch_shapes=[
             pltpu.VMEM((2, 1, COLS), jnp.int32),
             pltpu.VMEM((2, 1, COLS), jnp.int32),
             pltpu.VMEM((4, 16, 16, NZ), BF16),
             scratch(DEV * A_ROWS, 128),
-            sems(7),
+            scratch(2, 5, 16, 8, NZ),
+            scratch(16, 128),
+            sems(15),
         ],
-    )(owner_row, source_row, weights)
-    asked = exchange(request.reshape(DEV, A_ROWS, 1, 128)).reshape(DEV * A_ROWS, 128)
-
-    edge = pltpu.VMEM((5, 4, 16, NZ), F32), pltpu.VMEM((5, 16, 4, NZ), F32)
-    first_x, last_x, first_y, last_y = call(
-        faces_kernel,
-        (edge[0], edge[0], edge[1], edge[1]),
-        10,
-        1,
-        in_specs=[hbm] * 2,
-        out_specs=(near,) * 4,
-        scratch_shapes=[scratch(2, 5, 16, 8, NZ), sems(8)],
-    )(state_path, velocity)
+    )(owner_row, source_row, weights, state_path, velocity)
+    asked = exchange(request.reshape(DEV, A_ROWS, 1, 128))
+
     halos = neighbours(first_x, last_x, "gx") + neighbours(first_y, last_y, "gy")
-    slopes, before, hess = call(
+    slopes, before, hess, before_parts = call(
         stencil_kernel,
-        (struct(2, 3, 16, 16, NZ), struct(2, 16, 16, NZ), per_field(3)),
+        (struct(2, 3, 16, 16, NZ), struct(16, 16, NZ), per_field(3), pltpu.VMEM((2, COLS, NZ), BF16)),
         24,
         1000,
         in_specs=[hbm] * 6,
-        out_specs=(hbm,) * 3,
+        out_specs=(hbm,) * 3 + (near,),
         scratch_shapes=[
             scratch(5, 24, 16, NZ),
             scratch(5, 16, 32, NZ),
@@ -387,65 +397,77 @@
             sems(14),
         ],
     )(state_path, velocity, *halos)
-    before = before.reshape(2, COLS, NZ)
 
     supply = call(
         supply_kernel,
         struct(DEV * V_ROWS, 128),
         8,
         2,
-        in_specs=[near, hbm],
+        in_specs=[hbm, near],
         out_specs=hbm,
-        scratch_shapes=[scratch(COLS, NZ), scratch(DEV * V_ROWS, 128), sems(5)],
-    )(asked, before)
+        scratch_shapes=[scratch(DEV, 1, 128), scratch(DEV * V_ROWS, 128), sems(8)],
+    )(asked, before_parts)
     arrived = exchange(supply.reshape(DEV, CAP, 2, 128)).reshape(DEV * V_ROWS, 128)
 
-    normal, wanted_t = call(
+    normal, taken, weight0, before1, placed, wanted_t = call(
         normal_kernel,
-        (struct(4, COLS, NZ), struct(16, 128)),
+        (
+            scratch(4, COLS, NZ),
+            pltpu.VMEM((COLS, CAP * DEV), BF16),
+            pltpu.VMEM((4, 16, 16, NZ), BF16),
+            scratch(COLS, NZ),
+            pltpu.HBM((CAP * DEV, COLS), BF16),
+            struct(16, 128),
+        ),
         20,
         4,
-        in_specs=[near],
-        out_specs=(hbm, hbm),
-        scratch_shapes=[scratch(4, CAP * DEV, NZ), scratch(4, COLS, NZ), scratch(16, 128), sems(5)],
-    )(asked)
+        in_specs=[hbm] * 4,
+        out_specs=(near,) * 4 + (hbm,) * 2,
+        scratch_shapes=[
+            scratch(DEV * A_ROWS, 128),
+            scratch(4, CAP * DEV, NZ),
+            pltpu.VMEM((1, COLS), jnp.int32),
+            scratch(16, 128),
+            pltpu.VMEM((CAP * DEV, COLS), BF16),
+            sems(5),
+        ],
+    )(asked.reshape(DEV * A_ROWS, 128), owner_row, weights, before.reshape(COLS, NZ))
 
     lam, push = call(
         middle_kernel,
-        (struct(COLS, NZ), struct(DEV * V_ROWS, 128)),
-        14,
+        (scratch(COLS, NZ), struct(DEV * V_ROWS, 128)),
+        8,
         4,
-        in_specs=[near] + [hbm] * 4,
-        out_specs=(hbm, hbm),
+        in_specs=[near] * 5 + [hbm],
+        out_specs=(near, hbm),
         scratch_shapes=[
-            pltpu.VMEM((1, COLS), jnp.int32),
-            pltpu.VMEM((4, 16, 16, NZ), BF16),
-            scratch(COLS, NZ),
-            scratch(4, COLS, NZ),
-            scratch(COLS, NZ),
+            pltpu.VMEM((CAP * DEV, COLS), BF16),
             scratch(DEV * V_ROWS, 128),
             pltpu.VMEM((2, COLS, NZ), BF16),
-            sems(5),
+            scratch(16, 128),
+            sems(4),
         ],
-    )(arrived, owner_row, weights, before, normal)
+    )(arrived, normal, taken, weight0, before1, placed)
     returned = exchange(push.reshape(DEV, CAP, 2, 128)).reshape(DEV * V_ROWS, 128)
 
-    hess = hess - 0.5 * (lam.reshape(1, 16, 16, NZ) * slopes[1])
+    hess, slope0, onehot = call(
+        blend_kernel,
+        (scratch(3, COLS, NZ), scratch(3, COLS, NZ), pltpu.VMEM((COLS, CAP * DEV), BF16)),
+        8,
+        3,
+        in_specs=[near] + [hbm] * 3,
+        out_specs=(near,) * 3,
+        scratch_shapes=[scratch(16, 128), scratch(3, COLS, NZ), sems(4)],
+    )(lam, wanted_t, hess.reshape(3, COLS, NZ), slopes.reshape(2, 3, COLS, NZ))
     out = call(
         final_kernel,
         struct(3, COLS, NZ),
-        14,
+        8,
         2,
-        in_specs=[near] + [hbm] * 3,
+        in_specs=[near] * 4,
         out_specs=hbm,
-        scratch_shapes=[
-            scratch(16, 128),
-            scratch(3, COLS, NZ),
-            scratch(3, COLS, NZ),
-            scratch(3, COLS, NZ),
-            sems(3),
-        ],
-    )(returned, wanted_t, hess.reshape(3, COLS, NZ), slopes.reshape(2, 3, COLS, NZ))
+        scratch_shapes=[scratch(3, COLS, NZ), sems(3)],
+    )(returned, onehot, hess, slope0)
     return out.reshape(3, 16, 16, NZ)
 
 

time: 115 us -> 110 us (0.957)
  waiting for transfers between devices: 61.3 us -> 57.2 us
  other arithmetic: 2.05 us -> 0 us
  local copies, waits for them, and re-layouts: 0.01 us -> 1.7 us
    all_to_all x3, waiting for transfers between devices: 61.3 us -> 57.2 us  [exchange(): return lax.all_to_all(value, AXES, split_axis=0, concat_axis=0, tiled=True)]
    sub x1 -> x0, other arithmetic: 2.05 us -> none  [per_device(): hess = hess - 0.5 * (lam.reshape(1, 16, 16, NZ) * slopes[1])]
    unnamed x4 -> x8, local copies, waits for them, and re-layouts: 0.01 us -> 1.7 us
  transfers between devices with their start and end apart: 7 -> 7, of which waited for: 3 -> 3; matrix products, arithmetic and copies ran while one was open for 2% -> 0% of each run, Pallas kernels for 12% -> 14%
where the time goes in v6:
time: 110 us; the launch traced here: 109 us
  waiting for transfers between devices  57.2 us (52%)
  Pallas kernels  25.5 us (23%)
  starting transfers between devices  24.8 us (23%)
  local copies, waits for them, and re-layouts  1.7 us (2%)
    all_to_all x3, waiting for transfers between devices, exchange(): return lax.all_to_all(value, AXES, split_axis=0, concat_axis=0, tiled=True)  57.2 us
    pallas_call x7, Pallas kernels, placed(): run(*(pltpu.with_memory_space_constraint(x, pltpu.HBM) if spec.memory_spa...  25.5 us
    all_to_all x3, starting transfers between devices, exchange(): return lax.all_to_all(value, AXES, split_axis=0, concat_axis=0, tiled=True)  16.8 us
    ppermute x4, starting transfers between devices, neighbours(): return (lax.ppermute(last, axis, up), lax.ppermute(first, axis, down))  7.97 us
  transfers between devices with their start and end apart: 7, of which 3 were waited for; matrix products, arithmetic and copies ran while one was open for 0% of the time, Pallas kernels for 14%

profile of v6, /device:TPU:1, one launch (start us, length us, event | category | flops | bytes accessed | tf_op | source)
XLA Modules:
  0.0 109.4 jit_solution(5807305732798826259)
XLA Ops:
  0.0 3.3 %shard_map.55 = (f32[6272,128]{1,0:T(8,128)}, f32[5,4,16,256]{3,2,1,0:T(8,128)S(1)}, f32[5,4,16,256]{3,2,1,0:T(8,128)S(1)}, f32[5,16,4,256]{3,2,1,0:T(4,128)S(1)}, f32[5,16,4,256]{3,2,1,0:T(4,128)S(1)}) custom-call(s32[2,1,256]{2,1,0:T(1,128)} %bitcast.20, s32[2,1,256]{2,1,0:T(1,128)} %bitcast.22, bf16[2,4,16,16,256]{4,3,2,1,0:T(8,128)(2,1)} %w_hbm.3, ...), custom_call_target="tpu_custom_call" | custom-call | flops 300000000 | bytes 6000000 | tf_op jit(solution)/shard_map/pallas_call | solution.py:39
  3.3 3.0 %collective-permute-start = (f32[5,4,16,256]{3,2,1,0:T(8,128)S(1)}, f32[5,4,16,256]{3,2,1,0:T(8,128)S(1)}, u32[]{:S(2)}, u32[]{:S(2)}) collective-permute-start(f32[5,4,16,256]{3,2,1,0:T(8,128)S(1)} %get-tuple-element.26), channel_id=1, source_target_pairs={{0,16},{16,32},{32,48},{48,64},{64,80},{80,96},{96,112},{112,0},{1... | collective-permute-start | bytes 983048 | tf_op jit(solution)/shard_map/ppermute | solution.py:348
  6.3 0.0 collective-permute-start.1
  6.4 1.2 %collective-permute-start.2 = (f32[5,16,4,256]{3,2,1,0:T(4,128)S(1)}, f32[5,16,4,256]{3,2,1,0:T(4,128)S(1)}, u32[]{:S(2)}, u32[]{:S(2)}) collective-permute-start(f32[5,16,4,256]{3,2,1,0:T(4,128)S(1)} %get-tuple-element.28), channel_id=1, source_target_pairs={{0,1},{1,2},{2,3},{3,4},{4,5},{5,6},{6,7},{7,8},{8,9},{9,10},{10,1... | collective-permute-start | bytes 983048 | tf_op jit(solution)/shard_map/ppermute | solution.py:348
  7.6 3.7 %collective-permute-start.3 = (f32[5,16,4,256]{3,2,1,0:T(4,128)S(1)}, f32[5,16,4,256]{3,2,1,0:T(4,128)S(1)}, u32[]{:S(2)}, u32[]{:S(2)}) collective-permute-start(f32[5,16,4,256]{3,2,1,0:T(4,128)S(1)} %get-tuple-element.29), channel_id=1, source_target_pairs={{1,0},{2,1},{3,2},{4,3},{5,4},{6,5},{7,6},{8,7},{9,8},{10,9},{11,1... | collective-permute-start | bytes 983048 | tf_op jit(solution)/shard_map/ppermute | solution.py:348
  11.3 7.7 %all-to-all-start = ((f32[128,49,1,128]{3,2,1,0:T(1,128)}), f32[128,49,1,128]{3,2,1,0:T(1,128)}, u32[]{:S(2)}, u32[]{:S(2)}) async-start(f32[128,49,1,128]{3,2,1,0:T(1,128)} %bitcast.14), calls=%async_computation | async-start | bytes 6422528 | tf_op jit(solution)/shard_map/all_to_all | solution.py:341
  19.0 0.0 collective-permute-done.xlo
  19.0 0.0 copy-start
  19.0 0.0 collective-permute-done.1.xhi
  19.0 0.0 copy-start.1
  19.0 0.0 collective-permute-done.2.ylo
  19.1 0.0 copy-start.2
  19.1 0.0 collective-permute-done.3.yhi
  19.1 0.7 copy-done
  19.8 0.2 copy-done.1
  19.9 0.1 copy-done.2
  20.0 0.0 copy-start.3
  20.0 0.7 copy-done.3
  20.8 7.9 %shard_map.56 = (f32[2,3,16,16,256]{4,3,2,1,0:T(8,128)}, f32[16,16,256]{2,1,0:T(8,128)}, f32[3,16,16,256]{3,2,1,0:T(8,128)}, bf16[2,256,256]{2,1,0:T(8,128)(2,1)S(1)}) custom-call(f32[2,16,16,256]{3,2,1,0:T(8,128)} %st_hbm.3, f32[3,16,16,256]{3,2,1,0:T(8,128)} %ve_hbm.3, f32[5,4,16,256]{3,2,1,0:T(8,128)} %copy-done, f32[5,4,16,256]{3,2,1,0:T(8,128)} %copy-done.1, ...), custom_call_target="tpu_custom_call" | custom-call | flops 99999997952 | bytes 2000000000 | tf_op jit(solution)/shard_map/pallas_call | solution.py:39
  28.7 31.6 %all-to-all-done.asked_hbm = f32[128,49,1,128]{3,2,1,0:T(1,128)} async-done(((f32[128,49,1,128]{3,2,1,0:T(1,128)}), f32[128,49,1,128]{3,2,1,0:T(1,128)}, u32[]{:S(2)}, u32[]{:S(2)}) %all-to-all-start) | async-done | bytes 3211296 | tf_op jit(solution)/shard_map/all_to_all | solution.py:341
  60.3 2.7 %shard_map.57 = f32[1536,128]{1,0:T(8,128)} custom-call(f32[128,49,1,128]{3,2,1,0:T(1,128)} %all-to-all-done.asked_hbm, bf16[2,256,256]{2,1,0:T(8,128)(2,1)S(1)} %get-tuple-element.30.parts), custom_call_target="tpu_custom_call" | custom-call | flops 200000000 | bytes 4000000 | tf_op jit(solution)/shard_map/pallas_call | solution.py:39
  63.0 4.8 %all-to-all-start.1 = ((f32[128,6,2,128]{3,2,1,0:T(2,128)}), f32[128,6,2,128]{3,2,1,0:T(2,128)S(1)}, u32[]{:S(2)}, u32[]{:S(2)}) async-start(f32[128,6,2,128]{3,2,1,0:T(2,128)} %bitcast.15), calls=%async_computation.1 | async-start | bytes 1572864 | tf_op jit(solution)/shard_map/all_to_all | solution.py:341
  67.8 5.9 %shard_map.58 = (f32[4,256,256]{2,1,0:T(8,128)S(1)}, bf16[256,768]{1,0:T(8,128)(2,1)S(1)}, bf16[4,16,16,256]{3,2,1,0:T(8,128)(2,1)S(1)}, f32[256,256]{1,0:T(8,12...) custom-call(f32[6272,128]{1,0:T(8,128)} %bitcast.5.asked_hbm, s32[2,1,256]{2,1,0:T(1,128)} %bitcast.21, ...), custom_call_target="tpu_custom_call" | custom-call | flops 400000000 | bytes 8000000 | tf_op jit(solution)/shard_map/pallas_call | solution.py:39
  73.7 10.7 %all-to-all-done.1 = f32[128,6,2,128]{3,2,1,0:T(2,128)S(1)} async-done(((f32[128,6,2,128]{3,2,1,0:T(2,128)}), f32[128,6,2,128]{3,2,1,0:T(2,128)S(1)}, u32[]{:S(2)}, u32[]{:S(2)}) %all-to-all-start.1) | async-done | bytes 786464 | tf_op jit(solution)/shard_map/all_to_all | solution.py:341
  84.4 2.7 %shard_map.59 = (f32[256,256]{1,0:T(8,128)S(1)}, f32[1536,128]{1,0:T(8,128)}) custom-call(f32[1536,128]{1,0:T(8,128)S(1)} %bitcast.13, f32[4,256,256]{2,1,0:T(8,128)S(1)} %get-tuple-element.32.d, bf16[256,768]{1,0:T(8,128)(2,1)S(1)} %get-tuple-element.33.taken, bf16[4,16,16,256]{3,2,1,0:T(8,128)(2,1)S(1)} %get-tuple-element.34.w, ...), custom_call_target="tpu_custom_call" | custom-call | flops 400000000 | bytes 8000000 | tf_op jit(solution)/shard_map/pallas_call | solution.py:39
  87.1 4.3 %all-to-all-start.2 = ((f32[128,6,2,128]{3,2,1,0:T(2,128)}), f32[128,6,2,128]{3,2,1,0:T(2,128)S(1)}, u32[]{:S(2)}, u32[]{:S(2)}) async-start(f32[128,6,2,128]{3,2,1,0:T(2,128)} %bitcast.17), calls=%async_computation.2 | async-start | bytes 1572864 | tf_op jit(solution)/shard_map/all_to_all | solution.py:341
  91.3 1.8 %shard_map.60 = (f32[3,256,256]{2,1,0:T(8,128)S(1)}, f32[3,256,256]{2,1,0:T(8,128)S(1)}, bf16[256,768]{1,0:T(8,128)(2,1)S(1)}) custom-call(f32[256,256]{1,0:T(8,128)S(1)} %get-tuple-element.38.lam, f32[16,128]{1,0:T(8,128)} %get-tuple-element.39.wt_hbm, f32[3,256,256]{2,1,0:T(8,128)} %bitcast.18, f32[2,3,256,256]{3,2,1,0:T(8,128)} %bitcast.16), custom_call_target="tpu_custom_call" | custom-call | flops 300000000 | bytes 6000000 | tf_op jit(solution)/shard_map/pallas_call | solution.py:39
  93.1 14.9 %all-to-all-done.2 = f32[128,6,2,128]{3,2,1,0:T(2,128)S(1)} async-done(((f32[128,6,2,128]{3,2,1,0:T(2,128)}), f32[128,6,2,128]{3,2,1,0:T(2,128)S(1)}, u32[]{:S(2)}, u32[]{:S(2)}) %all-to-all-start.2) | async-done | bytes 786464 | tf_op jit(solution)/shard_map/all_to_all | solution.py:341
  108.1 1.3 %shard_map.61 = f32[3,256,256]{2,1,0:T(8,128)} custom-call(f32[1536,128]{1,0:T(8,128)S(1)} %bitcast.12, bf16[256,768]{1,0:T(8,128)(2,1)S(1)} %get-tuple-element.42.onehot, f32[3,256,256]{2,1,0:T(8,128)S(1)} %get-tuple-element.43.h, f32[3,256,256]{2,1,0:T(8,128)S(1)} %get-tuple-element.44.g), custom_call_target="tpu_custom_call" | custom-call | flops 200000000 | bytes 4000000 | tf_op jit(solution)/shard_map/pallas_call | solution.py:39
Async XLA Ops:
  3.3 15.7 %collective-permute-start = (f32[5,4,16,256]{3,2,1,0:T(8,128)S(1)}, f32[5,4,16,256]{3,2,1,0:T(8,128)S(1)}, u32[]{:S(2)}, u32[]{:S(2)}) collective-permute-start(f32[5,4,16,256]{3,2,1,0:T(8,128)S(1)} %get-tuple-element.26), channel_id=1, source_target_pairs={{0,16},{16,32},{32,48},{48,64},{64,80},{80,96},{96,112},{112,0},{1... | collective-permute-start | bytes 983048 | tf_op jit(solution)/shard_map/ppermute | solution.py:348
  6.3 12.7 %collective-permute-start.1 = (f32[5,4,16,256]{3,2,1,0:T(8,128)S(1)}, f32[5,4,16,256]{3,2,1,0:T(8,128)S(1)}, u32[]{:S(2)}, u32[]{:S(2)}) collective-permute-start(f32[5,4,16,256]{3,2,1,0:T(8,128)S(1)} %get-tuple-element.27), channel_id=1, source_target_pairs={{16,0},{32,16},{48,32},{64,48},{80,64},{96,80},{112,96},{0,112},{1... | collective-permute-start | bytes 983048 | tf_op jit(solution)/shard_map/ppermute | solution.py:348
  6.4 12.7 %collective-permute-start.2 = (f32[5,16,4,256]{3,2,1,0:T(4,128)S(1)}, f32[5,16,4,256]{3,2,1,0:T(4,128)S(1)}, u32[]{:S(2)}, u32[]{:S(2)}) collective-permute-start(f32[5,16,4,256]{3,2,1,0:T(4,128)S(1)} %get-tuple-element.28), channel_id=1, source_target_pairs={{0,1},{1,2},{2,3},{3,4},{4,5},{5,6},{6,7},{7,8},{8,9},{9,10},{10,1... | collective-permute-start | bytes 983048 | tf_op jit(solution)/shard_map/ppermute | solution.py:348
  7.6 11.5 %collective-permute-start.3 = (f32[5,16,4,256]{3,2,1,0:T(4,128)S(1)}, f32[5,16,4,256]{3,2,1,0:T(4,128)S(1)}, u32[]{:S(2)}, u32[]{:S(2)}) collective-permute-start(f32[5,16,4,256]{3,2,1,0:T(4,128)S(1)} %get-tuple-element.29), channel_id=1, source_target_pairs={{1,0},{2,1},{3,2},{4,3},{5,4},{6,5},{7,6},{8,7},{9,8},{10,9},{11,1... | collective-permute-start | bytes 983048 | tf_op jit(solution)/shard_map/ppermute | solution.py:348
  11.3 49.0 %all-to-all-start = ((f32[128,49,1,128]{3,2,1,0:T(1,128)}), f32[128,49,1,128]{3,2,1,0:T(1,128)}, u32[]{:S(2)}, u32[]{:S(2)}) async-start(f32[128,49,1,128]{3,2,1,0:T(1,128)} %bitcast.14), calls=%async_computation | async-start | bytes 6422528 | tf_op jit(solution)/shard_map/all_to_all | solution.py:341
  19.0 0.7 copy-start
  19.0 0.9 copy-start.1
  19.1 1.0 copy-start.2
  20.0 0.7 copy-start.3
  63.0 21.4 %all-to-all-start.1 = ((f32[128,6,2,128]{3,2,1,0:T(2,128)}), f32[128,6,2,128]{3,2,1,0:T(2,128)S(1)}, u32[]{:S(2)}, u32[]{:S(2)}) async-start(f32[128,6,2,128]{3,2,1,0:T(2,128)} %bitcast.15), calls=%async_computation.1 | async-start | bytes 1572864 | tf_op jit(solution)/shard_map/all_to_all | solution.py:341
  87.1 21.0 %all-to-all-start.2 = ((f32[128,6,2,128]{3,2,1,0:T(2,128)}), f32[128,6,2,128]{3,2,1,0:T(2,128)S(1)}, u32[]{:S(2)}, u32[]{:S(2)}) async-start(f32[128,6,2,128]{3,2,1,0:T(2,128)} %bitcast.17), calls=%async_computation.2 | async-start | bytes 1572864 | tf_op jit(solution)/shard_map/all_to_all | solution.py:341

commit v7 on v6

--- a/solution.py
+++ b/solution.py
@@ -216,10 +216,8 @@
 
 
 def supply_kernel(asked_hbm, parts, out_hbm, asked, out, sems):
-    count = DEV // 8
-    groups = [pl.ds(first, count) for first in range(0, DEV, count)]
-    wait_all(start_all([(asked_hbm.at[here, W_ROWS], asked.at[here]) for here in groups], sems))
-    wanted = asked[:, 0, :]
+    wait_all(start_all(((asked_hbm.at[:, W_ROWS, 0], asked),), sems))
+    wanted = asked[...]
     place = iota((PART, COLS), 1).astype(F32)
     sent = []
     for i, first in enumerate(range(0, DEV, PART)):
@@ -405,7 +403,7 @@
         2,
         in_specs=[hbm, near],
         out_specs=hbm,
-        scratch_shapes=[scratch(DEV, 1, 128), scratch(DEV * V_ROWS, 128), sems(8)],
+        scratch_shapes=[scratch(DEV, 128), scratch(DEV * V_ROWS, 128), sems(4)],
     )(asked, before_parts)
     arrived = exchange(supply.reshape(DEV, CAP, 2, 128)).reshape(DEV * V_ROWS, 128)
 

time: 110 us -> 109 us (level)
  no operation moved by 1% of the time
where the time goes in v7:
time: 109 us
  waiting for transfers between devices  57.2 us (52%)
  Pallas kernels  25 us (23%)
  starting transfers between devices  24.8 us (23%)
  local copies, waits for them, and re-layouts  1.7 us (2%)
    all_to_all x3, waiting for transfers between devices, exchange(): return lax.all_to_all(value, AXES, split_axis=0, concat_axis=0, tiled=True)  57.2 us
    pallas_call x7, Pallas kernels, placed(): run(*(pltpu.with_memory_space_constraint(x, pltpu.HBM) if spec.memory_spa...  25 us
    all_to_all x3, starting transfers between devices, exchange(): return lax.all_to_all(value, AXES, split_axis=0, concat_axis=0, tiled=True)  16.8 us
    ppermute x4, starting transfers between devices, neighbours(): return (lax.ppermute(last, axis, up), lax.ppermute(first, axis, down))  7.97 us
  transfers between devices with their start and end apart: 7, of which 3 were waited for; matrix products, arithmetic and copies ran while one was open for 0% of the time, Pallas kernels for 14%

profile of v7, /device:TPU:1, one launch (start us, length us, event | category | flops | bytes accessed | tf_op | source)
XLA Modules:
  0.0 108.8 jit_solution(6827827370882696608)
XLA Ops:
  0.0 3.3 %shard_map.55 = (f32[6272,128]{1,0:T(8,128)}, f32[5,4,16,256]{3,2,1,0:T(8,128)S(1)}, f32[5,4,16,256]{3,2,1,0:T(8,128)S(1)}, f32[5,16,4,256]{3,2,1,0:T(4,128)S(1)}, f32[5,16,4,256]{3,2,1,0:T(4,128)S(1)}) custom-call(s32[2,1,256]{2,1,0:T(1,128)} %bitcast.20, s32[2,1,256]{2,1,0:T(1,128)} %bitcast.22, bf16[2,4,16,16,256]{4,3,2,1,0:T(8,128)(2,1)} %w_hbm.3, ...), custom_call_target="tpu_custom_call" | custom-call | flops 300000000 | bytes 6000000 | tf_op jit(solution)/shard_map/pallas_call | solution.py:39
  3.3 3.0 %collective-permute-start = (f32[5,4,16,256]{3,2,1,0:T(8,128)S(1)}, f32[5,4,16,256]{3,2,1,0:T(8,128)S(1)}, u32[]{:S(2)}, u32[]{:S(2)}) collective-permute-start(f32[5,4,16,256]{3,2,1,0:T(8,128)S(1)} %get-tuple-element.26), channel_id=1, source_target_pairs={{0,16},{16,32},{32,48},{48,64},{64,80},{80,96},{96,112},{112,0},{1... | collective-permute-start | bytes 983048 | tf_op jit(solution)/shard_map/ppermute | solution.py:346
  6.3 0.0 collective-permute-start.1
  6.4 1.2 %collective-permute-start.2 = (f32[5,16,4,256]{3,2,1,0:T(4,128)S(1)}, f32[5,16,4,256]{3,2,1,0:T(4,128)S(1)}, u32[]{:S(2)}, u32[]{:S(2)}) collective-permute-start(f32[5,16,4,256]{3,2,1,0:T(4,128)S(1)} %get-tuple-element.28), channel_id=1, source_target_pairs={{0,1},{1,2},{2,3},{3,4},{4,5},{5,6},{6,7},{7,8},{8,9},{9,10},{10,1... | collective-permute-start | bytes 983048 | tf_op jit(solution)/shard_map/ppermute | solution.py:346
  7.6 3.7 %collective-permute-start.3 = (f32[5,16,4,256]{3,2,1,0:T(4,128)S(1)}, f32[5,16,4,256]{3,2,1,0:T(4,128)S(1)}, u32[]{:S(2)}, u32[]{:S(2)}) collective-permute-start(f32[5,16,4,256]{3,2,1,0:T(4,128)S(1)} %get-tuple-element.29), channel_id=1, source_target_pairs={{1,0},{2,1},{3,2},{4,3},{5,4},{6,5},{7,6},{8,7},{9,8},{10,9},{11,1... | collective-permute-start | bytes 983048 | tf_op jit(solution)/shard_map/ppermute | solution.py:346
  11.3 7.7 %all-to-all-start = ((f32[128,49,1,128]{3,2,1,0:T(1,128)}), f32[128,49,1,128]{3,2,1,0:T(1,128)}, u32[]{:S(2)}, u32[]{:S(2)}) async-start(f32[128,49,1,128]{3,2,1,0:T(1,128)} %bitcast.14), calls=%async_computation | async-start | bytes 6422528 | tf_op jit(solution)/shard_map/all_to_all | solution.py:339
  19.0 0.0 collective-permute-done.xlo
  19.0 0.0 copy-start
  19.0 0.0 collective-permute-done.1.xhi
  19.0 0.0 copy-start.1
  19.0 0.0 collective-permute-done.2.ylo
  19.1 0.0 copy-start.2
  19.1 0.0 collective-permute-done.3.yhi
  19.1 0.7 copy-done
  19.8 0.2 copy-done.1
  19.9 0.1 copy-done.2
  20.0 0.0 copy-start.3
  20.0 0.7 copy-done.3
  20.8 7.9 %shard_map.56 = (f32[2,3,16,16,256]{4,3,2,1,0:T(8,128)}, f32[16,16,256]{2,1,0:T(8,128)}, f32[3,16,16,256]{3,2,1,0:T(8,128)}, bf16[2,256,256]{2,1,0:T(8,128)(2,1)S(1)}) custom-call(f32[2,16,16,256]{3,2,1,0:T(8,128)} %st_hbm.3, f32[3,16,16,256]{3,2,1,0:T(8,128)} %ve_hbm.3, f32[5,4,16,256]{3,2,1,0:T(8,128)} %copy-done, f32[5,4,16,256]{3,2,1,0:T(8,128)} %copy-done.1, ...), custom_call_target="tpu_custom_call" | custom-call | flops 99999997952 | bytes 2000000000 | tf_op jit(solution)/shard_map/pallas_call | solution.py:39
  28.7 31.6 %all-to-all-done.asked_hbm = f32[128,49,1,128]{3,2,1,0:T(1,128)} async-done(((f32[128,49,1,128]{3,2,1,0:T(1,128)}), f32[128,49,1,128]{3,2,1,0:T(1,128)}, u32[]{:S(2)}, u32[]{:S(2)}) %all-to-all-start) | async-done | bytes 3211296 | tf_op jit(solution)/shard_map/all_to_all | solution.py:339
  60.3 2.1 %shard_map.57 = f32[1536,128]{1,0:T(8,128)} custom-call(f32[128,49,1,128]{3,2,1,0:T(1,128)} %all-to-all-done.asked_hbm, bf16[2,256,256]{2,1,0:T(8,128)(2,1)S(1)} %get-tuple-element.30.parts), custom_call_target="tpu_custom_call" | custom-call | flops 200000000 | bytes 4000000 | tf_op jit(solution)/shard_map/pallas_call | solution.py:39
  62.4 4.8 %all-to-all-start.1 = ((f32[128,6,2,128]{3,2,1,0:T(2,128)}), f32[128,6,2,128]{3,2,1,0:T(2,128)S(1)}, u32[]{:S(2)}, u32[]{:S(2)}) async-start(f32[128,6,2,128]{3,2,1,0:T(2,128)} %bitcast.15), calls=%async_computation.1 | async-start | bytes 1572864 | tf_op jit(solution)/shard_map/all_to_all | solution.py:339
  67.2 5.9 %shard_map.58 = (f32[4,256,256]{2,1,0:T(8,128)S(1)}, bf16[256,768]{1,0:T(8,128)(2,1)S(1)}, bf16[4,16,16,256]{3,2,1,0:T(8,128)(2,1)S(1)}, f32[256,256]{1,0:T(8,12...) custom-call(f32[6272,128]{1,0:T(8,128)} %bitcast.5.asked_hbm, s32[2,1,256]{2,1,0:T(1,128)} %bitcast.21, ...), custom_call_target="tpu_custom_call" | custom-call | flops 400000000 | bytes 8000000 | tf_op jit(solution)/shard_map/pallas_call | solution.py:39
  73.1 10.7 %all-to-all-done.1 = f32[128,6,2,128]{3,2,1,0:T(2,128)S(1)} async-done(((f32[128,6,2,128]{3,2,1,0:T(2,128)}), f32[128,6,2,128]{3,2,1,0:T(2,128)S(1)}, u32[]{:S(2)}, u32[]{:S(2)}) %all-to-all-start.1) | async-done | bytes 786464 | tf_op jit(solution)/shard_map/all_to_all | solution.py:339
  83.8 2.7 %shard_map.59 = (f32[256,256]{1,0:T(8,128)S(1)}, f32[1536,128]{1,0:T(8,128)}) custom-call(f32[1536,128]{1,0:T(8,128)S(1)} %bitcast.13, f32[4,256,256]{2,1,0:T(8,128)S(1)} %get-tuple-element.32.d, bf16[256,768]{1,0:T(8,128)(2,1)S(1)} %get-tuple-element.33.taken, bf16[4,16,16,256]{3,2,1,0:T(8,128)(2,1)S(1)} %get-tuple-element.34.w, ...), custom_call_target="tpu_custom_call" | custom-call | flops 400000000 | bytes 8000000 | tf_op jit(solution)/shard_map/pallas_call | solution.py:39
  86.5 4.3 %all-to-all-start.2 = ((f32[128,6,2,128]{3,2,1,0:T(2,128)}), f32[128,6,2,128]{3,2,1,0:T(2,128)S(1)}, u32[]{:S(2)}, u32[]{:S(2)}) async-start(f32[128,6,2,128]{3,2,1,0:T(2,128)} %bitcast.17), calls=%async_computation.2 | async-start | bytes 1572864 | tf_op jit(solution)/shard_map/all_to_all | solution.py:339
  90.8 1.8 %shard_map.60 = (f32[3,256,256]{2,1,0:T(8,128)S(1)}, f32[3,256,256]{2,1,0:T(8,128)S(1)}, bf16[256,768]{1,0:T(8,128)(2,1)S(1)}) custom-call(f32[256,256]{1,0:T(8,128)S(1)} %get-tuple-element.38.lam, f32[16,128]{1,0:T(8,128)} %get-tuple-element.39.wt_hbm, f32[3,256,256]{2,1,0:T(8,128)} %bitcast.18, f32[2,3,256,256]{3,2,1,0:T(8,128)} %bitcast.16), custom_call_target="tpu_custom_call" | custom-call | flops 300000000 | bytes 6000000 | tf_op jit(solution)/shard_map/pallas_call | solution.py:39
  92.5 14.9 %all-to-all-done.2 = f32[128,6,2,128]{3,2,1,0:T(2,128)S(1)} async-done(((f32[128,6,2,128]{3,2,1,0:T(2,128)}), f32[128,6,2,128]{3,2,1,0:T(2,128)S(1)}, u32[]{:S(2)}, u32[]{:S(2)}) %all-to-all-start.2) | async-done | bytes 786464 | tf_op jit(solution)/shard_map/all_to_all | solution.py:339
  107.5 1.3 %shard_map.61 = f32[3,256,256]{2,1,0:T(8,128)} custom-call(f32[1536,128]{1,0:T(8,128)S(1)} %bitcast.12, bf16[256,768]{1,0:T(8,128)(2,1)S(1)} %get-tuple-element.42.onehot, f32[3,256,256]{2,1,0:T(8,128)S(1)} %get-tuple-element.43.h, f32[3,256,256]{2,1,0:T(8,128)S(1)} %get-tuple-element.44.g), custom_call_target="tpu_custom_call" | custom-call | flops 200000000 | bytes 4000000 | tf_op jit(solution)/shard_map/pallas_call | solution.py:39
Async XLA Ops:
  3.3 15.7 %collective-permute-start = (f32[5,4,16,256]{3,2,1,0:T(8,128)S(1)}, f32[5,4,16,256]{3,2,1,0:T(8,128)S(1)}, u32[]{:S(2)}, u32[]{:S(2)}) collective-permute-start(f32[5,4,16,256]{3,2,1,0:T(8,128)S(1)} %get-tuple-element.26), channel_id=1, source_target_pairs={{0,16},{16,32},{32,48},{48,64},{64,80},{80,96},{96,112},{112,0},{1... | collective-permute-start | bytes 983048 | tf_op jit(solution)/shard_map/ppermute | solution.py:346
  6.3 12.7 %collective-permute-start.1 = (f32[5,4,16,256]{3,2,1,0:T(8,128)S(1)}, f32[5,4,16,256]{3,2,1,0:T(8,128)S(1)}, u32[]{:S(2)}, u32[]{:S(2)}) collective-permute-start(f32[5,4,16,256]{3,2,1,0:T(8,128)S(1)} %get-tuple-element.27), channel_id=1, source_target_pairs={{16,0},{32,16},{48,32},{64,48},{80,64},{96,80},{112,96},{0,112},{1... | collective-permute-start | bytes 983048 | tf_op jit(solution)/shard_map/ppermute | solution.py:346
  6.4 12.7 %collective-permute-start.2 = (f32[5,16,4,256]{3,2,1,0:T(4,128)S(1)}, f32[5,16,4,256]{3,2,1,0:T(4,128)S(1)}, u32[]{:S(2)}, u32[]{:S(2)}) collective-permute-start(f32[5,16,4,256]{3,2,1,0:T(4,128)S(1)} %get-tuple-element.28), channel_id=1, source_target_pairs={{0,1},{1,2},{2,3},{3,4},{4,5},{5,6},{6,7},{7,8},{8,9},{9,10},{10,1... | collective-permute-start | bytes 983048 | tf_op jit(solution)/shard_map/ppermute | solution.py:346
  7.6 11.5 %collective-permute-start.3 = (f32[5,16,4,256]{3,2,1,0:T(4,128)S(1)}, f32[5,16,4,256]{3,2,1,0:T(4,128)S(1)}, u32[]{:S(2)}, u32[]{:S(2)}) collective-permute-start(f32[5,16,4,256]{3,2,1,0:T(4,128)S(1)} %get-tuple-element.29), channel_id=1, source_target_pairs={{1,0},{2,1},{3,2},{4,3},{5,4},{6,5},{7,6},{8,7},{9,8},{10,9},{11,1... | collective-permute-start | bytes 983048 | tf_op jit(solution)/shard_map/ppermute | solution.py:346
  11.3 49.0 %all-to-all-start = ((f32[128,49,1,128]{3,2,1,0:T(1,128)}), f32[128,49,1,128]{3,2,1,0:T(1,128)}, u32[]{:S(2)}, u32[]{:S(2)}) async-start(f32[128,49,1,128]{3,2,1,0:T(1,128)} %bitcast.14), calls=%async_computation | async-start | bytes 6422528 | tf_op jit(solution)/shard_map/all_to_all | solution.py:339
  19.0 0.7 copy-start
  19.0 0.9 copy-start.1
  19.1 1.0 copy-start.2
  20.0 0.7 copy-start.3
  62.4 21.4 %all-to-all-start.1 = ((f32[128,6,2,128]{3,2,1,0:T(2,128)}), f32[128,6,2,128]{3,2,1,0:T(2,128)S(1)}, u32[]{:S(2)}, u32[]{:S(2)}) async-start(f32[128,6,2,128]{3,2,1,0:T(2,128)} %bitcast.15), calls=%async_computation.1 | async-start | bytes 1572864 | tf_op jit(solution)/shard_map/all_to_all | solution.py:339
  86.5 21.0 %all-to-all-start.2 = ((f32[128,6,2,128]{3,2,1,0:T(2,128)}), f32[128,6,2,128]{3,2,1,0:T(2,128)S(1)}, u32[]{:S(2)}, u32[]{:S(2)}) async-start(f32[128,6,2,128]{3,2,1,0:T(2,128)} %bitcast.17), calls=%async_computation.2 | async-start | bytes 1572864 | tf_op jit(solution)/shard_map/all_to_all | solution.py:339

commit v8 on v7

--- a/solution.py
+++ b/solution.py
@@ -287,11 +287,11 @@
 def middle_kernel(arr, d, taken, w, b, placed_hbm, lam_out, out_hbm, placed, out, parts, tile, sems):
     copies = start_all(((placed_hbm, placed),), sems)
     under_way(tile)
-    mine_all = select(taken[...], split(read_slots(arr)))
+    received = split(read_slots(arr))
     rows = 128
     for start in range(0, COLS, rows):
         here = slice(start, start + rows)
-        mine = mine_all[here]
+        mine = select(taken[here], received)
         weights = [
             w[k, start // 16 : (start + rows) // 16].reshape(rows, NZ).astype(F32) for k in range(4)
         ]

time: 109 us -> 109 us (level)
  no operation moved by 1% of the time
where the time goes in v8:
time: 109 us
  waiting for transfers between devices  57.2 us (52%)
  Pallas kernels  24.8 us (23%)
  starting transfers between devices  24.8 us (23%)
  local copies, waits for them, and re-layouts  1.7 us (2%)
    all_to_all x3, waiting for transfers between devices, exchange(): return lax.all_to_all(value, AXES, split_axis=0, concat_axis=0, tiled=True)  57.2 us
    pallas_call x7, Pallas kernels, placed(): run(*(pltpu.with_memory_space_constraint(x, pltpu.HBM) if spec.memory_spa...  24.8 us
    all_to_all x3, starting transfers between devices, exchange(): return lax.all_to_all(value, AXES, split_axis=0, concat_axis=0, tiled=True)  16.8 us
    ppermute x4, starting transfers between devices, neighbours(): return (lax.ppermute(last, axis, up), lax.ppermute(first, axis, down))  7.97 us
  transfers between devices with their start and end apart: 7, of which 3 were waited for; matrix products, arithmetic and copies ran while one was open for 0% of the time, Pallas kernels for 14%

profile of v8, /device:TPU:1, one launch (start us, length us, event | category | flops | bytes accessed | tf_op | source)
XLA Modules:
  0.0 108.6 jit_solution(457032766091011091)
XLA Ops:
  0.0 3.3 %shard_map.55 = (f32[6272,128]{1,0:T(8,128)}, f32[5,4,16,256]{3,2,1,0:T(8,128)S(1)}, f32[5,4,16,256]{3,2,1,0:T(8,128)S(1)}, f32[5,16,4,256]{3,2,1,0:T(4,128)S(1)}, f32[5,16,4,256]{3,2,1,0:T(4,128)S(1)}) custom-call(s32[2,1,256]{2,1,0:T(1,128)} %bitcast.20, s32[2,1,256]{2,1,0:T(1,128)} %bitcast.22, bf16[2,4,16,16,256]{4,3,2,1,0:T(8,128)(2,1)} %w_hbm.3, ...), custom_call_target="tpu_custom_call" | custom-call | flops 300000000 | bytes 6000000 | tf_op jit(solution)/shard_map/pallas_call | solution.py:39
  3.3 3.0 %collective-permute-start = (f32[5,4,16,256]{3,2,1,0:T(8,128)S(1)}, f32[5,4,16,256]{3,2,1,0:T(8,128)S(1)}, u32[]{:S(2)}, u32[]{:S(2)}) collective-permute-start(f32[5,4,16,256]{3,2,1,0:T(8,128)S(1)} %get-tuple-element.26), channel_id=1, source_target_pairs={{0,16},{16,32},{32,48},{48,64},{64,80},{80,96},{96,112},{112,0},{1... | collective-permute-start | bytes 983048 | tf_op jit(solution)/shard_map/ppermute | solution.py:346
  6.3 0.0 collective-permute-start.1
  6.4 1.2 %collective-permute-start.2 = (f32[5,16,4,256]{3,2,1,0:T(4,128)S(1)}, f32[5,16,4,256]{3,2,1,0:T(4,128)S(1)}, u32[]{:S(2)}, u32[]{:S(2)}) collective-permute-start(f32[5,16,4,256]{3,2,1,0:T(4,128)S(1)} %get-tuple-element.28), channel_id=1, source_target_pairs={{0,1},{1,2},{2,3},{3,4},{4,5},{5,6},{6,7},{7,8},{8,9},{9,10},{10,1... | collective-permute-start | bytes 983048 | tf_op jit(solution)/shard_map/ppermute | solution.py:346
  7.6 3.7 %collective-permute-start.3 = (f32[5,16,4,256]{3,2,1,0:T(4,128)S(1)}, f32[5,16,4,256]{3,2,1,0:T(4,128)S(1)}, u32[]{:S(2)}, u32[]{:S(2)}) collective-permute-start(f32[5,16,4,256]{3,2,1,0:T(4,128)S(1)} %get-tuple-element.29), channel_id=1, source_target_pairs={{1,0},{2,1},{3,2},{4,3},{5,4},{6,5},{7,6},{8,7},{9,8},{10,9},{11,1... | collective-permute-start | bytes 983048 | tf_op jit(solution)/shard_map/ppermute | solution.py:346
  11.3 7.7 %all-to-all-start = ((f32[128,49,1,128]{3,2,1,0:T(1,128)}), f32[128,49,1,128]{3,2,1,0:T(1,128)}, u32[]{:S(2)}, u32[]{:S(2)}) async-start(f32[128,49,1,128]{3,2,1,0:T(1,128)} %bitcast.14), calls=%async_computation | async-start | bytes 6422528 | tf_op jit(solution)/shard_map/all_to_all | solution.py:339
  19.0 0.0 collective-permute-done.xlo
  19.0 0.0 copy-start
  19.0 0.0 collective-permute-done.1.xhi
  19.0 0.0 copy-start.1
  19.0 0.0 collective-permute-done.2.ylo
  19.1 0.0 copy-start.2
  19.1 0.0 collective-permute-done.3.yhi
  19.1 0.7 copy-done
  19.8 0.2 copy-done.1
  19.9 0.1 copy-done.2
  20.0 0.0 copy-start.3
  20.0 0.7 copy-done.3
  20.8 7.9 %shard_map.56 = (f32[2,3,16,16,256]{4,3,2,1,0:T(8,128)}, f32[16,16,256]{2,1,0:T(8,128)}, f32[3,16,16,256]{3,2,1,0:T(8,128)}, bf16[2,256,256]{2,1,0:T(8,128)(2,1)S(1)}) custom-call(f32[2,16,16,256]{3,2,1,0:T(8,128)} %st_hbm.3, f32[3,16,16,256]{3,2,1,0:T(8,128)} %ve_hbm.3, f32[5,4,16,256]{3,2,1,0:T(8,128)} %copy-done, f32[5,4,16,256]{3,2,1,0:T(8,128)} %copy-done.1, ...), custom_call_target="tpu_custom_call" | custom-call | flops 99999997952 | bytes 2000000000 | tf_op jit(solution)/shard_map/pallas_call | solution.py:39
  28.7 31.6 %all-to-all-done.asked_hbm = f32[128,49,1,128]{3,2,1,0:T(1,128)} async-done(((f32[128,49,1,128]{3,2,1,0:T(1,128)}), f32[128,49,1,128]{3,2,1,0:T(1,128)}, u32[]{:S(2)}, u32[]{:S(2)}) %all-to-all-start) | async-done | bytes 3211296 | tf_op jit(solution)/shard_map/all_to_all | solution.py:339
  60.3 2.1 %shard_map.57 = f32[1536,128]{1,0:T(8,128)} custom-call(f32[128,49,1,128]{3,2,1,0:T(1,128)} %all-to-all-done.asked_hbm, bf16[2,256,256]{2,1,0:T(8,128)(2,1)S(1)} %get-tuple-element.30.parts), custom_call_target="tpu_custom_call" | custom-call | flops 200000000 | bytes 4000000 | tf_op jit(solution)/shard_map/pallas_call | solution.py:39
  62.4 4.8 %all-to-all-start.1 = ((f32[128,6,2,128]{3,2,1,0:T(2,128)}), f32[128,6,2,128]{3,2,1,0:T(2,128)S(1)}, u32[]{:S(2)}, u32[]{:S(2)}) async-start(f32[128,6,2,128]{3,2,1,0:T(2,128)} %bitcast.15), calls=%async_computation.1 | async-start | bytes 1572864 | tf_op jit(solution)/shard_map/all_to_all | solution.py:339
  67.2 5.9 %shard_map.58 = (f32[4,256,256]{2,1,0:T(8,128)S(1)}, bf16[256,768]{1,0:T(8,128)(2,1)S(1)}, bf16[4,16,16,256]{3,2,1,0:T(8,128)(2,1)S(1)}, f32[256,256]{1,0:T(8,12...) custom-call(f32[6272,128]{1,0:T(8,128)} %bitcast.5.asked_hbm, s32[2,1,256]{2,1,0:T(1,128)} %bitcast.21, ...), custom_call_target="tpu_custom_call" | custom-call | flops 400000000 | bytes 8000000 | tf_op jit(solution)/shard_map/pallas_call | solution.py:39
  73.1 10.7 %all-to-all-done.1 = f32[128,6,2,128]{3,2,1,0:T(2,128)S(1)} async-done(((f32[128,6,2,128]{3,2,1,0:T(2,128)}), f32[128,6,2,128]{3,2,1,0:T(2,128)S(1)}, u32[]{:S(2)}, u32[]{:S(2)}) %all-to-all-start.1) | async-done | bytes 786464 | tf_op jit(solution)/shard_map/all_to_all | solution.py:339
  83.8 2.6 %shard_map.59 = (f32[256,256]{1,0:T(8,128)S(1)}, f32[1536,128]{1,0:T(8,128)}) custom-call(f32[1536,128]{1,0:T(8,128)S(1)} %bitcast.13, f32[4,256,256]{2,1,0:T(8,128)S(1)} %get-tuple-element.32.d, bf16[256,768]{1,0:T(8,128)(2,1)S(1)} %get-tuple-element.33.taken, bf16[4,16,16,256]{3,2,1,0:T(8,128)(2,1)S(1)} %get-tuple-element.34.w, ...), custom_call_target="tpu_custom_call" | custom-call | flops 400000000 | bytes 8000000 | tf_op jit(solution)/shard_map/pallas_call | solution.py:39
  86.4 4.2 %all-to-all-start.2 = ((f32[128,6,2,128]{3,2,1,0:T(2,128)}), f32[128,6,2,128]{3,2,1,0:T(2,128)S(1)}, u32[]{:S(2)}, u32[]{:S(2)}) async-start(f32[128,6,2,128]{3,2,1,0:T(2,128)} %bitcast.17), calls=%async_computation.2 | async-start | bytes 1572864 | tf_op jit(solution)/shard_map/all_to_all | solution.py:339
  90.6 1.8 %shard_map.60 = (f32[3,256,256]{2,1,0:T(8,128)S(1)}, f32[3,256,256]{2,1,0:T(8,128)S(1)}, bf16[256,768]{1,0:T(8,128)(2,1)S(1)}) custom-call(f32[256,256]{1,0:T(8,128)S(1)} %get-tuple-element.38.lam, f32[16,128]{1,0:T(8,128)} %get-tuple-element.39.wt_hbm, f32[3,256,256]{2,1,0:T(8,128)} %bitcast.18, f32[2,3,256,256]{3,2,1,0:T(8,128)} %bitcast.16), custom_call_target="tpu_custom_call" | custom-call | flops 300000000 | bytes 6000000 | tf_op jit(solution)/shard_map/pallas_call | solution.py:39
  92.4 14.9 %all-to-all-done.2 = f32[128,6,2,128]{3,2,1,0:T(2,128)S(1)} async-done(((f32[128,6,2,128]{3,2,1,0:T(2,128)}), f32[128,6,2,128]{3,2,1,0:T(2,128)S(1)}, u32[]{:S(2)}, u32[]{:S(2)}) %all-to-all-start.2) | async-done | bytes 786464 | tf_op jit(solution)/shard_map/all_to_all | solution.py:339
  107.3 1.3 %shard_map.61 = f32[3,256,256]{2,1,0:T(8,128)} custom-call(f32[1536,128]{1,0:T(8,128)S(1)} %bitcast.12, bf16[256,768]{1,0:T(8,128)(2,1)S(1)} %get-tuple-element.42.onehot, f32[3,256,256]{2,1,0:T(8,128)S(1)} %get-tuple-element.43.h, f32[3,256,256]{2,1,0:T(8,128)S(1)} %get-tuple-element.44.g), custom_call_target="tpu_custom_call" | custom-call | flops 200000000 | bytes 4000000 | tf_op jit(solution)/shard_map/pallas_call | solution.py:39
Async XLA Ops:
  3.3 15.7 %collective-permute-start = (f32[5,4,16,256]{3,2,1,0:T(8,128)S(1)}, f32[5,4,16,256]{3,2,1,0:T(8,128)S(1)}, u32[]{:S(2)}, u32[]{:S(2)}) collective-permute-start(f32[5,4,16,256]{3,2,1,0:T(8,128)S(1)} %get-tuple-element.26), channel_id=1, source_target_pairs={{0,16},{16,32},{32,48},{48,64},{64,80},{80,96},{96,112},{112,0},{1... | collective-permute-start | bytes 983048 | tf_op jit(solution)/shard_map/ppermute | solution.py:346
  6.3 12.7 %collective-permute-start.1 = (f32[5,4,16,256]{3,2,1,0:T(8,128)S(1)}, f32[5,4,16,256]{3,2,1,0:T(8,128)S(1)}, u32[]{:S(2)}, u32[]{:S(2)}) collective-permute-start(f32[5,4,16,256]{3,2,1,0:T(8,128)S(1)} %get-tuple-element.27), channel_id=1, source_target_pairs={{16,0},{32,16},{48,32},{64,48},{80,64},{96,80},{112,96},{0,112},{1... | collective-permute-start | bytes 983048 | tf_op jit(solution)/shard_map/ppermute | solution.py:346
  6.4 12.7 %collective-permute-start.2 = (f32[5,16,4,256]{3,2,1,0:T(4,128)S(1)}, f32[5,16,4,256]{3,2,1,0:T(4,128)S(1)}, u32[]{:S(2)}, u32[]{:S(2)}) collective-permute-start(f32[5,16,4,256]{3,2,1,0:T(4,128)S(1)} %get-tuple-element.28), channel_id=1, source_target_pairs={{0,1},{1,2},{2,3},{3,4},{4,5},{5,6},{6,7},{7,8},{8,9},{9,10},{10,1... | collective-permute-start | bytes 983048 | tf_op jit(solution)/shard_map/ppermute | solution.py:346
  7.6 11.5 %collective-permute-start.3 = (f32[5,16,4,256]{3,2,1,0:T(4,128)S(1)}, f32[5,16,4,256]{3,2,1,0:T(4,128)S(1)}, u32[]{:S(2)}, u32[]{:S(2)}) collective-permute-start(f32[5,16,4,256]{3,2,1,0:T(4,128)S(1)} %get-tuple-element.29), channel_id=1, source_target_pairs={{1,0},{2,1},{3,2},{4,3},{5,4},{6,5},{7,6},{8,7},{9,8},{10,9},{11,1... | collective-permute-start | bytes 983048 | tf_op jit(solution)/shard_map/ppermute | solution.py:346
  11.3 49.0 %all-to-all-start = ((f32[128,49,1,128]{3,2,1,0:T(1,128)}), f32[128,49,1,128]{3,2,1,0:T(1,128)}, u32[]{:S(2)}, u32[]{:S(2)}) async-start(f32[128,49,1,128]{3,2,1,0:T(1,128)} %bitcast.14), calls=%async_computation | async-start | bytes 6422528 | tf_op jit(solution)/shard_map/all_to_all | solution.py:339
  19.0 0.7 copy-start
  19.0 0.9 copy-start.1
  19.1 1.0 copy-start.2
  20.0 0.7 copy-start.3
  62.4 21.4 %all-to-all-start.1 = ((f32[128,6,2,128]{3,2,1,0:T(2,128)}), f32[128,6,2,128]{3,2,1,0:T(2,128)S(1)}, u32[]{:S(2)}, u32[]{:S(2)}) async-start(f32[128,6,2,128]{3,2,1,0:T(2,128)} %bitcast.15), calls=%async_computation.1 | async-start | bytes 1572864 | tf_op jit(solution)/shard_map/all_to_all | solution.py:339
  86.4 21.0 %all-to-all-start.2 = ((f32[128,6,2,128]{3,2,1,0:T(2,128)}), f32[128,6,2,128]{3,2,1,0:T(2,128)S(1)}, u32[]{:S(2)}, u32[]{:S(2)}) async-start(f32[128,6,2,128]{3,2,1,0:T(2,128)} %bitcast.17), calls=%async_computation.2 | async-start | bytes 1572864 | tf_op jit(solution)/shard_map/all_to_all | solution.py:339

commit v9 on v8

--- a/solution.py
+++ b/solution.py
@@ -106,16 +106,21 @@
         tile[pl.ds(i * 8, 8), :] = jnp.zeros((8, 128), F32)
 
 
+def odd(axis):
+    return lax.rem(lax.axis_index(axis), 2)
+
+
 def wait_all(copies):
     for copy in copies:
         copy.wait()
 
 
 def request_kernel(
-    own_hbm, src_hbm, w_hbm, st_hbm, ve_hbm, out_hbm, xlo, xhi, ylo, yhi, own, src, w, out, edges, tile, sems
+    own_hbm, src_hbm, w_hbm, st_hbm, ve_hbm, out_hbm, xin, xout, yin, yout, own, src, w, out, edges, tile, sems
 ):
     pairs = [(own_hbm, own), (src_hbm, src), (w_hbm.at[1], w)]
-    for x_out, y_out, first, y_first in ((xlo, 0, 0, 0), (xhi, 1, 12, 8)):
+    odd_x, odd_y = odd("gx"), odd("gy")
+    for x_out, y_out, first, y_first in ((xin, 0, 12 - 12 * odd_x, 0), (xout, 1, 12 * odd_x, 8)):
         for source, place in ((st_hbm, pl.ds(0, 2)), (ve_hbm, pl.ds(2, 3))):
             pairs.append((source.at[:, pl.ds(first, 4)], x_out.at[place]))
             pairs.append((source.at[:, :, pl.ds(y_first, 8)], edges.at[y_out, place]))
@@ -146,19 +151,20 @@
         block = pl.ds(first * A_ROWS, PART * A_ROWS)
         sent += start_all(((out.at[block], out_hbm.at[block]),), sems, 11 + i)
     wait_all(copies[3:])
-    ylo[...] = edges[0, :, :, 0:4]
-    yhi[...] = edges[1, :, :, 4:8]
+    yin[...] = jnp.where(odd_y == 1, edges[0, :, :, 0:4], edges[1, :, :, 4:8])
+    yout[...] = jnp.where(odd_y == 1, edges[1, :, :, 4:8], edges[0, :, :, 0:4])
     wait_all(sent)
 
 
-def fill(sources, halos, xpad, ypad, ylo, yhi, sems, extra=()):
-    pairs = list(extra) + [(halos[2], ylo), (halos[3], yhi)]
-    pairs += [(halos[0], xpad.at[:, pl.ds(0, 4)]), (halos[1], xpad.at[:, pl.ds(20, 4)])]
+def fill(sources, halos, xpad, ypad, yin, yout, sems):
+    odd_x, odd_y = odd("gx"), odd("gy")
+    pairs = [(halos[2], yin), (halos[3], yout)]
+    pairs += [(halos[0], xpad.at[:, pl.ds(20 - 20 * odd_x, 4)]), (halos[1], xpad.at[:, pl.ds(20 * odd_x, 4)])]
     for i, source in enumerate(sources):
         pairs += [(source, xpad.at[i, pl.ds(4, 16)]), (source, ypad.at[i, :, pl.ds(8, 16)])]
     wait_all(start_all(pairs, sems))
-    ypad[:, :, 4:8] = ylo[...]
-    ypad[:, :, 24:28] = yhi[...]
+    ypad[:, :, 4:8] = jnp.where(odd_y == 1, yin[...], yout[...])
+    ypad[:, :, 24:28] = jnp.where(odd_y == 1, yout[...], yin[...])
 
 
 def differences(xpad, ypad, i, x, rows, coeffs, sign):
@@ -181,10 +187,10 @@
 
 
 def stencil_kernel(
-    st_hbm, ve_hbm, xlo, xhi, ylo, yhi, g_hbm, b_hbm, h_hbm, first_parts, xpad, ypad, ylo_scr, yhi_scr, g, b, h, sems
+    st_hbm, ve_hbm, yout, yin, xout, xin, g_hbm, b_hbm, h_hbm, first_parts, xpad, ypad, yin_scr, yout_scr, g, b, h, sems
 ):
     sources = [st_hbm.at[j] for j in range(2)] + [ve_hbm.at[c] for c in range(3)]
-    fill(sources, (xlo, xhi, ylo, yhi), xpad, ypad, ylo_scr, yhi_scr, sems)
+    fill(sources, (xin, xout, yin, yout), xpad, ypad, yin_scr, yout_scr, sems)
     sent = []
     for j in range(2):
 
@@ -339,11 +345,12 @@
     return lax.all_to_all(value, AXES, split_axis=0, concat_axis=0, tiled=True)
 
 
-def neighbours(first, last, axis):
+def swapped(inner, outer, axis):
     count = lax.axis_size(axis)
-    up = [(i, (i + 1) % count) for i in range(count)]
-    down = [(j, i) for i, j in up]
-    return lax.ppermute(last, axis, up), lax.ppermute(first, axis, down)
+    within = [(i, i ^ 1) for i in range(count)]
+    across = [(i, (i + 1) % count if i % 2 else (i - 1) % count) for i in range(count)]
+    far = lax.ppermute(outer, axis, across)
+    return lax.ppermute(inner, axis, within), far
 
 
 def per_device(state_path, velocity, weights, owners, sources):
@@ -357,7 +364,7 @@
     per_field = lambda count: struct(count, 16, 16, NZ)
 
     edge_x, edge_y = pltpu.VMEM((5, 4, 16, NZ), F32), pltpu.VMEM((5, 16, 4, NZ), F32)
-    request, first_x, last_x, first_y, last_y = call(
+    request, inner_x, outer_x, inner_y, outer_y = call(
         request_kernel,
         (struct(DEV * A_ROWS, 128), edge_x, edge_x, edge_y, edge_y),
         16,
@@ -376,7 +383,9 @@
     )(owner_row, source_row, weights, state_path, velocity)
     asked = exchange(request.reshape(DEV, A_ROWS, 1, 128))
 
-    halos = neighbours(first_x, last_x, "gx") + neighbours(first_y, last_y, "gy")
+    in_x, out_x = swapped(inner_x, outer_x, "gx")
+    in_y, out_y = swapped(inner_y, outer_y, "gy")
+    halos = out_y, in_y, out_x, in_x
     slopes, before, hess, before_parts = call(
         stencil_kernel,
         (struct(2, 3, 16, 16, NZ), struct(16, 16, NZ), per_field(3), pltpu.VMEM((2, COLS, NZ), BF16)),

time: 109 us -> 109 us (level)
    ppermute x4, starting transfers between devices: 7.97 us -> 9.99 us  [the longest x2 8.31 us: swapped(): far = lax.ppermute(outer, axis, across)]
    all_to_all x3, starting transfers between devices: 16.8 us -> 15 us  [exchange(): return lax.all_to_all(value, AXES, split_axis=0, concat_axis=0, tiled=True)]
where the time goes in v9:
time: 109 us
  waiting for transfers between devices  57.2 us (52%)
  starting transfers between devices  25 us (23%)
  Pallas kernels  24.8 us (23%)
  local copies, waits for them, and re-layouts  1.7 us (2%)
    all_to_all x3, waiting for transfers between devices, exchange(): return lax.all_to_all(value, AXES, split_axis=0, concat_axis=0, tiled=True)  57.2 us
    pallas_call x7, Pallas kernels, placed(): run(*(pltpu.with_memory_space_constraint(x, pltpu.HBM) if spec.memory_spa...  24.8 us
    all_to_all x3, starting transfers between devices, exchange(): return lax.all_to_all(value, AXES, split_axis=0, concat_axis=0, tiled=True)  15 us
    ppermute x2, starting transfers between devices, swapped(): far = lax.ppermute(outer, axis, across)  8.31 us
  transfers between devices with their start and end apart: 7, of which 3 were waited for; matrix products, arithmetic and copies ran while one was open for 0% of the time, Pallas kernels for 14%

profile of v9, /device:TPU:1, one launch (start us, length us, event | category | flops | bytes accessed | tf_op | source)
XLA Modules:
  0.0 108.9 jit_solution(826754599391636580)
XLA Ops:
  0.0 3.3 %shard_map.55 = (f32[6272,128]{1,0:T(8,128)}, f32[5,4,16,256]{3,2,1,0:T(8,128)S(1)}, f32[5,4,16,256]{3,2,1,0:T(8,128)S(1)}, f32[5,16,4,256]{3,2,1,0:T(4,128)S(1)}, f32[5,16,4,256]{3,2,1,0:T(4,128)S(1)}) custom-call(s32[2,1,256]{2,1,0:T(1,128)} %bitcast.20, s32[2,1,256]{2,1,0:T(1,128)} %bitcast.22, bf16[2,4,16,16,256]{4,3,2,1,0:T(8,128)(2,1)} %w_hbm.3, ...), custom_call_target="tpu_custom_call" | custom-call | flops 300000000 | bytes 6000000 | tf_op jit(solution)/shard_map/pallas_call | solution.py:39
  3.3 5.8 %collective-permute-start = (f32[5,16,4,256]{3,2,1,0:T(4,128)S(1)}, f32[5,16,4,256]{3,2,1,0:T(4,128)S(1)}, u32[]{:S(2)}, u32[]{:S(2)}) collective-permute-start(f32[5,16,4,256]{3,2,1,0:T(4,128)S(1)} %get-tuple-element.26), channel_id=1, source_target_pairs={{0,15},{1,2},{2,1},{3,4},{4,3},{5,6},{6,5},{7,8},{8,7},{9,10},{10,... | collective-permute-start | bytes 983048 | tf_op jit(solution)/shard_map/ppermute | solution.py:352
  9.1 0.0 collective-permute-start.1
  9.1 2.5 %collective-permute-start.2 = (f32[5,4,16,256]{3,2,1,0:T(8,128)S(1)}, f32[5,4,16,256]{3,2,1,0:T(8,128)S(1)}, u32[]{:S(2)}, u32[]{:S(2)}) collective-permute-start(f32[5,4,16,256]{3,2,1,0:T(8,128)S(1)} %get-tuple-element.28), channel_id=1, source_target_pairs={{0,112},{16,32},{32,16},{48,64},{64,48},{80,96},{96,80},{112,0},{1... | collective-permute-start | bytes 983048 | tf_op jit(solution)/shard_map/ppermute | solution.py:352
  11.6 1.7 %collective-permute-start.3 = (f32[5,4,16,256]{3,2,1,0:T(8,128)S(1)}, f32[5,4,16,256]{3,2,1,0:T(8,128)S(1)}, u32[]{:S(2)}, u32[]{:S(2)}) collective-permute-start(f32[5,4,16,256]{3,2,1,0:T(8,128)S(1)} %get-tuple-element.29), channel_id=1, source_target_pairs={{0,16},{16,0},{32,48},{48,32},{64,80},{80,64},{96,112},{112,96},{1... | collective-permute-start | bytes 983048 | tf_op jit(solution)/shard_map/ppermute | solution.py:353
  13.3 6.0 %all-to-all-start = ((f32[128,49,1,128]{3,2,1,0:T(1,128)}), f32[128,49,1,128]{3,2,1,0:T(1,128)}, u32[]{:S(2)}, u32[]{:S(2)}) async-start(f32[128,49,1,128]{3,2,1,0:T(1,128)} %bitcast.14), calls=%async_computation | async-start | bytes 6422528 | tf_op jit(solution)/shard_map/all_to_all | solution.py:345
  19.3 0.0 collective-permute-done.yout
  19.3 0.0 copy-start
  19.3 0.0 collective-permute-done.1.yin
  19.3 0.0 copy-start.1
  19.3 0.0 collective-permute-done.2.xout
  19.3 0.0 copy-start.2
  19.3 0.0 collective-permute-done.3.xin
  19.3 0.7 copy-done
  20.0 0.2 copy-done.1
  20.2 0.1 copy-done.2
  20.3 0.0 copy-start.3
  20.3 0.7 copy-done.3
  21.0 7.9 %shard_map.56 = (f32[2,3,16,16,256]{4,3,2,1,0:T(8,128)}, f32[16,16,256]{2,1,0:T(8,128)}, f32[3,16,16,256]{3,2,1,0:T(8,128)}, bf16[2,256,256]{2,1,0:T(8,128)(2,1)S(1)}) custom-call(f32[2,16,16,256]{3,2,1,0:T(8,128)} %st_hbm.3, f32[3,16,16,256]{3,2,1,0:T(8,128)} %ve_hbm.3, f32[5,16,4,256]{3,2,1,0:T(4,128)} %copy-done, f32[5,16,4,256]{3,2,1,0:T(4,128)} %copy-done.1, ...), custom_call_target="tpu_custom_call" | custom-call | flops 99999997952 | bytes 2000000000 | tf_op jit(solution)/shard_map/pallas_call | solution.py:39
  29.0 31.6 %all-to-all-done.asked_hbm = f32[128,49,1,128]{3,2,1,0:T(1,128)} async-done(((f32[128,49,1,128]{3,2,1,0:T(1,128)}), f32[128,49,1,128]{3,2,1,0:T(1,128)}, u32[]{:S(2)}, u32[]{:S(2)}) %all-to-all-start) | async-done | bytes 3211296 | tf_op jit(solution)/shard_map/all_to_all | solution.py:345
  60.5 2.1 %shard_map.57 = f32[1536,128]{1,0:T(8,128)} custom-call(f32[128,49,1,128]{3,2,1,0:T(1,128)} %all-to-all-done.asked_hbm, bf16[2,256,256]{2,1,0:T(8,128)(2,1)S(1)} %get-tuple-element.30.parts), custom_call_target="tpu_custom_call" | custom-call | flops 200000000 | bytes 4000000 | tf_op jit(solution)/shard_map/pallas_call | solution.py:39
  62.6 4.8 %all-to-all-start.1 = ((f32[128,6,2,128]{3,2,1,0:T(2,128)}), f32[128,6,2,128]{3,2,1,0:T(2,128)S(1)}, u32[]{:S(2)}, u32[]{:S(2)}) async-start(f32[128,6,2,128]{3,2,1,0:T(2,128)} %bitcast.15), calls=%async_computation.1 | async-start | bytes 1572864 | tf_op jit(solution)/shard_map/all_to_all | solution.py:345
  67.5 5.9 %shard_map.58 = (f32[4,256,256]{2,1,0:T(8,128)S(1)}, bf16[256,768]{1,0:T(8,128)(2,1)S(1)}, bf16[4,16,16,256]{3,2,1,0:T(8,128)(2,1)S(1)}, f32[256,256]{1,0:T(8,12...) custom-call(f32[6272,128]{1,0:T(8,128)} %bitcast.5.asked_hbm, s32[2,1,256]{2,1,0:T(1,128)} %bitcast.21, ...), custom_call_target="tpu_custom_call" | custom-call | flops 400000000 | bytes 8000000 | tf_op jit(solution)/shard_map/pallas_call | solution.py:39
  73.3 10.7 %all-to-all-done.1 = f32[128,6,2,128]{3,2,1,0:T(2,128)S(1)} async-done(((f32[128,6,2,128]{3,2,1,0:T(2,128)}), f32[128,6,2,128]{3,2,1,0:T(2,128)S(1)}, u32[]{:S(2)}, u32[]{:S(2)}) %all-to-all-start.1) | async-done | bytes 786464 | tf_op jit(solution)/shard_map/all_to_all | solution.py:345
  84.0 2.6 %shard_map.59 = (f32[256,256]{1,0:T(8,128)S(1)}, f32[1536,128]{1,0:T(8,128)}) custom-call(f32[1536,128]{1,0:T(8,128)S(1)} %bitcast.13, f32[4,256,256]{2,1,0:T(8,128)S(1)} %get-tuple-element.32.d, bf16[256,768]{1,0:T(8,128)(2,1)S(1)} %get-tuple-element.33.taken, bf16[4,16,16,256]{3,2,1,0:T(8,128)(2,1)S(1)} %get-tuple-element.34.w, ...), custom_call_target="tpu_custom_call" | custom-call | flops 400000000 | bytes 8000000 | tf_op jit(solution)/shard_map/pallas_call | solution.py:39
  86.6 4.3 %all-to-all-start.2 = ((f32[128,6,2,128]{3,2,1,0:T(2,128)}), f32[128,6,2,128]{3,2,1,0:T(2,128)S(1)}, u32[]{:S(2)}, u32[]{:S(2)}) async-start(f32[128,6,2,128]{3,2,1,0:T(2,128)} %bitcast.17), calls=%async_computation.2 | async-start | bytes 1572864 | tf_op jit(solution)/shard_map/all_to_all | solution.py:345
  90.9 1.8 %shard_map.60 = (f32[3,256,256]{2,1,0:T(8,128)S(1)}, f32[3,256,256]{2,1,0:T(8,128)S(1)}, bf16[256,768]{1,0:T(8,128)(2,1)S(1)}) custom-call(f32[256,256]{1,0:T(8,128)S(1)} %get-tuple-element.38.lam, f32[16,128]{1,0:T(8,128)} %get-tuple-element.39.wt_hbm, f32[3,256,256]{2,1,0:T(8,128)} %bitcast.18, f32[2,3,256,256]{3,2,1,0:T(8,128)} %bitcast.16), custom_call_target="tpu_custom_call" | custom-call | flops 300000000 | bytes 6000000 | tf_op jit(solution)/shard_map/pallas_call | solution.py:39
  92.7 14.9 %all-to-all-done.2 = f32[128,6,2,128]{3,2,1,0:T(2,128)S(1)} async-done(((f32[128,6,2,128]{3,2,1,0:T(2,128)}), f32[128,6,2,128]{3,2,1,0:T(2,128)S(1)}, u32[]{:S(2)}, u32[]{:S(2)}) %all-to-all-start.2) | async-done | bytes 786464 | tf_op jit(solution)/shard_map/all_to_all | solution.py:345
  107.6 1.3 %shard_map.61 = f32[3,256,256]{2,1,0:T(8,128)} custom-call(f32[1536,128]{1,0:T(8,128)S(1)} %bitcast.12, bf16[256,768]{1,0:T(8,128)(2,1)S(1)} %get-tuple-element.42.onehot, f32[3,256,256]{2,1,0:T(8,128)S(1)} %get-tuple-element.43.h, f32[3,256,256]{2,1,0:T(8,128)S(1)} %get-tuple-element.44.g), custom_call_target="tpu_custom_call" | custom-call | flops 200000000 | bytes 4000000 | tf_op jit(solution)/shard_map/pallas_call | solution.py:39
Async XLA Ops:
  3.3 16.0 %collective-permute-start = (f32[5,16,4,256]{3,2,1,0:T(4,128)S(1)}, f32[5,16,4,256]{3,2,1,0:T(4,128)S(1)}, u32[]{:S(2)}, u32[]{:S(2)}) collective-permute-start(f32[5,16,4,256]{3,2,1,0:T(4,128)S(1)} %get-tuple-element.26), channel_id=1, source_target_pairs={{0,15},{1,2},{2,1},{3,4},{4,3},{5,6},{6,5},{7,8},{8,7},{9,10},{10,... | collective-permute-start | bytes 983048 | tf_op jit(solution)/shard_map/ppermute | solution.py:352
  9.1 10.1 %collective-permute-start.1 = (f32[5,16,4,256]{3,2,1,0:T(4,128)S(1)}, f32[5,16,4,256]{3,2,1,0:T(4,128)S(1)}, u32[]{:S(2)}, u32[]{:S(2)}) collective-permute-start(f32[5,16,4,256]{3,2,1,0:T(4,128)S(1)} %get-tuple-element.27), channel_id=1, source_target_pairs={{0,1},{1,0},{2,3},{3,2},{4,5},{5,4},{6,7},{7,6},{8,9},{9,8},{10,11... | collective-permute-start | bytes 983048 | tf_op jit(solution)/shard_map/ppermute | solution.py:353
  9.1 10.2 %collective-permute-start.2 = (f32[5,4,16,256]{3,2,1,0:T(8,128)S(1)}, f32[5,4,16,256]{3,2,1,0:T(8,128)S(1)}, u32[]{:S(2)}, u32[]{:S(2)}) collective-permute-start(f32[5,4,16,256]{3,2,1,0:T(8,128)S(1)} %get-tuple-element.28), channel_id=1, source_target_pairs={{0,112},{16,32},{32,16},{48,64},{64,48},{80,96},{96,80},{112,0},{1... | collective-permute-start | bytes 983048 | tf_op jit(solution)/shard_map/ppermute | solution.py:352
  11.6 7.7 %collective-permute-start.3 = (f32[5,4,16,256]{3,2,1,0:T(8,128)S(1)}, f32[5,4,16,256]{3,2,1,0:T(8,128)S(1)}, u32[]{:S(2)}, u32[]{:S(2)}) collective-permute-start(f32[5,4,16,256]{3,2,1,0:T(8,128)S(1)} %get-tuple-element.29), channel_id=1, source_target_pairs={{0,16},{16,0},{32,48},{48,32},{64,80},{80,64},{96,112},{112,96},{1... | collective-permute-start | bytes 983048 | tf_op jit(solution)/shard_map/ppermute | solution.py:353
  13.3 47.2 %all-to-all-start = ((f32[128,49,1,128]{3,2,1,0:T(1,128)}), f32[128,49,1,128]{3,2,1,0:T(1,128)}, u32[]{:S(2)}, u32[]{:S(2)}) async-start(f32[128,49,1,128]{3,2,1,0:T(1,128)} %bitcast.14), calls=%async_computation | async-start | bytes 6422528 | tf_op jit(solution)/shard_map/all_to_all | solution.py:345
  19.3 0.7 copy-start
  19.3 0.9 copy-start.1
  19.3 1.0 copy-start.2
  20.3 0.7 copy-start.3
  62.6 21.4 %all-to-all-start.1 = ((f32[128,6,2,128]{3,2,1,0:T(2,128)}), f32[128,6,2,128]{3,2,1,0:T(2,128)S(1)}, u32[]{:S(2)}, u32[]{:S(2)}) async-start(f32[128,6,2,128]{3,2,1,0:T(2,128)} %bitcast.15), calls=%async_computation.1 | async-start | bytes 1572864 | tf_op jit(solution)/shard_map/all_to_all | solution.py:345
  86.6 21.0 %all-to-all-start.2 = ((f32[128,6,2,128]{3,2,1,0:T(2,128)}), f32[128,6,2,128]{3,2,1,0:T(2,128)S(1)}, u32[]{:S(2)}, u32[]{:S(2)}) async-start(f32[128,6,2,128]{3,2,1,0:T(2,128)} %bitcast.17), calls=%async_computation.2 | async-start | bytes 1572864 | tf_op jit(solution)/shard_map/all_to_all | solution.py:345

commit v10 on v7

--- a/solution.py
+++ b/solution.py
@@ -106,16 +106,21 @@
         tile[pl.ds(i * 8, 8), :] = jnp.zeros((8, 128), F32)
 
 
+def odd(axis):
+    return lax.rem(lax.axis_index(axis), 2)
+
+
 def wait_all(copies):
     for copy in copies:
         copy.wait()
 
 
 def request_kernel(
-    own_hbm, src_hbm, w_hbm, st_hbm, ve_hbm, out_hbm, xlo, xhi, ylo, yhi, own, src, w, out, edges, tile, sems
+    own_hbm, src_hbm, w_hbm, st_hbm, ve_hbm, out_hbm, xin, xout, ylo, yhi, own, src, w, out, edges, tile, sems
 ):
     pairs = [(own_hbm, own), (src_hbm, src), (w_hbm.at[1], w)]
-    for x_out, y_out, first, y_first in ((xlo, 0, 0, 0), (xhi, 1, 12, 8)):
+    odd_x = odd("gx")
+    for x_out, y_out, first, y_first in ((xin, 0, 12 - 12 * odd_x, 0), (xout, 1, 12 * odd_x, 8)):
         for source, place in ((st_hbm, pl.ds(0, 2)), (ve_hbm, pl.ds(2, 3))):
             pairs.append((source.at[:, pl.ds(first, 4)], x_out.at[place]))
             pairs.append((source.at[:, :, pl.ds(y_first, 8)], edges.at[y_out, place]))
@@ -152,8 +157,9 @@
 
 
 def fill(sources, halos, xpad, ypad, ylo, yhi, sems, extra=()):
+    odd_x = odd("gx")
     pairs = list(extra) + [(halos[2], ylo), (halos[3], yhi)]
-    pairs += [(halos[0], xpad.at[:, pl.ds(0, 4)]), (halos[1], xpad.at[:, pl.ds(20, 4)])]
+    pairs += [(halos[0], xpad.at[:, pl.ds(20 - 20 * odd_x, 4)]), (halos[1], xpad.at[:, pl.ds(20 * odd_x, 4)])]
     for i, source in enumerate(sources):
         pairs += [(source, xpad.at[i, pl.ds(4, 16)]), (source, ypad.at[i, :, pl.ds(8, 16)])]
     wait_all(start_all(pairs, sems))
@@ -181,10 +187,10 @@
 
 
 def stencil_kernel(
-    st_hbm, ve_hbm, xlo, xhi, ylo, yhi, g_hbm, b_hbm, h_hbm, first_parts, xpad, ypad, ylo_scr, yhi_scr, g, b, h, sems
+    st_hbm, ve_hbm, xin, xout, ylo, yhi, g_hbm, b_hbm, h_hbm, first_parts, xpad, ypad, ylo_scr, yhi_scr, g, b, h, sems
 ):
     sources = [st_hbm.at[j] for j in range(2)] + [ve_hbm.at[c] for c in range(3)]
-    fill(sources, (xlo, xhi, ylo, yhi), xpad, ypad, ylo_scr, yhi_scr, sems)
+    fill(sources, (xin, xout, ylo, yhi), xpad, ypad, ylo_scr, yhi_scr, sems)
     sent = []
     for j in range(2):
 
@@ -339,6 +345,13 @@
     return lax.all_to_all(value, AXES, split_axis=0, concat_axis=0, tiled=True)
 
 
+def swapped(inner, outer, axis):
+    count = lax.axis_size(axis)
+    within = [(i, i ^ 1) for i in range(count)]
+    across = [(i, (i + 1) % count if i % 2 else (i - 1) % count) for i in range(count)]
+    return lax.ppermute(inner, axis, within), lax.ppermute(outer, axis, across)
+
+
 def neighbours(first, last, axis):
     count = lax.axis_size(axis)
     up = [(i, (i + 1) % count) for i in range(count)]
@@ -357,7 +370,7 @@
     per_field = lambda count: struct(count, 16, 16, NZ)
 
     edge_x, edge_y = pltpu.VMEM((5, 4, 16, NZ), F32), pltpu.VMEM((5, 16, 4, NZ), F32)
-    request, first_x, last_x, first_y, last_y = call(
+    request, inner_x, outer_x, first_y, last_y = call(
         request_kernel,
         (struct(DEV * A_ROWS, 128), edge_x, edge_x, edge_y, edge_y),
         16,
@@ -376,7 +389,7 @@
     )(owner_row, source_row, weights, state_path, velocity)
     asked = exchange(request.reshape(DEV, A_ROWS, 1, 128))
 
-    halos = neighbours(first_x, last_x, "gx") + neighbours(first_y, last_y, "gy")
+    halos = swapped(inner_x, outer_x, "gx") + neighbours(first_y, last_y, "gy")
     slopes, before, hess, before_parts = call(
         stencil_kernel,
         (struct(2, 3, 16, 16, NZ), struct(16, 16, NZ), per_field(3), pltpu.VMEM((2, COLS, NZ), BF16)),

time: 109 us -> 109 us (level)
    ppermute x0 -> x2, starting transfers between devices: none -> 3.2 us  [the longest x1 1.7 us: swapped(): lax.ppermute(outer, axis, across)]
    ppermute x4 -> x2, starting transfers between devices: 7.97 us -> 4.93 us  [neighbours(): return (lax.ppermute(last, axis, up), lax.ppermute(first, axis, down))]
where the time goes in v10:
time: 109 us
  waiting for transfers between devices  57.4 us (53%)
  Pallas kernels  25 us (23%)
  starting transfers between devices  24.6 us (23%)
  local copies, waits for them, and re-layouts  1.7 us (2%)
    all_to_all x3, waiting for transfers between devices, exchange(): return lax.all_to_all(value, AXES, split_axis=0, concat_axis=0, tiled=True)  57.3 us
    pallas_call x7, Pallas kernels, placed(): run(*(pltpu.with_memory_space_constraint(x, pltpu.HBM) if spec.memory_spa...  25 us
    all_to_all x3, starting transfers between devices, exchange(): return lax.all_to_all(value, AXES, split_axis=0, concat_axis=0, tiled=True)  16.5 us
    ppermute x2, starting transfers between devices, neighbours(): return (lax.ppermute(last, axis, up), lax.ppermute(first, axis, down))  4.93 us
  transfers between devices with their start and end apart: 7, of which 3 were waited for; matrix products, arithmetic and copies ran while one was open for 0% of the time, Pallas kernels for 14%

profile of v10, /device:TPU:1, one launch (start us, length us, event | category | flops | bytes accessed | tf_op | source)
XLA Modules:
  0.0 108.8 jit_solution(7084766108564636884)
XLA Ops:
  0.0 3.3 %shard_map.55 = (f32[6272,128]{1,0:T(8,128)}, f32[5,4,16,256]{3,2,1,0:T(8,128)S(1)}, f32[5,4,16,256]{3,2,1,0:T(8,128)S(1)}, f32[5,16,4,256]{3,2,1,0:T(4,128)S(1)}, f32[5,16,4,256]{3,2,1,0:T(4,128)S(1)}) custom-call(s32[2,1,256]{2,1,0:T(1,128)} %bitcast.20, s32[2,1,256]{2,1,0:T(1,128)} %bitcast.22, bf16[2,4,16,16,256]{4,3,2,1,0:T(8,128)(2,1)} %w_hbm.3, ...), custom_call_target="tpu_custom_call" | custom-call | flops 300000000 | bytes 6000000 | tf_op jit(solution)/shard_map/pallas_call | solution.py:39
  3.3 1.5 %collective-permute-start = (f32[5,4,16,256]{3,2,1,0:T(8,128)S(1)}, f32[5,4,16,256]{3,2,1,0:T(8,128)S(1)}, u32[]{:S(2)}, u32[]{:S(2)}) collective-permute-start(f32[5,4,16,256]{3,2,1,0:T(8,128)S(1)} %get-tuple-element.26), channel_id=1, source_target_pairs={{0,16},{16,0},{32,48},{48,32},{64,80},{80,64},{96,112},{112,96},{1... | collective-permute-start | bytes 983048 | tf_op jit(solution)/shard_map/ppermute | solution.py:352
  4.8 1.7 %collective-permute-start.1 = (f32[5,4,16,256]{3,2,1,0:T(8,128)S(1)}, f32[5,4,16,256]{3,2,1,0:T(8,128)S(1)}, u32[]{:S(2)}, u32[]{:S(2)}) collective-permute-start(f32[5,4,16,256]{3,2,1,0:T(8,128)S(1)} %get-tuple-element.27), channel_id=1, source_target_pairs={{0,112},{16,32},{32,16},{48,64},{64,48},{80,96},{96,80},{112,0},{1... | collective-permute-start | bytes 983048 | tf_op jit(solution)/shard_map/ppermute | solution.py:352
  6.5 1.2 %collective-permute-start.2 = (f32[5,16,4,256]{3,2,1,0:T(4,128)S(1)}, f32[5,16,4,256]{3,2,1,0:T(4,128)S(1)}, u32[]{:S(2)}, u32[]{:S(2)}) collective-permute-start(f32[5,16,4,256]{3,2,1,0:T(4,128)S(1)} %get-tuple-element.28), channel_id=1, source_target_pairs={{0,1},{1,2},{2,3},{3,4},{4,5},{5,6},{6,7},{7,8},{8,9},{9,10},{10,1... | collective-permute-start | bytes 983048 | tf_op jit(solution)/shard_map/ppermute | solution.py:359
  7.7 3.7 %collective-permute-start.3 = (f32[5,16,4,256]{3,2,1,0:T(4,128)S(1)}, f32[5,16,4,256]{3,2,1,0:T(4,128)S(1)}, u32[]{:S(2)}, u32[]{:S(2)}) collective-permute-start(f32[5,16,4,256]{3,2,1,0:T(4,128)S(1)} %get-tuple-element.29), channel_id=1, source_target_pairs={{1,0},{2,1},{3,2},{4,3},{5,4},{6,5},{7,6},{8,7},{9,8},{10,9},{11,1... | collective-permute-start | bytes 983048 | tf_op jit(solution)/shard_map/ppermute | solution.py:359
  11.4 7.4 %all-to-all-start = ((f32[128,49,1,128]{3,2,1,0:T(1,128)}), f32[128,49,1,128]{3,2,1,0:T(1,128)}, u32[]{:S(2)}, u32[]{:S(2)}) async-start(f32[128,49,1,128]{3,2,1,0:T(1,128)} %bitcast.14), calls=%async_computation | async-start | bytes 6422528 | tf_op jit(solution)/shard_map/all_to_all | solution.py:345
  18.9 0.0 collective-permute-done.xin
  18.9 0.0 copy-start
  18.9 0.0 collective-permute-done.1.xout
  18.9 0.0 copy-start.1
  18.9 0.0 collective-permute-done.2.ylo
  18.9 0.0 copy-start.2
  18.9 0.0 collective-permute-done.3.yhi
  18.9 0.7 copy-done
  19.6 0.2 copy-done.1
  19.8 0.1 copy-done.2
  19.9 0.0 copy-start.3
  19.9 0.7 copy-done.3
  20.6 7.9 %shard_map.56 = (f32[2,3,16,16,256]{4,3,2,1,0:T(8,128)}, f32[16,16,256]{2,1,0:T(8,128)}, f32[3,16,16,256]{3,2,1,0:T(8,128)}, bf16[2,256,256]{2,1,0:T(8,128)(2,1)S(1)}) custom-call(f32[2,16,16,256]{3,2,1,0:T(8,128)} %st_hbm.3, f32[3,16,16,256]{3,2,1,0:T(8,128)} %ve_hbm.3, f32[5,4,16,256]{3,2,1,0:T(8,128)} %copy-done, f32[5,4,16,256]{3,2,1,0:T(8,128)} %copy-done.1, ...), custom_call_target="tpu_custom_call" | custom-call | flops 99999997952 | bytes 2000000000 | tf_op jit(solution)/shard_map/pallas_call | solution.py:39
  28.6 31.7 %all-to-all-done.asked_hbm = f32[128,49,1,128]{3,2,1,0:T(1,128)} async-done(((f32[128,49,1,128]{3,2,1,0:T(1,128)}), f32[128,49,1,128]{3,2,1,0:T(1,128)}, u32[]{:S(2)}, u32[]{:S(2)}) %all-to-all-start) | async-done | bytes 3211296 | tf_op jit(solution)/shard_map/all_to_all | solution.py:345
  60.3 2.1 %shard_map.57 = f32[1536,128]{1,0:T(8,128)} custom-call(f32[128,49,1,128]{3,2,1,0:T(1,128)} %all-to-all-done.asked_hbm, bf16[2,256,256]{2,1,0:T(8,128)(2,1)S(1)} %get-tuple-element.30.parts), custom_call_target="tpu_custom_call" | custom-call | flops 200000000 | bytes 4000000 | tf_op jit(solution)/shard_map/pallas_call | solution.py:39
  62.4 4.8 %all-to-all-start.1 = ((f32[128,6,2,128]{3,2,1,0:T(2,128)}), f32[128,6,2,128]{3,2,1,0:T(2,128)S(1)}, u32[]{:S(2)}, u32[]{:S(2)}) async-start(f32[128,6,2,128]{3,2,1,0:T(2,128)} %bitcast.15), calls=%async_computation.1 | async-start | bytes 1572864 | tf_op jit(solution)/shard_map/all_to_all | solution.py:345
  67.2 5.9 %shard_map.58 = (f32[4,256,256]{2,1,0:T(8,128)S(1)}, bf16[256,768]{1,0:T(8,128)(2,1)S(1)}, bf16[4,16,16,256]{3,2,1,0:T(8,128)(2,1)S(1)}, f32[256,256]{1,0:T(8,12...) custom-call(f32[6272,128]{1,0:T(8,128)} %bitcast.5.asked_hbm, s32[2,1,256]{2,1,0:T(1,128)} %bitcast.21, ...), custom_call_target="tpu_custom_call" | custom-call | flops 400000000 | bytes 8000000 | tf_op jit(solution)/shard_map/pallas_call | solution.py:39
  73.1 10.7 %all-to-all-done.1 = f32[128,6,2,128]{3,2,1,0:T(2,128)S(1)} async-done(((f32[128,6,2,128]{3,2,1,0:T(2,128)}), f32[128,6,2,128]{3,2,1,0:T(2,128)S(1)}, u32[]{:S(2)}, u32[]{:S(2)}) %all-to-all-start.1) | async-done | bytes 786464 | tf_op jit(solution)/shard_map/all_to_all | solution.py:345
  83.8 2.7 %shard_map.59 = (f32[256,256]{1,0:T(8,128)S(1)}, f32[1536,128]{1,0:T(8,128)}) custom-call(f32[1536,128]{1,0:T(8,128)S(1)} %bitcast.13, f32[4,256,256]{2,1,0:T(8,128)S(1)} %get-tuple-element.32.d, bf16[256,768]{1,0:T(8,128)(2,1)S(1)} %get-tuple-element.33.taken, bf16[4,16,16,256]{3,2,1,0:T(8,128)(2,1)S(1)} %get-tuple-element.34.w, ...), custom_call_target="tpu_custom_call" | custom-call | flops 400000000 | bytes 8000000 | tf_op jit(solution)/shard_map/pallas_call | solution.py:39
  86.5 4.3 %all-to-all-start.2 = ((f32[128,6,2,128]{3,2,1,0:T(2,128)}), f32[128,6,2,128]{3,2,1,0:T(2,128)S(1)}, u32[]{:S(2)}, u32[]{:S(2)}) async-start(f32[128,6,2,128]{3,2,1,0:T(2,128)} %bitcast.17), calls=%async_computation.2 | async-start | bytes 1572864 | tf_op jit(solution)/shard_map/all_to_all | solution.py:345
  90.8 1.8 %shard_map.60 = (f32[3,256,256]{2,1,0:T(8,128)S(1)}, f32[3,256,256]{2,1,0:T(8,128)S(1)}, bf16[256,768]{1,0:T(8,128)(2,1)S(1)}) custom-call(f32[256,256]{1,0:T(8,128)S(1)} %get-tuple-element.38.lam, f32[16,128]{1,0:T(8,128)} %get-tuple-element.39.wt_hbm, f32[3,256,256]{2,1,0:T(8,128)} %bitcast.18, f32[2,3,256,256]{3,2,1,0:T(8,128)} %bitcast.16), custom_call_target="tpu_custom_call" | custom-call | flops 300000000 | bytes 6000000 | tf_op jit(solution)/shard_map/pallas_call | solution.py:39
  92.5 14.9 %all-to-all-done.2 = f32[128,6,2,128]{3,2,1,0:T(2,128)S(1)} async-done(((f32[128,6,2,128]{3,2,1,0:T(2,128)}), f32[128,6,2,128]{3,2,1,0:T(2,128)S(1)}, u32[]{:S(2)}, u32[]{:S(2)}) %all-to-all-start.2) | async-done | bytes 786464 | tf_op jit(solution)/shard_map/all_to_all | solution.py:345
  107.5 1.3 %shard_map.61 = f32[3,256,256]{2,1,0:T(8,128)} custom-call(f32[1536,128]{1,0:T(8,128)S(1)} %bitcast.12, bf16[256,768]{1,0:T(8,128)(2,1)S(1)} %get-tuple-element.42.onehot, f32[3,256,256]{2,1,0:T(8,128)S(1)} %get-tuple-element.43.h, f32[3,256,256]{2,1,0:T(8,128)S(1)} %get-tuple-element.44.g), custom_call_target="tpu_custom_call" | custom-call | flops 200000000 | bytes 4000000 | tf_op jit(solution)/shard_map/pallas_call | solution.py:39
Async XLA Ops:
  3.3 15.6 %collective-permute-start = (f32[5,4,16,256]{3,2,1,0:T(8,128)S(1)}, f32[5,4,16,256]{3,2,1,0:T(8,128)S(1)}, u32[]{:S(2)}, u32[]{:S(2)}) collective-permute-start(f32[5,4,16,256]{3,2,1,0:T(8,128)S(1)} %get-tuple-element.26), channel_id=1, source_target_pairs={{0,16},{16,0},{32,48},{48,32},{64,80},{80,64},{96,112},{112,96},{1... | collective-permute-start | bytes 983048 | tf_op jit(solution)/shard_map/ppermute | solution.py:352
  4.8 14.1 %collective-permute-start.1 = (f32[5,4,16,256]{3,2,1,0:T(8,128)S(1)}, f32[5,4,16,256]{3,2,1,0:T(8,128)S(1)}, u32[]{:S(2)}, u32[]{:S(2)}) collective-permute-start(f32[5,4,16,256]{3,2,1,0:T(8,128)S(1)} %get-tuple-element.27), channel_id=1, source_target_pairs={{0,112},{16,32},{32,16},{48,64},{64,48},{80,96},{96,80},{112,0},{1... | collective-permute-start | bytes 983048 | tf_op jit(solution)/shard_map/ppermute | solution.py:352
  6.5 12.4 %collective-permute-start.2 = (f32[5,16,4,256]{3,2,1,0:T(4,128)S(1)}, f32[5,16,4,256]{3,2,1,0:T(4,128)S(1)}, u32[]{:S(2)}, u32[]{:S(2)}) collective-permute-start(f32[5,16,4,256]{3,2,1,0:T(4,128)S(1)} %get-tuple-element.28), channel_id=1, source_target_pairs={{0,1},{1,2},{2,3},{3,4},{4,5},{5,6},{6,7},{7,8},{8,9},{9,10},{10,1... | collective-permute-start | bytes 983048 | tf_op jit(solution)/shard_map/ppermute | solution.py:359
  7.7 11.2 %collective-permute-start.3 = (f32[5,16,4,256]{3,2,1,0:T(4,128)S(1)}, f32[5,16,4,256]{3,2,1,0:T(4,128)S(1)}, u32[]{:S(2)}, u32[]{:S(2)}) collective-permute-start(f32[5,16,4,256]{3,2,1,0:T(4,128)S(1)} %get-tuple-element.29), channel_id=1, source_target_pairs={{1,0},{2,1},{3,2},{4,3},{5,4},{6,5},{7,6},{8,7},{9,8},{10,9},{11,1... | collective-permute-start | bytes 983048 | tf_op jit(solution)/shard_map/ppermute | solution.py:359
  11.4 48.8 %all-to-all-start = ((f32[128,49,1,128]{3,2,1,0:T(1,128)}), f32[128,49,1,128]{3,2,1,0:T(1,128)}, u32[]{:S(2)}, u32[]{:S(2)}) async-start(f32[128,49,1,128]{3,2,1,0:T(1,128)} %bitcast.14), calls=%async_computation | async-start | bytes 6422528 | tf_op jit(solution)/shard_map/all_to_all | solution.py:345
  18.9 0.7 copy-start
  18.9 0.9 copy-start.1
  18.9 1.0 copy-start.2
  19.9 0.7 copy-start.3
  62.4 21.4 %all-to-all-start.1 = ((f32[128,6,2,128]{3,2,1,0:T(2,128)}), f32[128,6,2,128]{3,2,1,0:T(2,128)S(1)}, u32[]{:S(2)}, u32[]{:S(2)}) async-start(f32[128,6,2,128]{3,2,1,0:T(2,128)} %bitcast.15), calls=%async_computation.1 | async-start | bytes 1572864 | tf_op jit(solution)/shard_map/all_to_all | solution.py:345
  86.5 21.0 %all-to-all-start.2 = ((f32[128,6,2,128]{3,2,1,0:T(2,128)}), f32[128,6,2,128]{3,2,1,0:T(2,128)S(1)}, u32[]{:S(2)}, u32[]{:S(2)}) async-start(f32[128,6,2,128]{3,2,1,0:T(2,128)} %bitcast.17), calls=%async_computation.2 | async-start | bytes 1572864 | tf_op jit(solution)/shard_map/all_to_all | solution.py:345

commit v11 on v8

--- a/solution.py
+++ b/solution.py
@@ -21,6 +21,7 @@
 A_ROWS = W_ROWS + 1
 V_ROWS = CAP * 2
 PART = 32
+FIRST_PART = 16
 
 
 def call(kernel, out_shape, mib, micros, in_specs, **kw):
@@ -112,7 +113,7 @@
 
 
 def request_kernel(
-    own_hbm, src_hbm, w_hbm, st_hbm, ve_hbm, out_hbm, xlo, xhi, ylo, yhi, own, src, w, out, edges, tile, sems
+    own_hbm, src_hbm, w_hbm, st_hbm, ve_hbm, out_hbm, xlo, xhi, ylo, yhi, own, src, w, out, edges, sems
 ):
     pairs = [(own_hbm, own), (src_hbm, src), (w_hbm.at[1], w)]
     for x_out, y_out, first, y_first in ((xlo, 0, 0, 0), (xhi, 1, 12, 8)):
@@ -120,7 +121,6 @@
             pairs.append((source.at[:, pl.ds(first, 4)], x_out.at[place]))
             pairs.append((source.at[:, :, pl.ds(y_first, 8)], edges.at[y_out, place]))
     copies = start_all(pairs, sems)
-    under_way(tile)
     wait_all(copies[:2])
     lane = iota((DEV, 128), 1)
     wanted = jnp.zeros((DEV, 128), F32)
@@ -133,17 +133,17 @@
     out[pl.ds(W_ROWS, DEV, stride=A_ROWS), :] = wanted
     copies[2].wait()
     sent = []
-    for i, first in enumerate(range(0, DEV, PART)):
-        onehot = jnp.concatenate([ones(m[first : first + PART]) for m in masks], axis=0)
+    for i, first in enumerate(range(0, DEV, FIRST_PART)):
+        onehot = jnp.concatenate([ones(m[first : first + FIRST_PART]) for m in masks], axis=0)
         for k in range(4):
             placed = dot(onehot, w[k].reshape(COLS, NZ))
             for s in range(CAP):
                 for half in range(2):
                     row = first * A_ROWS + s * 8 + k * 2 + half
-                    out[pl.ds(row, PART, stride=A_ROWS), :] = placed[
-                        s * PART : (s + 1) * PART, half * 128 : half * 128 + 128
+                    out[pl.ds(row, FIRST_PART, stride=A_ROWS), :] = placed[
+                        s * FIRST_PART : (s + 1) * FIRST_PART, half * 128 : half * 128 + 128
                     ]
-        block = pl.ds(first * A_ROWS, PART * A_ROWS)
+        block = pl.ds(first * A_ROWS, FIRST_PART * A_ROWS)
         sent += start_all(((out.at[block], out_hbm.at[block]),), sems, 11 + i)
     wait_all(copies[3:])
     ylo[...] = edges[0, :, :, 0:4]
@@ -324,13 +324,14 @@
     wait_all(copies[1:])
     for c in range(3):
         h[c] = h[c] - 0.5 * (lam[...] * g1[c])
+        g[c] = 0.5 * g[c]
 
 
 def final_kernel(arr, onehot, h, g, out_hbm, out, sems):
     lam = select(onehot[...], split(read_slots(arr)))
     sent = []
     for c in range(3):
-        out[c] = h[c] - 0.5 * (lam * g[c])
+        out[c] = h[c] - lam * g[c]
         sent += start_all(((out.at[c], out_hbm.at[c]),), sems, c)
     wait_all(sent)
 
@@ -370,8 +371,7 @@
             pltpu.VMEM((4, 16, 16, NZ), BF16),
             scratch(DEV * A_ROWS, 128),
             scratch(2, 5, 16, 8, NZ),
-            scratch(16, 128),
-            sems(15),
+            sems(19),
         ],
     )(owner_row, source_row, weights, state_path, velocity)
     asked = exchange(request.reshape(DEV, A_ROWS, 1, 128))

time: 109 us -> 109 us (level)
  no operation moved by 1% of the time
where the time goes in v11:
time: 109 us
  waiting for transfers between devices  57.2 us (52%)
  Pallas kernels  24.9 us (23%)
  starting transfers between devices  24.8 us (23%)
  local copies, waits for them, and re-layouts  1.7 us (2%)
    all_to_all x3, waiting for transfers between devices, exchange(): return lax.all_to_all(value, AXES, split_axis=0, concat_axis=0, tiled=True)  57.2 us
    pallas_call x7, Pallas kernels, placed(): run(*(pltpu.with_memory_space_constraint(x, pltpu.HBM) if spec.memory_spa...  24.9 us
    all_to_all x3, starting transfers between devices, exchange(): return lax.all_to_all(value, AXES, split_axis=0, concat_axis=0, tiled=True)  16.8 us
    ppermute x4, starting transfers between devices, neighbours(): return (lax.ppermute(last, axis, up), lax.ppermute(first, axis, down))  7.97 us
  transfers between devices with their start and end apart: 7, of which 3 were waited for; matrix products, arithmetic and copies ran while one was open for 0% of the time, Pallas kernels for 14%

profile of v11, /device:TPU:1, one launch (start us, length us, event | category | flops | bytes accessed | tf_op | source)
XLA Modules:
  0.0 108.6 jit_solution(389721290057808748)
XLA Ops:
  0.0 3.3 %shard_map.55 = (f32[6272,128]{1,0:T(8,128)}, f32[5,4,16,256]{3,2,1,0:T(8,128)S(1)}, f32[5,4,16,256]{3,2,1,0:T(8,128)S(1)}, f32[5,16,4,256]{3,2,1,0:T(4,128)S(1)}, f32[5,16,4,256]{3,2,1,0:T(4,128)S(1)}) custom-call(s32[2,1,256]{2,1,0:T(1,128)} %bitcast.20, s32[2,1,256]{2,1,0:T(1,128)} %bitcast.22, bf16[2,4,16,16,256]{4,3,2,1,0:T(8,128)(2,1)} %w_hbm.3, ...), custom_call_target="tpu_custom_call" | custom-call | flops 300000000 | bytes 6000000 | tf_op jit(solution)/shard_map/pallas_call | solution.py:40
  3.3 3.0 %collective-permute-start = (f32[5,4,16,256]{3,2,1,0:T(8,128)S(1)}, f32[5,4,16,256]{3,2,1,0:T(8,128)S(1)}, u32[]{:S(2)}, u32[]{:S(2)}) collective-permute-start(f32[5,4,16,256]{3,2,1,0:T(8,128)S(1)} %get-tuple-element.26), channel_id=1, source_target_pairs={{0,16},{16,32},{32,48},{48,64},{64,80},{80,96},{96,112},{112,0},{1... | collective-permute-start | bytes 983048 | tf_op jit(solution)/shard_map/ppermute | solution.py:347
  6.4 0.0 collective-permute-start.1
  6.4 1.2 %collective-permute-start.2 = (f32[5,16,4,256]{3,2,1,0:T(4,128)S(1)}, f32[5,16,4,256]{3,2,1,0:T(4,128)S(1)}, u32[]{:S(2)}, u32[]{:S(2)}) collective-permute-start(f32[5,16,4,256]{3,2,1,0:T(4,128)S(1)} %get-tuple-element.28), channel_id=1, source_target_pairs={{0,1},{1,2},{2,3},{3,4},{4,5},{5,6},{6,7},{7,8},{8,9},{9,10},{10,1... | collective-permute-start | bytes 983048 | tf_op jit(solution)/shard_map/ppermute | solution.py:347
  7.6 3.7 %collective-permute-start.3 = (f32[5,16,4,256]{3,2,1,0:T(4,128)S(1)}, f32[5,16,4,256]{3,2,1,0:T(4,128)S(1)}, u32[]{:S(2)}, u32[]{:S(2)}) collective-permute-start(f32[5,16,4,256]{3,2,1,0:T(4,128)S(1)} %get-tuple-element.29), channel_id=1, source_target_pairs={{1,0},{2,1},{3,2},{4,3},{5,4},{6,5},{7,6},{8,7},{9,8},{10,9},{11,1... | collective-permute-start | bytes 983048 | tf_op jit(solution)/shard_map/ppermute | solution.py:347
  11.3 7.7 %all-to-all-start = ((f32[128,49,1,128]{3,2,1,0:T(1,128)}), f32[128,49,1,128]{3,2,1,0:T(1,128)}, u32[]{:S(2)}, u32[]{:S(2)}) async-start(f32[128,49,1,128]{3,2,1,0:T(1,128)} %bitcast.14), calls=%async_computation | async-start | bytes 6422528 | tf_op jit(solution)/shard_map/all_to_all | solution.py:340
  19.0 0.0 collective-permute-done.xlo
  19.0 0.0 copy-start
  19.0 0.0 collective-permute-done.1.xhi
  19.0 0.0 copy-start.1
  19.0 0.0 collective-permute-done.2.ylo
  19.1 0.0 copy-start.2
  19.1 0.0 collective-permute-done.3.yhi
  19.1 0.7 copy-done
  19.8 0.2 copy-done.1
  19.9 0.1 copy-done.2
  20.0 0.0 copy-start.3
  20.0 0.7 copy-done.3
  20.8 7.9 %shard_map.56 = (f32[2,3,16,16,256]{4,3,2,1,0:T(8,128)}, f32[16,16,256]{2,1,0:T(8,128)}, f32[3,16,16,256]{3,2,1,0:T(8,128)}, bf16[2,256,256]{2,1,0:T(8,128)(2,1)S(1)}) custom-call(f32[2,16,16,256]{3,2,1,0:T(8,128)} %st_hbm.3, f32[3,16,16,256]{3,2,1,0:T(8,128)} %ve_hbm.3, f32[5,4,16,256]{3,2,1,0:T(8,128)} %copy-done, f32[5,4,16,256]{3,2,1,0:T(8,128)} %copy-done.1, ...), custom_call_target="tpu_custom_call" | custom-call | flops 99999997952 | bytes 2000000000 | tf_op jit(solution)/shard_map/pallas_call | solution.py:40
  28.7 31.6 %all-to-all-done.asked_hbm = f32[128,49,1,128]{3,2,1,0:T(1,128)} async-done(((f32[128,49,1,128]{3,2,1,0:T(1,128)}), f32[128,49,1,128]{3,2,1,0:T(1,128)}, u32[]{:S(2)}, u32[]{:S(2)}) %all-to-all-start) | async-done | bytes 3211296 | tf_op jit(solution)/shard_map/all_to_all | solution.py:340
  60.3 2.1 %shard_map.57 = f32[1536,128]{1,0:T(8,128)} custom-call(f32[128,49,1,128]{3,2,1,0:T(1,128)} %all-to-all-done.asked_hbm, bf16[2,256,256]{2,1,0:T(8,128)(2,1)S(1)} %get-tuple-element.30.parts), custom_call_target="tpu_custom_call" | custom-call | flops 200000000 | bytes 4000000 | tf_op jit(solution)/shard_map/pallas_call | solution.py:40
  62.4 4.8 %all-to-all-start.1 = ((f32[128,6,2,128]{3,2,1,0:T(2,128)}), f32[128,6,2,128]{3,2,1,0:T(2,128)S(1)}, u32[]{:S(2)}, u32[]{:S(2)}) async-start(f32[128,6,2,128]{3,2,1,0:T(2,128)} %bitcast.15), calls=%async_computation.1 | async-start | bytes 1572864 | tf_op jit(solution)/shard_map/all_to_all | solution.py:340
  67.2 5.9 %shard_map.58 = (f32[4,256,256]{2,1,0:T(8,128)S(1)}, bf16[256,768]{1,0:T(8,128)(2,1)S(1)}, bf16[4,16,16,256]{3,2,1,0:T(8,128)(2,1)S(1)}, f32[256,256]{1,0:T(8,12...) custom-call(f32[6272,128]{1,0:T(8,128)} %bitcast.5.asked_hbm, s32[2,1,256]{2,1,0:T(1,128)} %bitcast.21, ...), custom_call_target="tpu_custom_call" | custom-call | flops 400000000 | bytes 8000000 | tf_op jit(solution)/shard_map/pallas_call | solution.py:40
  73.1 10.7 %all-to-all-done.1 = f32[128,6,2,128]{3,2,1,0:T(2,128)S(1)} async-done(((f32[128,6,2,128]{3,2,1,0:T(2,128)}), f32[128,6,2,128]{3,2,1,0:T(2,128)S(1)}, u32[]{:S(2)}, u32[]{:S(2)}) %all-to-all-start.1) | async-done | bytes 786464 | tf_op jit(solution)/shard_map/all_to_all | solution.py:340
  83.8 2.6 %shard_map.59 = (f32[256,256]{1,0:T(8,128)S(1)}, f32[1536,128]{1,0:T(8,128)}) custom-call(f32[1536,128]{1,0:T(8,128)S(1)} %bitcast.13, f32[4,256,256]{2,1,0:T(8,128)S(1)} %get-tuple-element.32.d, bf16[256,768]{1,0:T(8,128)(2,1)S(1)} %get-tuple-element.33.taken, bf16[4,16,16,256]{3,2,1,0:T(8,128)(2,1)S(1)} %get-tuple-element.34.w, ...), custom_call_target="tpu_custom_call" | custom-call | flops 400000000 | bytes 8000000 | tf_op jit(solution)/shard_map/pallas_call | solution.py:40
  86.4 4.3 %all-to-all-start.2 = ((f32[128,6,2,128]{3,2,1,0:T(2,128)}), f32[128,6,2,128]{3,2,1,0:T(2,128)S(1)}, u32[]{:S(2)}, u32[]{:S(2)}) async-start(f32[128,6,2,128]{3,2,1,0:T(2,128)} %bitcast.17), calls=%async_computation.2 | async-start | bytes 1572864 | tf_op jit(solution)/shard_map/all_to_all | solution.py:340
  90.6 1.8 %shard_map.60 = (f32[3,256,256]{2,1,0:T(8,128)S(1)}, f32[3,256,256]{2,1,0:T(8,128)S(1)}, bf16[256,768]{1,0:T(8,128)(2,1)S(1)}) custom-call(f32[256,256]{1,0:T(8,128)S(1)} %get-tuple-element.38.lam, f32[16,128]{1,0:T(8,128)} %get-tuple-element.39.wt_hbm, f32[3,256,256]{2,1,0:T(8,128)} %bitcast.18, f32[2,3,256,256]{3,2,1,0:T(8,128)} %bitcast.16), custom_call_target="tpu_custom_call" | custom-call | flops 300000000 | bytes 6000000 | tf_op jit(solution)/shard_map/pallas_call | solution.py:40
  92.5 14.9 %all-to-all-done.2 = f32[128,6,2,128]{3,2,1,0:T(2,128)S(1)} async-done(((f32[128,6,2,128]{3,2,1,0:T(2,128)}), f32[128,6,2,128]{3,2,1,0:T(2,128)S(1)}, u32[]{:S(2)}, u32[]{:S(2)}) %all-to-all-start.2) | async-done | bytes 786464 | tf_op jit(solution)/shard_map/all_to_all | solution.py:340
  107.3 1.3 %shard_map.61 = f32[3,256,256]{2,1,0:T(8,128)} custom-call(f32[1536,128]{1,0:T(8,128)S(1)} %bitcast.12, bf16[256,768]{1,0:T(8,128)(2,1)S(1)} %get-tuple-element.42.onehot, f32[3,256,256]{2,1,0:T(8,128)S(1)} %get-tuple-element.43.h, f32[3,256,256]{2,1,0:T(8,128)S(1)} %get-tuple-element.44.g), custom_call_target="tpu_custom_call" | custom-call | flops 200000000 | bytes 4000000 | tf_op jit(solution)/shard_map/pallas_call | solution.py:40
Async XLA Ops:
  3.3 15.7 %collective-permute-start = (f32[5,4,16,256]{3,2,1,0:T(8,128)S(1)}, f32[5,4,16,256]{3,2,1,0:T(8,128)S(1)}, u32[]{:S(2)}, u32[]{:S(2)}) collective-permute-start(f32[5,4,16,256]{3,2,1,0:T(8,128)S(1)} %get-tuple-element.26), channel_id=1, source_target_pairs={{0,16},{16,32},{32,48},{48,64},{64,80},{80,96},{96,112},{112,0},{1... | collective-permute-start | bytes 983048 | tf_op jit(solution)/shard_map/ppermute | solution.py:347
  6.4 12.7 %collective-permute-start.1 = (f32[5,4,16,256]{3,2,1,0:T(8,128)S(1)}, f32[5,4,16,256]{3,2,1,0:T(8,128)S(1)}, u32[]{:S(2)}, u32[]{:S(2)}) collective-permute-start(f32[5,4,16,256]{3,2,1,0:T(8,128)S(1)} %get-tuple-element.27), channel_id=1, source_target_pairs={{16,0},{32,16},{48,32},{64,48},{80,64},{96,80},{112,96},{0,112},{1... | collective-permute-start | bytes 983048 | tf_op jit(solution)/shard_map/ppermute | solution.py:347
  6.4 12.7 %collective-permute-start.2 = (f32[5,16,4,256]{3,2,1,0:T(4,128)S(1)}, f32[5,16,4,256]{3,2,1,0:T(4,128)S(1)}, u32[]{:S(2)}, u32[]{:S(2)}) collective-permute-start(f32[5,16,4,256]{3,2,1,0:T(4,128)S(1)} %get-tuple-element.28), channel_id=1, source_target_pairs={{0,1},{1,2},{2,3},{3,4},{4,5},{5,6},{6,7},{7,8},{8,9},{9,10},{10,1... | collective-permute-start | bytes 983048 | tf_op jit(solution)/shard_map/ppermute | solution.py:347
  7.6 11.5 %collective-permute-start.3 = (f32[5,16,4,256]{3,2,1,0:T(4,128)S(1)}, f32[5,16,4,256]{3,2,1,0:T(4,128)S(1)}, u32[]{:S(2)}, u32[]{:S(2)}) collective-permute-start(f32[5,16,4,256]{3,2,1,0:T(4,128)S(1)} %get-tuple-element.29), channel_id=1, source_target_pairs={{1,0},{2,1},{3,2},{4,3},{5,4},{6,5},{7,6},{8,7},{9,8},{10,9},{11,1... | collective-permute-start | bytes 983048 | tf_op jit(solution)/shard_map/ppermute | solution.py:347
  11.3 49.0 %all-to-all-start = ((f32[128,49,1,128]{3,2,1,0:T(1,128)}), f32[128,49,1,128]{3,2,1,0:T(1,128)}, u32[]{:S(2)}, u32[]{:S(2)}) async-start(f32[128,49,1,128]{3,2,1,0:T(1,128)} %bitcast.14), calls=%async_computation | async-start | bytes 6422528 | tf_op jit(solution)/shard_map/all_to_all | solution.py:340
  19.0 0.7 copy-start
  19.0 0.9 copy-start.1
  19.1 1.0 copy-start.2
  20.0 0.7 copy-start.3
  62.4 21.4 %all-to-all-start.1 = ((f32[128,6,2,128]{3,2,1,0:T(2,128)}), f32[128,6,2,128]{3,2,1,0:T(2,128)S(1)}, u32[]{:S(2)}, u32[]{:S(2)}) async-start(f32[128,6,2,128]{3,2,1,0:T(2,128)} %bitcast.15), calls=%async_computation.1 | async-start | bytes 1572864 | tf_op jit(solution)/shard_map/all_to_all | solution.py:340
  86.4 21.0 %all-to-all-start.2 = ((f32[128,6,2,128]{3,2,1,0:T(2,128)}), f32[128,6,2,128]{3,2,1,0:T(2,128)S(1)}, u32[]{:S(2)}, u32[]{:S(2)}) async-start(f32[128,6,2,128]{3,2,1,0:T(2,128)} %bitcast.17), calls=%async_computation.2 | async-start | bytes 1572864 | tf_op jit(solution)/shard_map/all_to_all | solution.py:340

commit v12 on v11

--- a/solution.py
+++ b/solution.py
@@ -181,7 +181,7 @@
 
 
 def stencil_kernel(
-    st_hbm, ve_hbm, xlo, xhi, ylo, yhi, g_hbm, b_hbm, h_hbm, first_parts, xpad, ypad, ylo_scr, yhi_scr, g, b, h, sems
+    st_hbm, ve_hbm, ylo, yhi, xlo, xhi, g_hbm, b_hbm, h_hbm, first_parts, xpad, ypad, ylo_scr, yhi_scr, g, b, h, sems
 ):
     sources = [st_hbm.at[j] for j in range(2)] + [ve_hbm.at[c] for c in range(3)]
     fill(sources, (xlo, xhi, ylo, yhi), xpad, ypad, ylo_scr, yhi_scr, sems)
@@ -376,7 +376,7 @@
     )(owner_row, source_row, weights, state_path, velocity)
     asked = exchange(request.reshape(DEV, A_ROWS, 1, 128))
 
-    halos = neighbours(first_x, last_x, "gx") + neighbours(first_y, last_y, "gy")
+    halos = neighbours(first_y, last_y, "gy") + neighbours(first_x, last_x, "gx")
     slopes, before, hess, before_parts = call(
         stencil_kernel,
         (struct(2, 3, 16, 16, NZ), struct(16, 16, NZ), per_field(3), pltpu.VMEM((2, COLS, NZ), BF16)),

time: 109 us -> 109 us (level)
  no operation moved by 1% of the time
where the time goes in v12:
time: 109 us
  waiting for transfers between devices  57.2 us (52%)
  Pallas kernels  24.9 us (23%)
  starting transfers between devices  24.8 us (23%)
  local copies, waits for them, and re-layouts  1.7 us (2%)
    all_to_all x3, waiting for transfers between devices, exchange(): return lax.all_to_all(value, AXES, split_axis=0, concat_axis=0, tiled=True)  57.2 us
    pallas_call x7, Pallas kernels, placed(): run(*(pltpu.with_memory_space_constraint(x, pltpu.HBM) if spec.memory_spa...  24.9 us
    all_to_all x3, starting transfers between devices, exchange(): return lax.all_to_all(value, AXES, split_axis=0, concat_axis=0, tiled=True)  16.4 us
    ppermute x4, starting transfers between devices, neighbours(): return (lax.ppermute(last, axis, up), lax.ppermute(first, axis, down))  8.44 us
  transfers between devices with their start and end apart: 7, of which 3 were waited for; matrix products, arithmetic and copies ran while one was open for 0% of the time, Pallas kernels for 14%

profile of v12, /device:TPU:1, one launch (start us, length us, event | category | flops | bytes accessed | tf_op | source)
XLA Modules:
  0.0 108.7 jit_solution(3833408509065768594)
XLA Ops:
  0.0 3.3 %shard_map.55 = (f32[6272,128]{1,0:T(8,128)}, f32[5,4,16,256]{3,2,1,0:T(8,128)S(1)}, f32[5,4,16,256]{3,2,1,0:T(8,128)S(1)}, f32[5,16,4,256]{3,2,1,0:T(4,128)S(1)}, f32[5,16,4,256]{3,2,1,0:T(4,128)S(1)}) custom-call(s32[2,1,256]{2,1,0:T(1,128)} %bitcast.20, s32[2,1,256]{2,1,0:T(1,128)} %bitcast.22, bf16[2,4,16,16,256]{4,3,2,1,0:T(8,128)(2,1)} %w_hbm.3, ...), custom_call_target="tpu_custom_call" | custom-call | flops 300000000 | bytes 6000000 | tf_op jit(solution)/shard_map/pallas_call | solution.py:40
  3.3 2.1 %collective-permute-start = (f32[5,16,4,256]{3,2,1,0:T(4,128)S(1)}, f32[5,16,4,256]{3,2,1,0:T(4,128)S(1)}, u32[]{:S(2)}, u32[]{:S(2)}) collective-permute-start(f32[5,16,4,256]{3,2,1,0:T(4,128)S(1)} %get-tuple-element.26), channel_id=1, source_target_pairs={{0,1},{1,2},{2,3},{3,4},{4,5},{5,6},{6,7},{7,8},{8,9},{9,10},{10,1... | collective-permute-start | bytes 983048 | tf_op jit(solution)/shard_map/ppermute | solution.py:347
  5.4 3.8 %collective-permute-start.1 = (f32[5,16,4,256]{3,2,1,0:T(4,128)S(1)}, f32[5,16,4,256]{3,2,1,0:T(4,128)S(1)}, u32[]{:S(2)}, u32[]{:S(2)}) collective-permute-start(f32[5,16,4,256]{3,2,1,0:T(4,128)S(1)} %get-tuple-element.27), channel_id=1, source_target_pairs={{1,0},{2,1},{3,2},{4,3},{5,4},{6,5},{7,6},{8,7},{9,8},{10,9},{11,1... | collective-permute-start | bytes 983048 | tf_op jit(solution)/shard_map/ppermute | solution.py:347
  9.2 2.5 %collective-permute-start.2 = (f32[5,4,16,256]{3,2,1,0:T(8,128)S(1)}, f32[5,4,16,256]{3,2,1,0:T(8,128)S(1)}, u32[]{:S(2)}, u32[]{:S(2)}) collective-permute-start(f32[5,4,16,256]{3,2,1,0:T(8,128)S(1)} %get-tuple-element.28), channel_id=1, source_target_pairs={{0,16},{16,32},{32,48},{48,64},{64,80},{80,96},{96,112},{112,0},{1... | collective-permute-start | bytes 983048 | tf_op jit(solution)/shard_map/ppermute | solution.py:347
  11.8 0.0 collective-permute-start.3
  11.8 7.3 %all-to-all-start = ((f32[128,49,1,128]{3,2,1,0:T(1,128)}), f32[128,49,1,128]{3,2,1,0:T(1,128)}, u32[]{:S(2)}, u32[]{:S(2)}) async-start(f32[128,49,1,128]{3,2,1,0:T(1,128)} %bitcast.14), calls=%async_computation | async-start | bytes 6422528 | tf_op jit(solution)/shard_map/all_to_all | solution.py:340
  19.1 0.0 collective-permute-done.ylo
  19.1 0.0 copy-start
  19.1 0.0 collective-permute-done.1.yhi
  19.1 0.0 copy-start.1
  19.1 0.0 collective-permute-done.2.xlo
  19.1 0.0 copy-start.2
  19.1 0.0 collective-permute-done.3.xhi
  19.1 0.7 copy-done
  19.8 0.2 copy-done.1
  20.0 0.1 copy-done.2
  20.1 0.0 copy-start.3
  20.1 0.7 copy-done.3
  20.8 7.9 %shard_map.56 = (f32[2,3,16,16,256]{4,3,2,1,0:T(8,128)}, f32[16,16,256]{2,1,0:T(8,128)}, f32[3,16,16,256]{3,2,1,0:T(8,128)}, bf16[2,256,256]{2,1,0:T(8,128)(2,1)S(1)}) custom-call(f32[2,16,16,256]{3,2,1,0:T(8,128)} %st_hbm.3, f32[3,16,16,256]{3,2,1,0:T(8,128)} %ve_hbm.3, f32[5,16,4,256]{3,2,1,0:T(4,128)} %copy-done, f32[5,16,4,256]{3,2,1,0:T(4,128)} %copy-done.1, ...), custom_call_target="tpu_custom_call" | custom-call | flops 99999997952 | bytes 2000000000 | tf_op jit(solution)/shard_map/pallas_call | solution.py:40
  28.8 31.6 %all-to-all-done.asked_hbm = f32[128,49,1,128]{3,2,1,0:T(1,128)} async-done(((f32[128,49,1,128]{3,2,1,0:T(1,128)}), f32[128,49,1,128]{3,2,1,0:T(1,128)}, u32[]{:S(2)}, u32[]{:S(2)}) %all-to-all-start) | async-done | bytes 3211296 | tf_op jit(solution)/shard_map/all_to_all | solution.py:340
  60.3 2.1 %shard_map.57 = f32[1536,128]{1,0:T(8,128)} custom-call(f32[128,49,1,128]{3,2,1,0:T(1,128)} %all-to-all-done.asked_hbm, bf16[2,256,256]{2,1,0:T(8,128)(2,1)S(1)} %get-tuple-element.30.parts), custom_call_target="tpu_custom_call" | custom-call | flops 200000000 | bytes 4000000 | tf_op jit(solution)/shard_map/pallas_call | solution.py:40
  62.4 4.8 %all-to-all-start.1 = ((f32[128,6,2,128]{3,2,1,0:T(2,128)}), f32[128,6,2,128]{3,2,1,0:T(2,128)S(1)}, u32[]{:S(2)}, u32[]{:S(2)}) async-start(f32[128,6,2,128]{3,2,1,0:T(2,128)} %bitcast.15), calls=%async_computation.1 | async-start | bytes 1572864 | tf_op jit(solution)/shard_map/all_to_all | solution.py:340
  67.3 5.9 %shard_map.58 = (f32[4,256,256]{2,1,0:T(8,128)S(1)}, bf16[256,768]{1,0:T(8,128)(2,1)S(1)}, bf16[4,16,16,256]{3,2,1,0:T(8,128)(2,1)S(1)}, f32[256,256]{1,0:T(8,12...) custom-call(f32[6272,128]{1,0:T(8,128)} %bitcast.5.asked_hbm, s32[2,1,256]{2,1,0:T(1,128)} %bitcast.21, ...), custom_call_target="tpu_custom_call" | custom-call | flops 400000000 | bytes 8000000 | tf_op jit(solution)/shard_map/pallas_call | solution.py:40
  73.1 10.7 %all-to-all-done.1 = f32[128,6,2,128]{3,2,1,0:T(2,128)S(1)} async-done(((f32[128,6,2,128]{3,2,1,0:T(2,128)}), f32[128,6,2,128]{3,2,1,0:T(2,128)S(1)}, u32[]{:S(2)}, u32[]{:S(2)}) %all-to-all-start.1) | async-done | bytes 786464 | tf_op jit(solution)/shard_map/all_to_all | solution.py:340
  83.8 2.6 %shard_map.59 = (f32[256,256]{1,0:T(8,128)S(1)}, f32[1536,128]{1,0:T(8,128)}) custom-call(f32[1536,128]{1,0:T(8,128)S(1)} %bitcast.13, f32[4,256,256]{2,1,0:T(8,128)S(1)} %get-tuple-element.32.d, bf16[256,768]{1,0:T(8,128)(2,1)S(1)} %get-tuple-element.33.taken, bf16[4,16,16,256]{3,2,1,0:T(8,128)(2,1)S(1)} %get-tuple-element.34.w, ...), custom_call_target="tpu_custom_call" | custom-call | flops 400000000 | bytes 8000000 | tf_op jit(solution)/shard_map/pallas_call | solution.py:40
  86.4 4.3 %all-to-all-start.2 = ((f32[128,6,2,128]{3,2,1,0:T(2,128)}), f32[128,6,2,128]{3,2,1,0:T(2,128)S(1)}, u32[]{:S(2)}, u32[]{:S(2)}) async-start(f32[128,6,2,128]{3,2,1,0:T(2,128)} %bitcast.17), calls=%async_computation.2 | async-start | bytes 1572864 | tf_op jit(solution)/shard_map/all_to_all | solution.py:340
  90.7 1.8 %shard_map.60 = (f32[3,256,256]{2,1,0:T(8,128)S(1)}, f32[3,256,256]{2,1,0:T(8,128)S(1)}, bf16[256,768]{1,0:T(8,128)(2,1)S(1)}) custom-call(f32[256,256]{1,0:T(8,128)S(1)} %get-tuple-element.38.lam, f32[16,128]{1,0:T(8,128)} %get-tuple-element.39.wt_hbm, f32[3,256,256]{2,1,0:T(8,128)} %bitcast.18, f32[2,3,256,256]{3,2,1,0:T(8,128)} %bitcast.16), custom_call_target="tpu_custom_call" | custom-call | flops 300000000 | bytes 6000000 | tf_op jit(solution)/shard_map/pallas_call | solution.py:40
  92.5 14.9 %all-to-all-done.2 = f32[128,6,2,128]{3,2,1,0:T(2,128)S(1)} async-done(((f32[128,6,2,128]{3,2,1,0:T(2,128)}), f32[128,6,2,128]{3,2,1,0:T(2,128)S(1)}, u32[]{:S(2)}, u32[]{:S(2)}) %all-to-all-start.2) | async-done | bytes 786464 | tf_op jit(solution)/shard_map/all_to_all | solution.py:340
  107.4 1.3 %shard_map.61 = f32[3,256,256]{2,1,0:T(8,128)} custom-call(f32[1536,128]{1,0:T(8,128)S(1)} %bitcast.12, bf16[256,768]{1,0:T(8,128)(2,1)S(1)} %get-tuple-element.42.onehot, f32[3,256,256]{2,1,0:T(8,128)S(1)} %get-tuple-element.43.h, f32[3,256,256]{2,1,0:T(8,128)S(1)} %get-tuple-element.44.g), custom_call_target="tpu_custom_call" | custom-call | flops 200000000 | bytes 4000000 | tf_op jit(solution)/shard_map/pallas_call | solution.py:40
Async XLA Ops:
  3.3 15.8 %collective-permute-start = (f32[5,16,4,256]{3,2,1,0:T(4,128)S(1)}, f32[5,16,4,256]{3,2,1,0:T(4,128)S(1)}, u32[]{:S(2)}, u32[]{:S(2)}) collective-permute-start(f32[5,16,4,256]{3,2,1,0:T(4,128)S(1)} %get-tuple-element.26), channel_id=1, source_target_pairs={{0,1},{1,2},{2,3},{3,4},{4,5},{5,6},{6,7},{7,8},{8,9},{9,10},{10,1... | collective-permute-start | bytes 983048 | tf_op jit(solution)/shard_map/ppermute | solution.py:347
  5.4 13.7 %collective-permute-start.1 = (f32[5,16,4,256]{3,2,1,0:T(4,128)S(1)}, f32[5,16,4,256]{3,2,1,0:T(4,128)S(1)}, u32[]{:S(2)}, u32[]{:S(2)}) collective-permute-start(f32[5,16,4,256]{3,2,1,0:T(4,128)S(1)} %get-tuple-element.27), channel_id=1, source_target_pairs={{1,0},{2,1},{3,2},{4,3},{5,4},{6,5},{7,6},{8,7},{9,8},{10,9},{11,1... | collective-permute-start | bytes 983048 | tf_op jit(solution)/shard_map/ppermute | solution.py:347
  9.2 9.9 %collective-permute-start.2 = (f32[5,4,16,256]{3,2,1,0:T(8,128)S(1)}, f32[5,4,16,256]{3,2,1,0:T(8,128)S(1)}, u32[]{:S(2)}, u32[]{:S(2)}) collective-permute-start(f32[5,4,16,256]{3,2,1,0:T(8,128)S(1)} %get-tuple-element.28), channel_id=1, source_target_pairs={{0,16},{16,32},{32,48},{48,64},{64,80},{80,96},{96,112},{112,0},{1... | collective-permute-start | bytes 983048 | tf_op jit(solution)/shard_map/ppermute | solution.py:347
  11.8 7.4 %collective-permute-start.3 = (f32[5,4,16,256]{3,2,1,0:T(8,128)S(1)}, f32[5,4,16,256]{3,2,1,0:T(8,128)S(1)}, u32[]{:S(2)}, u32[]{:S(2)}) collective-permute-start(f32[5,4,16,256]{3,2,1,0:T(8,128)S(1)} %get-tuple-element.29), channel_id=1, source_target_pairs={{16,0},{32,16},{48,32},{64,48},{80,64},{96,80},{112,96},{0,112},{1... | collective-permute-start | bytes 983048 | tf_op jit(solution)/shard_map/ppermute | solution.py:347
  11.8 48.6 %all-to-all-start = ((f32[128,49,1,128]{3,2,1,0:T(1,128)}), f32[128,49,1,128]{3,2,1,0:T(1,128)}, u32[]{:S(2)}, u32[]{:S(2)}) async-start(f32[128,49,1,128]{3,2,1,0:T(1,128)} %bitcast.14), calls=%async_computation | async-start | bytes 6422528 | tf_op jit(solution)/shard_map/all_to_all | solution.py:340
  19.1 0.7 copy-start
  19.1 0.9 copy-start.1
  19.1 1.0 copy-start.2
  20.1 0.7 copy-start.3
  62.4 21.4 %all-to-all-start.1 = ((f32[128,6,2,128]{3,2,1,0:T(2,128)}), f32[128,6,2,128]{3,2,1,0:T(2,128)S(1)}, u32[]{:S(2)}, u32[]{:S(2)}) async-start(f32[128,6,2,128]{3,2,1,0:T(2,128)} %bitcast.15), calls=%async_computation.1 | async-start | bytes 1572864 | tf_op jit(solution)/shard_map/all_to_all | solution.py:340
  86.4 21.0 %all-to-all-start.2 = ((f32[128,6,2,128]{3,2,1,0:T(2,128)}), f32[128,6,2,128]{3,2,1,0:T(2,128)S(1)}, u32[]{:S(2)}, u32[]{:S(2)}) async-start(f32[128,6,2,128]{3,2,1,0:T(2,128)} %bitcast.17), calls=%async_computation.2 | async-start | bytes 1572864 | tf_op jit(solution)/shard_map/all_to_all | solution.py:340
